TPU v7x, 256 devices: a whole 4x4x8 slice. The times are simulated.
256 devices in a mesh: sec: 4 (over z_hi, core), tile: 64 (over z_lo, y, x).
Axes of the slice: x: 4, y: 4, z: 8 (z_hi: 2, z_lo: 4; z = z_hi * 4 + z_lo), core: 2. Of those that a mesh axis runs over, the one named last changes fastest.
Arguments:
- sections: bfloat16 [4, 4096, 2048], P('sec', 'tile'), may hold values from -6 to 6
- earlier: bfloat16 [2, 4096, 2048], P(None, 'tile'), may hold values from -6 to 6
- offsets: int32 [4], P('sec'), may hold values from 1 to 2, as said below
- patch_valid: int32 [4, 64, 32], P('sec', 'tile'), may hold values 0 or 1
Outputs:
- node_flows: float32 [4, 2, 64, 32], P('sec', None, 'tile')
- confidence: float32 [4, 64, 32], P('sec', 'tile')
- positions: float32 [4, 2, 64, 32], P('sec', None, 'tile')
Inputs may be any that keep to these rules, and one draw needn't show every extreme that they name: `offsets`: some section after the second takes 2, and another section after the first takes 1.
All inputs are finite; a program needn't handle non-finite values. No bound on the sum of `patch_valid` on one device may be relied on, other than what follows from the above.
Results may differ from a plain program's by a relative error of at most 0.0008.
Values may be sent and summed in bfloat16 or wider, within the bound.
No kernel may reach another device: no remote copies, remote signals or barrier semaphores. Data moves between devices by JAX's collectives and lax.ppermute only.
A program may use at most 64 MiB of HBM per device.

v0:
```python
import functools

import jax
import jax.numpy as jnp
import ml_dtypes
import numpy as np
from jax import lax
from jax.experimental import pallas as pl
from jax.experimental.pallas import tpu as pltpu
from jax.sharding import PartitionSpec as P

PATCH = 128
HALF = PATCH // 2
RIM = HALF // 2
STEPS = 3
SECTIONS = 4
COLS = 32
QCOLS = COLS // SECTIONS
QPIX = QCOLS * HALF
MSG = QPIX + PATCH
LANES = 128
FEATS = 16

score_scale = 800.0
spring_rate = 0.3
plane_weight = 0.5
f32 = jnp.float32
bf16 = jnp.bfloat16


def split_table(table):
    hi = table.astype(ml_dtypes.bfloat16)
    lo = (table - hi.astype(np.float64)).astype(ml_dtypes.bfloat16)
    return hi, lo


@functools.cache
def tables():
    n = np.arange(PATCH)
    angle = 2.0 * np.pi / PATCH * (np.outer(n, n) % PATCH)
    c, s = np.cos(angle), np.sin(angle)
    c[np.abs(c) < 1e-12] = 0.0
    s[np.abs(s) < 1e-12] = 0.0
    alt = (-1.0) ** n
    z = np.zeros_like(c)
    rows = np.concatenate([c[:HALF], alt[None], s[1:HALF]], axis=0)
    rows_hi, rows_lo = split_table(rows)
    rows2 = np.concatenate([rows_hi, rows_lo], axis=0)
    cols_cos = np.concatenate([c[:HALF], -s[:HALF]], axis=1)
    cols_sin = np.concatenate([-s[:HALF], -c[:HALF]], axis=1)
    even = np.concatenate([cols_cos, cols_sin], axis=0)
    odd = np.concatenate([cols_sin, cols_cos], axis=0) * np.concatenate([alt, alt])[None]
    even_hi, even_lo = split_table(even)
    odd_hi, odd_lo = split_table(odd)
    fwd = np.concatenate([even_hi, even_hi, even_lo, odd_hi, odd_hi, odd_lo], axis=0)
    inv = np.concatenate(
        [np.concatenate([c, s], axis=1), np.concatenate([-s, c], axis=1)], axis=0
    )
    inv2 = np.concatenate(split_table(inv), axis=0)
    back = np.concatenate([2.0 * c[:, :HALF], -2.0 * s[:, :HALF]], axis=1)
    back[:, 0] = 1.0
    back[:, HALF] = alt
    back_hi, back_lo = split_table(back / (PATCH * PATCH))
    back2 = np.concatenate(
        [np.concatenate([back_hi, back_hi], axis=1), np.concatenate([back_lo, back_lo], axis=1)],
        axis=0,
    )
    pair = np.concatenate([c[:HALF], -s[:HALF]], axis=1)
    zero = np.zeros_like(pair)
    edge_fwd = np.concatenate(
        [np.concatenate([pair, zero], axis=1), np.concatenate([zero, pair], axis=1)], axis=0
    )
    edge_inv = np.concatenate(
        [
            np.concatenate([c, z], axis=1),
            np.concatenate([-s, z], axis=1),
            np.concatenate([z, c], axis=1),
            np.concatenate([z, -s], axis=1),
        ],
        axis=0,
    )
    return (
        rows2,
        fwd,
        inv2,
        back2,
        np.concatenate(split_table(edge_fwd), axis=0),
        np.concatenate(split_table(edge_inv), axis=0),
    )


def dot(a, b):
    return jnp.dot(a, b, preferred_element_type=f32)


def split(x):
    hi = x.astype(bf16)
    return hi, (x - hi.astype(f32)).astype(bf16)


def dot3(x, hi, lo):
    xh, xl = split(x)
    return dot(xh, hi) + dot(xl, hi) + dot(xh, lo)


def iota(shape, dim):
    return lax.broadcasted_iota(jnp.int32, shape, dim)


def correlate_kernel(
    tile_count,
    m0, m1, m2, m3, he, ho, eq, ehe, eho, valid, off,
    rows2, fwd, inv2, back2, edge_fwd, edge_inv,
    out,
    x_ref, spec, spec0, row0, energy, u_ref, part, peak, off_s,
):
    q = lax.axis_index("sec")
    t = lax.axis_index("tile")
    even = lax.rem(t, 2) == 0
    messages = (m0, m1, m2, m3)
    at_even = pl.multiple_of(jnp.where(even, PATCH - RIM, 0), RIM)
    at_odd = pl.multiple_of(jnp.where(even, 0, PATCH - RIM), RIM)
    no_odd = jnp.logical_or(t == 0, t == tile_count - 1)
    keep = jnp.where(no_odd, 0.0, 1.0).astype(bf16)
    for i in range(2):
        x_ref[i, RIM : RIM + HALF, :] = eq[i]
        x_ref[i, pl.ds(at_even, RIM), :] = ehe[i]
        x_ref[i, pl.ds(at_odd, RIM), :] = eho[i] * keep
    for d in range(SECTIONS):
        x_ref[2 + d, RIM : RIM + HALF, :] = messages[d][...]
        x_ref[2 + d, pl.ds(at_even, RIM), :] = he[d]
        x_ref[2 + d, pl.ds(at_odd, RIM), :] = ho[d] * keep
        section = q ^ d
        off_s[section] = jnp.max(messages[d][:16, MSG - HALF :].astype(f32)).astype(jnp.int32)

    lane = iota((HALF, LANES), 1)
    low = lane < HALF
    window_row = iota((QCOLS, MSG), 0)
    window_lane = iota((QCOLS, MSG), 1)
    in_window = jnp.logical_and(
        window_lane >= window_row * HALF, window_lane < window_row * HALF + PATCH
    )
    for i in range(6):
        slot = i if i < 2 else (q ^ (i - 2)) + 2
        x = x_ref[i]
        xf = x.astype(f32)
        column = jnp.sum(xf * xf, axis=0, keepdims=True)
        windows = jnp.sum(jnp.where(in_window, column, 0.0), axis=1, keepdims=True)
        energy[slot] = jnp.broadcast_to(windows, (QCOLS, LANES))
        y2 = dot(rows2[...], x)
        y = y2[:PATCH] + y2[PATCH:]
        evens, odds = [], []
        for v in range(QCOLS // 2 + 1):
            a = y[:HALF, LANES * v : LANES * (v + 1)]
            b = pltpu.roll(y[HALF:, LANES * v : LANES * (v + 1)], HALF, 1)
            g = jnp.where(low, a, b)
            evens.append(g)
            row0[16 * i + 2 * v : 16 * i + 2 * v + 1, :] = g[0:1]
            if v < QCOLS // 2:
                g = jnp.where(low, b, a)
                odds.append(g)
                row0[16 * i + 2 * v + 1 : 16 * i + 2 * v + 2, :] = pltpu.roll(g[0:1], HALF, 1)
        row0[16 * i + QCOLS + 1 : 16 * i + 16, :] = jnp.zeros((7, LANES), f32)
        gh, gl = split(jnp.concatenate(evens, axis=0))
        de = dot(jnp.concatenate([gh, gl], axis=1), fwd[0:256]) + dot(gh, fwd[256:384])
        gh, gl = split(jnp.concatenate(odds, axis=0))
        do = dot(jnp.concatenate([gh, gl], axis=1), fwd[384:640]) + dot(gh, fwd[640:768])
        for j in range(QCOLS):
            v = j // 2
            if j % 2 == 0:
                first, second = de[HALF * v : HALF * (v + 1)], do[HALF * v : HALF * (v + 1)]
            else:
                first, second = do[HALF * v : HALF * (v + 1)], de[HALF * (v + 1) : HALF * (v + 2)]
            spec[slot, j] = first + second

    d0 = dot3(row0[...], edge_fwd[0:PATCH], edge_fwd[PATCH:])
    flip = (iota(d0.shape, 0) & iota(d0.shape, 1) & 1) == 1
    d0 = jnp.where(flip, -d0, d0)
    for i in range(6):
        slot = i if i < 2 else (q ^ (i - 2)) + 2
        spec0[slot] = d0[16 * i : 16 * i + QCOLS] + d0[16 * i + 1 : 16 * i + QCOLS + 1]
    products = []
    prior = []
    for s in range(SECTIONS):
        prev = s + 2 - off_s[s]
        prior.append(prev)
        f, g = spec0[s + 2], spec0[prev]
        parts = []
        for h in range(2):
            fr, fi = f[:, 256 * h : 256 * h + 128], f[:, 256 * h + 128 : 256 * h + 256]
            gr, gi = g[:, 256 * h : 256 * h + 128], g[:, 256 * h + 128 : 256 * h + 256]
            parts += [fr * gr + fi * gi, fi * gr - fr * gi]
        products.append(jnp.concatenate(parts, axis=1))
    u0 = dot3(jnp.concatenate(products, axis=0), edge_inv[0:512], edge_inv[512:])

    lane1 = iota((1, LANES), 1)
    shift_lane = jnp.where(lane1 < HALF, lane1, lane1 - PATCH).astype(f32)
    sub8 = iota((8, LANES), 0).astype(f32)
    scales = []
    for s in range(SECTIONS):
        prev = prior[s]
        scale8 = score_scale / jnp.sqrt(energy[s + 2] * energy[prev] + 1e-6)
        scales.append(scale8)
        highs, lows = [], []
        for j in range(QCOLS):
            f, g = spec[s + 2, j], spec[prev, j]
            fr, fi = f[:, :PATCH], f[:, PATCH:]
            gr, gi = g[:, :PATCH], g[:, PATCH:]
            ph, plo = split(jnp.concatenate([fr * gr + fi * gi, fi * gr - fr * gi], axis=1))
            highs.append(ph)
            lows.append(plo)
        ph, plo = jnp.concatenate(highs, axis=0), jnp.concatenate(lows, axis=0)
        u = dot(ph, inv2[0:256]) + dot(plo, inv2[0:256]) + dot(ph, inv2[256:512])
        for j in range(QCOLS):
            u_ref[s, j] = u[HALF * j : HALF * (j + 1)]
            u_ref[s, j, 0:1, :] = u0[QCOLS * s + j : QCOLS * s + j + 1]
        for j in range(0, QCOLS, 2):
            sides = []
            for k in (j, j + 1):
                uh, ul = split(u_ref[s, k])
                sides.append(
                    jnp.concatenate([uh[:, :PATCH], uh[:, PATCH:], ul[:, :PATCH], ul[:, PATCH:]], axis=0)
                )
            c2 = dot(back2[...], jnp.concatenate(sides, axis=1))
            both = c2[:PATCH] + c2[PATCH:]
            for k in (j, j + 1):
                c = both[:, PATCH * (k - j) : PATCH * (k - j + 1)]
                top = jnp.max(jnp.max(c, axis=0, keepdims=True), axis=1, keepdims=True)
                rate = scale8[k : k + 1, :]
                w = jnp.exp((c - top) * rate)
                total = w[0:8]
                moment = jnp.zeros((8, LANES), f32)
                for a in range(1, PATCH // 8):
                    block = w[8 * a : 8 * a + 8]
                    total = total + block
                    moment = moment + block * float(8 * a if 8 * a < HALF else 8 * a - PATCH)
                moment = moment + total * sub8
                total = jnp.sum(total, axis=0, keepdims=True)
                part[k, s : s + 1, :] = jnp.sum(moment, axis=0, keepdims=True)
                part[k, 4 + s : 5 + s, :] = total * shift_lane
                part[k, 8 + s : 9 + s, :] = total
                peak[k, s : s + 1, :] = jnp.broadcast_to(top, (1, LANES))

    lane16 = iota((FEATS, LANES), 1)
    lane4 = iota((SECTIONS, LANES), 1)
    lane8 = iota((QCOLS, LANES), 1)
    first_lane = q * QCOLS
    sums = jnp.zeros((FEATS, LANES), f32)
    tops = jnp.zeros((SECTIONS, LANES), f32)
    for j in range(QCOLS):
        part[j, 12:16, :] = jnp.zeros((4, LANES), f32)
        sums = sums + jnp.where(
            lane16 == first_lane + j, jnp.sum(part[j], axis=1, keepdims=True), 0.0
        )
        tops = tops + jnp.where(lane4 == first_lane + j, peak[j], 0.0)
    pick = lane8 == first_lane + iota((QCOLS, LANES), 0)
    rates = jnp.concatenate(
        [jnp.sum(jnp.where(pick, scale8, 0.0), axis=0, keepdims=True) for scale8 in scales], axis=0
    )
    mine = jnp.logical_and(lane4 >= first_lane, lane4 < first_lane + QCOLS)
    total = jnp.where(mine, sums[8:12], 1.0)
    out[0:4, :] = sums[0:4] / total
    out[4:8, :] = sums[4:8] / total
    out[8:12, :] = jnp.where(mine, (tops * rates + jnp.log(total)) / score_scale, 0.0)
    row4 = iota((SECTIONS, LANES), 0)
    flags = jnp.concatenate(
        [valid[0].astype(f32), jnp.broadcast_to(off[...], (1, COLS)), jnp.zeros((1, HALF), f32)],
        axis=1,
    )
    out[12:16, :] = jnp.where(row4 == q, flags, 0.0)


def relax_kernel(tile_count, own, near, far, third, flows_out, conf_out, pos_out):
    q = lax.axis_index("sec")
    t = lax.axis_index("tile")
    even = lax.rem(t, 2) == 0
    step = jnp.where(even, 1, -1)
    inside = lambda row: jnp.logical_and(row >= 0, row < tile_count)
    rows = [far[1], far[0], own[...], near[...], third[...]]
    shape = (2 * SECTIONS, LANES)
    lane = iota(shape, 1)
    row = iota(shape, 0)
    sec = lax.rem(row, SECTIONS)
    live = lane < COLS
    offsets = jnp.max(
        jnp.where(iota((SECTIONS, LANES), 1) >= COLS, own[12:16, :], 0.0), axis=1, keepdims=True
    )
    offsets = jnp.broadcast_to(jnp.concatenate([offsets, offsets], axis=0), shape)
    one = offsets < 1.5
    flows, stiff, present = [], [], []
    for i, cells in enumerate(rows):
        ok = jnp.logical_and(live, inside(t + step * (i - 2)))
        present.append(ok)
        flows.append(jnp.where(ok, cells[0:8], 0.0))
        stiffness = cells[8:12] * cells[12:16]
        stiff.append(jnp.where(ok, jnp.concatenate([stiffness, stiffness], axis=0), 0.0))

    def back(x, n):
        return jnp.where(sec >= n, pltpu.roll(x, n, 0), 0.0)

    def ahead(x, n):
        return jnp.where(sec < SECTIONS - n, pltpu.roll(x, 2 * SECTIONS - n, 0), 0.0)

    zero = jnp.zeros(shape, f32)
    positions = [zero] * 5
    for iteration in range(STEPS):
        new = list(positions)
        for i in range(iteration, 5 - iteration):
            p = positions[i]
            if iteration == 0:
                tension = stiff[i] * flows[i]
                bending = zero
            else:
                pulled = jnp.where(one, back(p, 1), back(p, 2))
                tension = stiff[i] * (p - pulled + flows[i])
                bending = (
                    4.0 * p
                    - positions[i - 1]
                    - positions[i + 1]
                    - pltpu.roll(p, 1, 1)
                    - pltpu.roll(p, LANES - 1, 1)
                )
            returned = ahead(jnp.where(one, tension, 0.0), 1) + ahead(jnp.where(one, 0.0, tension), 2)
            gradient = tension - returned + plane_weight * bending
            new[i] = jnp.where(present[i], p - spring_rate * gradient, 0.0)
        positions = new
    for c in range(2):
        chosen = row == q + SECTIONS * c
        flows_out[0, c] = jnp.sum(jnp.where(chosen, flows[2], 0.0), axis=0, keepdims=True)[:, :COLS]
        pos_out[0, c] = jnp.sum(jnp.where(chosen, positions[2], 0.0), axis=0, keepdims=True)[:, :COLS]
    chosen = iota((SECTIONS, LANES), 0) == q
    conf_out[0] = jnp.sum(jnp.where(chosen, own[8:12, :], 0.0), axis=0, keepdims=True)[:, :COLS]


def xor_route(count, d):
    return [(i, i ^ d) for i in range(count)]


def odd_route(count):
    return [(i, min(max(i + (1 if i % 2 else -1), 0), count - 1)) for i in range(count)]


def per_device(sections, earlier, offsets, patch_valid):
    tile_count = lax.axis_size("tile")
    q = lax.axis_index("sec")
    t = lax.axis_index("tile")
    even = t % 2 == 0
    swap_even = functools.partial(lax.ppermute, axis_name="tile", perm=xor_route(tile_count, 1))
    swap_odd = functools.partial(lax.ppermute, axis_name="tile", perm=odd_route(tile_count))
    width = 2 * RIM + COLS * HALF + HALF
    offset = offsets.astype(bf16)
    wide = jnp.pad(sections[0], ((0, 0), (RIM, width - RIM - COLS * HALF)))
    marked = lax.broadcasted_iota(jnp.int32, (HALF, MSG), 1) >= MSG - HALF

    def message(d):
        cut = lax.dynamic_slice_in_dim(wide, QPIX * (q ^ d), MSG, axis=1)
        return jnp.where(marked, offset[0], cut)

    messages = [message(d) for d in range(SECTIONS)]
    got = [messages[0]]
    for d in (2, 3, 1):
        got.append(lax.ppermute(messages[d], "sec", xor_route(SECTIONS, d)))
    got = [got[0], got[3], got[1], got[2]]
    eq = lax.dynamic_slice_in_dim(
        jnp.pad(earlier, ((0, 0), (0, 0), (RIM, width - RIM - COLS * HALF))), QPIX * q, MSG, axis=2
    )
    to_even = jnp.where(even, RIM, 0)
    to_odd = jnp.where(even, 0, RIM)
    e_even = swap_even(lax.dynamic_slice_in_dim(eq, to_even, RIM, axis=1))
    e_odd = swap_odd(lax.dynamic_slice_in_dim(eq, to_odd, RIM, axis=1))
    stacked = jnp.stack(got)
    h_odd = swap_odd(lax.dynamic_slice_in_dim(stacked, to_odd, RIM, axis=1))
    h_even = swap_even(lax.dynamic_slice_in_dim(stacked, to_even, RIM, axis=1))
    vmem = pl.BlockSpec(memory_space=pltpu.VMEM)
    consts = [jnp.asarray(x) for x in tables()]
    cells = pl.pallas_call(
        functools.partial(correlate_kernel, tile_count),
        out_shape=jax.ShapeDtypeStruct((FEATS, LANES), f32),
        in_specs=[vmem] * 17,
        out_specs=vmem,
        scratch_shapes=[
            pltpu.VMEM((6, PATCH, MSG), bf16),
            pltpu.VMEM((6, QCOLS, HALF, 256), f32),
            pltpu.VMEM((6, QCOLS, 512), f32),
            pltpu.VMEM((96, LANES), f32),
            pltpu.VMEM((6, QCOLS, LANES), f32),
            pltpu.VMEM((SECTIONS, QCOLS, HALF, 256), f32),
            pltpu.VMEM((QCOLS, FEATS, LANES), f32),
            pltpu.VMEM((QCOLS, SECTIONS, LANES), f32),
            pltpu.SMEM((SECTIONS,), jnp.int32),
        ],
        compiler_params=pltpu.CompilerParams(vmem_limit_bytes=48 * 1024 * 1024),
        name="correlate",
    )(*got, h_even, h_odd, eq, e_even, e_odd, patch_valid, offsets.astype(f32)[None], *consts)
    cells = cells + lax.ppermute(cells, "sec", xor_route(SECTIONS, 1))
    cells = cells + lax.ppermute(cells, "sec", xor_route(SECTIONS, 2))
    near = swap_even(cells)
    far = swap_odd(jnp.stack([cells, near]))
    third = swap_even(far[0])
    return pl.pallas_call(
        functools.partial(relax_kernel, tile_count),
        out_shape=(
            jax.ShapeDtypeStruct((1, 2, 1, COLS), f32),
            jax.ShapeDtypeStruct((1, 1, COLS), f32),
            jax.ShapeDtypeStruct((1, 2, 1, COLS), f32),
        ),
        in_specs=[vmem] * 4,
        out_specs=(vmem,) * 3,
        name="relax",
    )(cells, near, far, third)


def solution(mesh):
    in_specs = (P("sec", "tile", None), P(None, "tile", None), P("sec"), P("sec", "tile", None))
    out_specs = (P("sec", None, "tile", None), P("sec", "tile", None), P("sec", None, "tile", None))
    return jax.shard_map(
        per_device, mesh=mesh, in_specs=in_specs, out_specs=out_specs, check_vma=False
    )
```

profile of v0, /device:TPU:32, one launch (start us, length us, event | category | flops | bytes accessed | tf_op | source)
XLA Modules:
  0.0 72.7 jit_solution(2136082933653376194)
XLA Ops:
  1.3 1.2 %fusion.3 = (bf16[64,640]{1,0:T(8,128)(2,1)S(1)}, bf16[64,640]{1,0:T(8,128)(2,1)S(1)}, bf16[64,640]{1,0:T(8,128)(2,1)S(1)}, bf16[64,640]{1,0:T(8,128)(2,1)S(1)}) fusion(s32[]{:T(128)S(6)} %select_n.56, bf16[64,2048]{1,0:T(8,128)(2,1)} %bitcast.15, pred[640]{0:T(1024)(128)(4,1)S(1)} %iota_compare_fusion, bf16[]{:T(256)} %bitcast, s32[]{:T(128)S(6)} %select_n.52, ...), kind=kLoop, calls=%fused_computation.11 | loop fusion | flops 163840 | bytes 590482 | tf_op jit(solution)/shard_map/jit(_where)/select_n | solution.py:357
  2.5 0.1 collective-permute-start
  2.6 6.4 %collective-permute-start.1 = (bf16[64,640]{1,0:T(8,128)(2,1)S(1)}, bf16[64,640]{1,0:T(8,128)(2,1)S(1)}, u32[]{:S(2)}, u32[]{:S(2)}) collective-permute-start(bf16[64,640]{1,0:T(8,128)(2,1)S(1)} %get-tuple-element.9), channel_id=1, source_target_pairs={{0,128},{64,192},{128,0},{192,64},{1,129},{65,193},{129,1},{193,65... | collective-permute-start | bytes 245768 | tf_op jit(solution)/shard_map/ppermute | solution.py:362
  9.0 0.1 collective-permute-start.2
  9.1 0.0 collective-permute-done.m1
  9.1 6.1 %collective-permute-done.1.m2 = bf16[64,640]{1,0:T(8,128)(2,1)S(1)} collective-permute-done((bf16[64,640]{1,0:T(8,128)(2,1)S(1)}, bf16[64,640]{1,0:T(8,128)(2,1)S(1)}, u32[]{:S(2)}, u32[]{:S(2)}) %collective-permute-start.1) | collective-permute-done | bytes 81952 | tf_op jit(solution)/shard_map/ppermute | solution.py:362
  15.2 3.9 %collective-permute-done.2.m3 = bf16[64,640]{1,0:T(8,128)(2,1)S(1)} collective-permute-done((bf16[64,640]{1,0:T(8,128)(2,1)S(1)}, bf16[64,640]{1,0:T(8,128)(2,1)S(1)}, u32[]{:S(2)}, u32[]{:S(2)}) %collective-permute-start.2) | collective-permute-done | bytes 81952 | tf_op jit(solution)/shard_map/ppermute | solution.py:362
  19.1 0.1 pad_maximum_fusion
  19.2 0.0 copy-start.3
  19.2 0.1 constant_dynamic-slice_fusion
  19.2 1.6 %collective-permute-start.3 = (bf16[4,32,640]{2,1,0:T(8,128)(2,1)S(1)}, bf16[4,32,640]{2,1,0:T(8,128)(2,1)S(1)}, u32[]{:S(2)}, u32[]{:S(2)}) collective-permute-start(bf16[4,32,640]{2,1,0:T(8,128)(2,1)S(1)} %get-tuple-element.6), channel_id=1, source_target_pairs={{0,1},{1,0},{2,3},{3,2},{4,5},{5,4},{6,7},{7,6},{8,9},{9,8},{10,11... | collective-permute-start | bytes 491528 | tf_op jit(solution)/shard_map/ppermute | solution.py:373
  20.8 6.4 %collective-permute-start.4 = (bf16[4,32,640]{2,1,0:T(8,128)(2,1)S(1)}, bf16[4,32,640]{2,1,0:T(8,128)(2,1)S(1)}, u32[]{:S(2)}, u32[]{:S(2)}) collective-permute-start(bf16[4,32,640]{2,1,0:T(8,128)(2,1)S(1)} %get-tuple-element.5), channel_id=1, source_target_pairs={{0,0},{1,2},{2,1},{3,4},{4,3},{5,6},{6,5},{7,8},{8,7},{9,10},{10,9... | collective-permute-start | bytes 491528 | tf_op jit(solution)/shard_map/ppermute | solution.py:372
  27.2 0.0 copy-done.7
  27.2 0.0 copy-start.4
  27.2 0.0 copy-start.5
  27.2 0.2 pad_dynamic-slice_fusion
  27.4 0.0 copy-start.1
  27.4 0.1 collective-permute-start.5
  27.5 3.8 %collective-permute-start.6 = (bf16[2,32,640]{2,1,0:T(8,128)(2,1)S(1)}, bf16[2,32,640]{2,1,0:T(8,128)(2,1)S(1)}, u32[]{:S(2)}, u32[]{:S(2)}) collective-permute-start(bf16[2,32,640]{2,1,0:T(8,128)(2,1)S(1)} %get-tuple-element.3), channel_id=1, source_target_pairs={{0,0},{1,2},{2,1},{3,4},{4,3},{5,6},{6,5},{7,8},{8,7},{9,10},{10,9... | collective-permute-start | bytes 245768 | tf_op jit(solution)/shard_map/ppermute | solution.py:370
  31.3 0.0 copy-start.2
  31.3 0.1 pad_dynamic-slice_fusion.2.eq
  31.5 0.0 copy-start.6
  31.5 0.5 collective-permute-done.5.ehe
  31.9 6.1 %collective-permute-done.6.eho = bf16[2,32,640]{2,1,0:T(8,128)(2,1)S(1)} collective-permute-done((bf16[2,32,640]{2,1,0:T(8,128)(2,1)S(1)}, bf16[2,32,640]{2,1,0:T(8,128)(2,1)S(1)}, u32[]{:S(2)}, u32[]{:S(2)}) %collective-permute-start.6) | collective-permute-done | bytes 81952 | tf_op jit(solution)/shard_map/ppermute | solution.py:370
  38.1 0.0 collective-permute-done.3.he
  38.1 0.0 collective-permute-done.4.ho
  38.1 0.0 copy-done.3
  38.1 0.0 copy-done
  38.1 0.0 copy-done.4
  38.1 0.0 copy-done.5
  38.1 0.0 copy-done.1
  38.1 0.0 copy-done.2
  38.1 0.0 copy-done.6
  38.1 5.7 %correlate.1 = f32[16,128]{1,0:T(8,128)S(1)} custom-call(bf16[64,640]{1,0:T(8,128)(2,1)S(1)} %get-tuple-element.10.m0, bf16[64,640]{1,0:T(8,128)(2,1)S(1)} %collective-permute-done.m1, bf16[64,640]{1,0:T(8,128)(2,1)S(1)} %collective-permute-done.1.m2, bf16[64,640]{1,0:T(8,128)(2,1)S(1)} %collective-permute-done.2.m3, ...), custom_call_target="tpu_custom_call" | custom-call | tf_op jit(solution)/shard_map/correlate/pallas_call | solution.py:376
  43.9 0.1 collective-permute-start.7
  44.0 1.2 %collective-permute-done.7 = f32[16,128]{1,0:T(8,128)S(1)} collective-permute-done((f32[16,128]{1,0:T(8,128)S(1)}, f32[16,128]{1,0:T(8,128)S(1)}, u32[]{:S(2)}, u32[]{:S(2)}) %collective-permute-start.7) | collective-permute-done | bytes 8224 | tf_op jit(solution)/shard_map/ppermute | solution.py:395
  45.2 2.3 %collective-permute-start.8 = (f32[16,128]{1,0:T(8,128)S(1)}, f32[16,128]{1,0:T(8,128)S(1)}, u32[]{:S(2)}, u32[]{:S(2)}) collective-permute-start(f32[16,128]{1,0:T(8,128)S(1)} %add.42), channel_id=1, source_target_pairs={{0,128},{64,192},{128,0},{192,64},{1,129},{65,193},{129,1},{193,65... | collective-permute-start | bytes 24584 | tf_op jit(solution)/shard_map/ppermute | solution.py:396
  47.4 5.3 %collective-permute-done.8 = f32[16,128]{1,0:T(8,128)S(1)} collective-permute-done((f32[16,128]{1,0:T(8,128)S(1)}, f32[16,128]{1,0:T(8,128)S(1)}, u32[]{:S(2)}, u32[]{:S(2)}) %collective-permute-start.8) | collective-permute-done | bytes 8224 | tf_op jit(solution)/shard_map/ppermute | solution.py:396
  52.7 0.0 collective-permute-start.9
  52.7 3.6 %collective-permute-done.9.near = f32[16,128]{1,0:T(8,128)S(1)} collective-permute-done((f32[16,128]{1,0:T(8,128)S(1)}, f32[16,128]{1,0:T(8,128)S(1)}, u32[]{:S(2)}, u32[]{:S(2)}) %collective-permute-start.9) | collective-permute-done | bytes 8224 | tf_op jit(solution)/shard_map/ppermute | solution.py:397
  56.4 0.0 copy-done.8
  56.4 0.6 copy-done.10
  57.0 3.8 %collective-permute-start.10 = (f32[2,16,128]{2,1,0:T(8,128)S(1)}, f32[2,16,128]{2,1,0:T(8,128)S(1)}, u32[]{:S(2)}, u32[]{:S(2)}) collective-permute-start(f32[2,16,128]{2,1,0:T(8,128)S(1)} %pad_maximum_fusion.1), channel_id=1, source_target_pairs={{0,0},{1,2},{2,1},{3,4},{4,3},{5,6},{6,5},{7,8},{8,7},{9,10},{10,9... | collective-permute-start | bytes 49160 | tf_op jit(solution)/shard_map/ppermute | solution.py:398
  60.7 6.1 %collective-permute-done.10.far = f32[2,16,128]{2,1,0:T(8,128)S(1)} collective-permute-done((f32[2,16,128]{2,1,0:T(8,128)S(1)}, f32[2,16,128]{2,1,0:T(8,128)S(1)}, u32[]{:S(2)}, u32[]{:S(2)}) %collective-permute-start.10) | collective-permute-done | bytes 16416 | tf_op jit(solution)/shard_map/ppermute | solution.py:398
  66.8 0.0 collective-permute-start.11
  66.8 3.6 %collective-permute-done.11.third = f32[16,128]{1,0:T(8,128)S(1)} collective-permute-done((f32[16,128]{1,0:T(8,128)S(1)}, f32[16,128]{1,0:T(8,128)S(1)}, u32[]{:S(2)}, u32[]{:S(2)}) %collective-permute-start.11) | collective-permute-done | bytes 8224 | tf_op jit(solution)/shard_map/ppermute | solution.py:399
  70.5 0.6 copy-done.11
  71.1 1.6 %relax.1 = (f32[1,2,1,32]{3,2,1,0:T(1,128)}, f32[1,1,32]{2,1,0:T(1,128)}, f32[1,2,1,32]{3,2,1,0:T(1,128)}) custom-call(f32[16,128]{1,0:T(8,128)} %copy-done.8, f32[16,128]{1,0:T(8,128)} %copy-done.10, f32[2,16,128]{2,1,0:T(8,128)} %copy-done.9, f32[16,128]{1,0:T(8,128)} %copy-done.11), custom_call_target="tpu_custom_call" | custom-call | tf_op jit(solution)/shard_map/relax/pallas_call | solution.py:400
  (12 shorter events, 0.0 us)
Async XLA Ops:
  2.5 6.5 %collective-permute-start = (bf16[64,640]{1,0:T(8,128)(2,1)S(1)}, bf16[64,640]{1,0:T(8,128)(2,1)S(1)}, u32[]{:S(2)}, u32[]{:S(2)}) collective-permute-start(bf16[64,640]{1,0:T(8,128)(2,1)S(1)} %get-tuple-element.8), channel_id=1, source_target_pairs={{0,64},{64,0},{128,192},{192,128},{1,65},{65,1},{129,193},{193,129... | collective-permute-start | bytes 245768 | tf_op jit(solution)/shard_map/ppermute | solution.py:362
  2.6 12.5 %collective-permute-start.1 = (bf16[64,640]{1,0:T(8,128)(2,1)S(1)}, bf16[64,640]{1,0:T(8,128)(2,1)S(1)}, u32[]{:S(2)}, u32[]{:S(2)}) collective-permute-start(bf16[64,640]{1,0:T(8,128)(2,1)S(1)} %get-tuple-element.9), channel_id=1, source_target_pairs={{0,128},{64,192},{128,0},{192,64},{1,129},{65,193},{129,1},{193,65... | collective-permute-start | bytes 245768 | tf_op jit(solution)/shard_map/ppermute | solution.py:362
  9.0 10.1 %collective-permute-start.2 = (bf16[64,640]{1,0:T(8,128)(2,1)S(1)}, bf16[64,640]{1,0:T(8,128)(2,1)S(1)}, u32[]{:S(2)}, u32[]{:S(2)}) collective-permute-start(bf16[64,640]{1,0:T(8,128)(2,1)S(1)} %get-tuple-element.7), channel_id=1, source_target_pairs={{0,192},{64,128},{128,64},{192,0},{1,193},{65,129},{129,65},{193,1... | collective-permute-start | bytes 245768 | tf_op jit(solution)/shard_map/ppermute | solution.py:362
  19.1 8.1 %copy-start.7 = (bf16[2,64,2048]{2,1,0:T(8,128)(2,1)S(1)}, bf16[2,64,2048]{2,1,0:T(8,128)(2,1)}, u32[]{:S(2)}) copy-start(bf16[2,64,2048]{2,1,0:T(8,128)(2,1)} %param.11) | copy-start | bytes 1572868
  19.2 18.9 %copy-start.3 = (bf16[256,512]{1,0:T(8,128)(2,1)S(1)}, bf16[256,512]{1,0:T(8,128)(2,1)}, u32[]{:S(2)}) copy-start(bf16[256,512]{1,0:T(8,128)(2,1)} %constant.86.clone.edge_fwd) | copy-start | bytes 786436
  19.2 18.9 %collective-permute-start.3 = (bf16[4,32,640]{2,1,0:T(8,128)(2,1)S(1)}, bf16[4,32,640]{2,1,0:T(8,128)(2,1)S(1)}, u32[]{:S(2)}, u32[]{:S(2)}) collective-permute-start(bf16[4,32,640]{2,1,0:T(8,128)(2,1)S(1)} %get-tuple-element.6), channel_id=1, source_target_pairs={{0,1},{1,0},{2,3},{3,2},{4,5},{5,4},{6,7},{7,6},{8,9},{9,8},{10,11... | collective-permute-start | bytes 491528 | tf_op jit(solution)/shard_map/ppermute | solution.py:373
  20.8 17.3 %copy-start = (bf16[1024,256]{1,0:T(8,128)(2,1)S(1)}, bf16[1024,256]{1,0:T(8,128)(2,1)}, u32[]{:S(2)}) copy-start(bf16[1024,256]{1,0:T(8,128)(2,1)} %constant.87.clone.edge_inv) | copy-start | bytes 1572868
  20.8 17.3 %collective-permute-start.4 = (bf16[4,32,640]{2,1,0:T(8,128)(2,1)S(1)}, bf16[4,32,640]{2,1,0:T(8,128)(2,1)S(1)}, u32[]{:S(2)}, u32[]{:S(2)}) collective-permute-start(bf16[4,32,640]{2,1,0:T(8,128)(2,1)S(1)} %get-tuple-element.5), channel_id=1, source_target_pairs={{0,0},{1,2},{2,1},{3,4},{4,3},{5,6},{6,5},{7,8},{8,7},{9,10},{10,9... | collective-permute-start | bytes 491528 | tf_op jit(solution)/shard_map/ppermute | solution.py:372
  27.2 10.9 %copy-start.4 = (bf16[256,256]{1,0:T(8,128)(2,1)S(1)}, bf16[256,256]{1,0:T(8,128)(2,1)}, u32[]{:S(2)}) copy-start(bf16[256,256]{1,0:T(8,128)(2,1)} %constant.85.clone.back2) | copy-start | bytes 393220
  27.2 10.9 %copy-start.5 = (bf16[256,128]{1,0:T(8,128)(2,1)S(1)}, bf16[256,128]{1,0:T(8,128)(2,1)}, u32[]{:S(2)}) copy-start(bf16[256,128]{1,0:T(8,128)(2,1)} %constant.82.clone.rows2) | copy-start | bytes 196612
  27.4 10.7 %copy-start.1 = (bf16[768,256]{1,0:T(8,128)(2,1)S(1)}, bf16[768,256]{1,0:T(8,128)(2,1)}, u32[]{:S(2)}) copy-start(bf16[768,256]{1,0:T(8,128)(2,1)} %constant.83.clone.fwd) | copy-start | bytes 1179652
  27.4 4.5 %collective-permute-start.5 = (bf16[2,32,640]{2,1,0:T(8,128)(2,1)S(1)}, bf16[2,32,640]{2,1,0:T(8,128)(2,1)S(1)}, u32[]{:S(2)}, u32[]{:S(2)}) collective-permute-start(bf16[2,32,640]{2,1,0:T(8,128)(2,1)S(1)} %get-tuple-element.4), channel_id=1, source_target_pairs={{0,1},{1,0},{2,3},{3,2},{4,5},{5,4},{6,7},{7,6},{8,9},{9,8},{10,11... | collective-permute-start | bytes 245768 | tf_op jit(solution)/shard_map/ppermute | solution.py:369
  27.5 10.6 %collective-permute-start.6 = (bf16[2,32,640]{2,1,0:T(8,128)(2,1)S(1)}, bf16[2,32,640]{2,1,0:T(8,128)(2,1)S(1)}, u32[]{:S(2)}, u32[]{:S(2)}) collective-permute-start(bf16[2,32,640]{2,1,0:T(8,128)(2,1)S(1)} %get-tuple-element.3), channel_id=1, source_target_pairs={{0,0},{1,2},{2,1},{3,4},{4,3},{5,6},{6,5},{7,8},{8,7},{9,10},{10,9... | collective-permute-start | bytes 245768 | tf_op jit(solution)/shard_map/ppermute | solution.py:370
  31.3 6.8 %copy-start.2 = (bf16[512,256]{1,0:T(8,128)(2,1)S(1)}, bf16[512,256]{1,0:T(8,128)(2,1)}, u32[]{:S(2)}) copy-start(bf16[512,256]{1,0:T(8,128)(2,1)} %constant.84.clone.inv2) | copy-start | bytes 786436
  31.5 6.7 %copy-start.6 = (s32[1,1,32]{2,1,0:T(1,128)S(1)}, s32[1,1,32]{2,1,0:T(1,128)}, u32[]{:S(2)}) copy-start(s32[1,1,32]{2,1,0:T(1,128)} %valid.1) | copy-start | bytes 388
  43.9 1.3 %collective-permute-start.7 = (f32[16,128]{1,0:T(8,128)S(1)}, f32[16,128]{1,0:T(8,128)S(1)}, u32[]{:S(2)}, u32[]{:S(2)}) collective-permute-start(f32[16,128]{1,0:T(8,128)S(1)} %correlate.1), channel_id=1, source_target_pairs={{0,64},{64,0},{128,192},{192,128},{1,65},{65,1},{129,193},{193,129... | collective-permute-start | bytes 24584 | tf_op jit(solution)/shard_map/ppermute | solution.py:395
  45.2 7.6 %collective-permute-start.8 = (f32[16,128]{1,0:T(8,128)S(1)}, f32[16,128]{1,0:T(8,128)S(1)}, u32[]{:S(2)}, u32[]{:S(2)}) collective-permute-start(f32[16,128]{1,0:T(8,128)S(1)} %add.42), channel_id=1, source_target_pairs={{0,128},{64,192},{128,0},{192,64},{1,129},{65,193},{129,1},{193,65... | collective-permute-start | bytes 24584 | tf_op jit(solution)/shard_map/ppermute | solution.py:396
  52.7 3.7 %copy-start.8 = (f32[16,128]{1,0:T(8,128)}, f32[16,128]{1,0:T(8,128)S(1)}, u32[]{:S(2)}) copy-start(f32[16,128]{1,0:T(8,128)S(1)} %add.43.own) | copy-start | bytes 24580
  52.7 3.7 %collective-permute-start.9 = (f32[16,128]{1,0:T(8,128)S(1)}, f32[16,128]{1,0:T(8,128)S(1)}, u32[]{:S(2)}, u32[]{:S(2)}) collective-permute-start(f32[16,128]{1,0:T(8,128)S(1)} %add.43.own), channel_id=1, source_target_pairs={{0,1},{1,0},{2,3},{3,2},{4,5},{5,4},{6,7},{7,6},{8,9},{9,8},{10,11... | collective-permute-start | bytes 24584 | tf_op jit(solution)/shard_map/ppermute | solution.py:397
  56.4 0.6 copy-start.10
  57.0 9.8 %collective-permute-start.10 = (f32[2,16,128]{2,1,0:T(8,128)S(1)}, f32[2,16,128]{2,1,0:T(8,128)S(1)}, u32[]{:S(2)}, u32[]{:S(2)}) collective-permute-start(f32[2,16,128]{2,1,0:T(8,128)S(1)} %pad_maximum_fusion.1), channel_id=1, source_target_pairs={{0,0},{1,2},{2,1},{3,4},{4,3},{5,6},{6,5},{7,8},{8,7},{9,10},{10,9... | collective-permute-start | bytes 49160 | tf_op jit(solution)/shard_map/ppermute | solution.py:398
  66.8 3.7 %copy-start.9 = (f32[2,16,128]{2,1,0:T(8,128)}, f32[2,16,128]{2,1,0:T(8,128)S(1)}, u32[]{:S(2)}) copy-start(f32[2,16,128]{2,1,0:T(8,128)S(1)} %collective-permute-done.10.far) | copy-start | bytes 49156
  66.8 3.7 %collective-permute-start.11 = (f32[16,128]{1,0:T(8,128)S(1)}, f32[16,128]{1,0:T(8,128)S(1)}, u32[]{:S(2)}, u32[]{:S(2)}) collective-permute-start(f32[16,128]{1,0:T(8,128)S(1)} %slice_bitcast_fusion), channel_id=1, source_target_pairs={{0,1},{1,0},{2,3},{3,2},{4,5},{5,4},{6,7},{7,6},{8,9},{9,8},{10,11... | collective-permute-start | bytes 24584 | tf_op jit(solution)/shard_map/ppermute | solution.py:399
  70.5 0.6 copy-start.11
where the time goes:
time: 73 us; the launch traced here: 72.7 us
  waiting for transfers between devices  36.4 us (50%)
  starting transfers between devices  24.5 us (34%)
  Pallas kernels  7.39 us (10%)
  local copies, waits for them, and re-layouts  1.57 us (2%)
  between operations  1.53 us (2%)
  other arithmetic  1.27 us (2%)
    ppermute x3, waiting for transfers between devices, per_device(): got.append(lax.ppermute(messages[d], 'sec', xor_route(SECTIONS, d)))  10 us
    ppermute x3, starting transfers between devices, per_device(): got.append(lax.ppermute(messages[d], 'sec', xor_route(SECTIONS, d)))  6.52 us
    ppermute x1, starting transfers between devices, per_device(): h_odd = swap_odd(lax.dynamic_slice_in_dim(stacked, to_odd, RIM, axis=1))  6.4 us
    ppermute x1, waiting for transfers between devices, per_device(): e_odd = swap_odd(lax.dynamic_slice_in_dim(eq, to_odd, RIM, axis=1))  6.13 us
    ppermute x1, waiting for transfers between devices, per_device(): far = swap_odd(jnp.stack([cells, near]))  6.07 us
    pallas_call x1, Pallas kernels, per_device(): pl.pallas_call(functools.partial(correlate_kernel, tile_count), out_shape...  5.75 us
    ppermute x1, waiting for transfers between devices, per_device(): cells = cells + lax.ppermute(cells, 'sec', xor_route(SECTIONS, 2))  5.28 us
    ppermute x1, starting transfers between devices, per_device(): e_odd = swap_odd(lax.dynamic_slice_in_dim(eq, to_odd, RIM, axis=1))  3.78 us
  transfers between devices with their start and end apart: 12, of which 9 were waited for; matrix products, arithmetic and copies ran while one was open for 0% of the time, Pallas kernels for 0%

commit v1 on v0

--- a/solution.py
+++ b/solution.py
@@ -18,6 +18,7 @@
 QCOLS = COLS // SECTIONS
 QPIX = QCOLS * HALF
 MSG = QPIX + PATCH
+HALF_MSG = 2 * QPIX + PATCH
 LANES = 128
 FEATS = 16
 
@@ -109,7 +110,7 @@
 
 def correlate_kernel(
     tile_count,
-    m0, m1, m2, m3, he, ho, eq, ehe, eho, valid, off,
+    mine, sib, eq, near, far, valid, off,
     rows2, fwd, inv2, back2, edge_fwd, edge_inv,
     out,
     x_ref, spec, spec0, row0, energy, u_ref, part, peak, off_s,
@@ -117,21 +118,19 @@
     q = lax.axis_index("sec")
     t = lax.axis_index("tile")
     even = lax.rem(t, 2) == 0
-    messages = (m0, m1, m2, m3)
     at_even = pl.multiple_of(jnp.where(even, PATCH - RIM, 0), RIM)
     at_odd = pl.multiple_of(jnp.where(even, 0, PATCH - RIM), RIM)
     no_odd = jnp.logical_or(t == 0, t == tile_count - 1)
     keep = jnp.where(no_odd, 0.0, 1.0).astype(bf16)
-    for i in range(2):
-        x_ref[i, RIM : RIM + HALF, :] = eq[i]
-        x_ref[i, pl.ds(at_even, RIM), :] = ehe[i]
-        x_ref[i, pl.ds(at_odd, RIM), :] = eho[i] * keep
-    for d in range(SECTIONS):
-        x_ref[2 + d, RIM : RIM + HALF, :] = messages[d][...]
-        x_ref[2 + d, pl.ds(at_even, RIM), :] = he[d]
-        x_ref[2 + d, pl.ds(at_odd, RIM), :] = ho[d] * keep
-        section = q ^ d
-        off_s[section] = jnp.max(messages[d][:16, MSG - HALF :].astype(f32)).astype(jnp.int32)
+    centers = [eq.at[0], eq.at[1], mine.at[0], mine.at[1], sib.at[0], sib.at[1]]
+    slots = [0, 1, q + 2, (q ^ 2) + 2, (q ^ 1) + 2, (q ^ 3) + 2]
+    for i, center in enumerate(centers):
+        x_ref[i, RIM : RIM + HALF, :] = center[...]
+        x_ref[i, pl.ds(at_even, RIM), :] = near[i]
+        x_ref[i, pl.ds(at_odd, RIM), :] = far[i] * keep
+        if i >= 2:
+            offset = jnp.max(center[:16, MSG - HALF :].astype(f32))
+            off_s[slots[i] - 2] = offset.astype(jnp.int32)
 
     lane = iota((HALF, LANES), 1)
     low = lane < HALF
@@ -141,7 +140,7 @@
         window_lane >= window_row * HALF, window_lane < window_row * HALF + PATCH
     )
     for i in range(6):
-        slot = i if i < 2 else (q ^ (i - 2)) + 2
+        slot = slots[i]
         x = x_ref[i]
         xf = x.astype(f32)
         column = jnp.sum(xf * xf, axis=0, keepdims=True)
@@ -177,7 +176,7 @@
     flip = (iota(d0.shape, 0) & iota(d0.shape, 1) & 1) == 1
     d0 = jnp.where(flip, -d0, d0)
     for i in range(6):
-        slot = i if i < 2 else (q ^ (i - 2)) + 2
+        slot = slots[i]
         spec0[slot] = d0[16 * i : 16 * i + QCOLS] + d0[16 * i + 1 : 16 * i + QCOLS + 1]
     products = []
     prior = []
@@ -336,8 +335,14 @@
     return [(i, i ^ d) for i in range(count)]
 
 
-def odd_route(count):
-    return [(i, min(max(i + (1 if i % 2 else -1), 0), count - 1)) for i in range(count)]
+def joint_route(tile_count, odd):
+    route = []
+    for s in range(SECTIONS):
+        for t in range(tile_count):
+            to = t ^ 1 if not odd else t + (1 if t % 2 else -1)
+            pair = (s, to) if 0 <= to < tile_count else (s ^ 1, t)
+            route.append((s * tile_count + t, pair[0] * tile_count + pair[1]))
+    return route
 
 
 def per_device(sections, earlier, offsets, patch_valid):
@@ -345,38 +350,50 @@
     q = lax.axis_index("sec")
     t = lax.axis_index("tile")
     even = t % 2 == 0
-    swap_even = functools.partial(lax.ppermute, axis_name="tile", perm=xor_route(tile_count, 1))
-    swap_odd = functools.partial(lax.ppermute, axis_name="tile", perm=odd_route(tile_count))
-    width = 2 * RIM + COLS * HALF + HALF
-    offset = offsets.astype(bf16)
-    wide = jnp.pad(sections[0], ((0, 0), (RIM, width - RIM - COLS * HALF)))
-    marked = lax.broadcasted_iota(jnp.int32, (HALF, MSG), 1) >= MSG - HALF
-
-    def message(d):
-        cut = lax.dynamic_slice_in_dim(wide, QPIX * (q ^ d), MSG, axis=1)
-        return jnp.where(marked, offset[0], cut)
-
-    messages = [message(d) for d in range(SECTIONS)]
-    got = [messages[0]]
-    for d in (2, 3, 1):
-        got.append(lax.ppermute(messages[d], "sec", xor_route(SECTIONS, d)))
-    got = [got[0], got[3], got[1], got[2]]
+    swap = functools.partial(lax.ppermute, axis_name=("sec", "tile"))
+    swap_even = functools.partial(swap, perm=joint_route(tile_count, False))
+    swap_odd = functools.partial(swap, perm=joint_route(tile_count, True))
+    right = 2 * QPIX * (SECTIONS // 2 - 1) + HALF_MSG - RIM - COLS * HALF
+    offset = offsets.astype(bf16)[0]
+    wide = jnp.pad(sections[0], ((0, 0), (RIM, right)))
+    half_lane = lax.broadcasted_iota(jnp.int32, (HALF, HALF_MSG), 1)
+
+    def half(h):
+        cut = lax.dynamic_slice_in_dim(wide, 2 * QPIX * h, HALF_MSG, axis=1)
+        return jnp.where(half_lane >= HALF_MSG - HALF, offset, cut)
+
+    own = half(q // 2)
+    across = lax.ppermute(half(1 - q // 2), "sec", xor_route(SECTIONS, 2))
+
+    def quarter(strip, c):
+        cut = lax.dynamic_slice_in_dim(strip, QPIX * c, MSG - HALF, axis=1)
+        return jnp.concatenate([cut, strip[:, HALF_MSG - HALF :]], axis=1)
+
+    def quarters(c):
+        return jnp.stack([quarter(own, c), quarter(across, c)])
+
+    core = q % 2
+    mine = quarters(core)
+    sib = lax.ppermute(quarters(1 - core), "sec", xor_route(SECTIONS, 1))
     eq = lax.dynamic_slice_in_dim(
-        jnp.pad(earlier, ((0, 0), (0, 0), (RIM, width - RIM - COLS * HALF))), QPIX * q, MSG, axis=2
+        jnp.pad(earlier, ((0, 0), (0, 0), (RIM, right))), QPIX * q, MSG, axis=2
     )
     to_even = jnp.where(even, RIM, 0)
     to_odd = jnp.where(even, 0, RIM)
-    e_even = swap_even(lax.dynamic_slice_in_dim(eq, to_even, RIM, axis=1))
-    e_odd = swap_odd(lax.dynamic_slice_in_dim(eq, to_odd, RIM, axis=1))
-    stacked = jnp.stack(got)
-    h_odd = swap_odd(lax.dynamic_slice_in_dim(stacked, to_odd, RIM, axis=1))
-    h_even = swap_even(lax.dynamic_slice_in_dim(stacked, to_even, RIM, axis=1))
+
+    def rows(start):
+        return jnp.concatenate(
+            [lax.dynamic_slice_in_dim(x, start, RIM, axis=1) for x in (eq, mine, sib)], axis=0
+        )
+
+    far = swap_odd(rows(to_odd))
+    near = swap_even(rows(to_even))
     vmem = pl.BlockSpec(memory_space=pltpu.VMEM)
     consts = [jnp.asarray(x) for x in tables()]
     cells = pl.pallas_call(
         functools.partial(correlate_kernel, tile_count),
         out_shape=jax.ShapeDtypeStruct((FEATS, LANES), f32),
-        in_specs=[vmem] * 17,
+        in_specs=[vmem] * 13,
         out_specs=vmem,
         scratch_shapes=[
             pltpu.VMEM((6, PATCH, MSG), bf16),
@@ -391,7 +408,7 @@
         ],
         compiler_params=pltpu.CompilerParams(vmem_limit_bytes=48 * 1024 * 1024),
         name="correlate",
-    )(*got, h_even, h_odd, eq, e_even, e_odd, patch_valid, offsets.astype(f32)[None], *consts)
+    )(mine, sib, eq, near, far, patch_valid, offsets.astype(f32)[None], *consts)
     cells = cells + lax.ppermute(cells, "sec", xor_route(SECTIONS, 1))
     cells = cells + lax.ppermute(cells, "sec", xor_route(SECTIONS, 2))
     near = swap_even(cells)
@@ -406,6 +423,7 @@
         ),
         in_specs=[vmem] * 4,
         out_specs=(vmem,) * 3,
+        compiler_params=pltpu.CompilerParams(vmem_limit_bytes=8 * 1024 * 1024),
         name="relax",
     )(cells, near, far, third)
 

time: 73 us -> 62.2 us (0.85)
  waiting for transfers between devices: 36.4 us -> 30.3 us
  starting transfers between devices: 24.5 us -> 20.6 us
  Pallas kernels: 7.39 us -> 6.63 us
    ppermute x7 -> x4, starting transfers between devices: 18.4 us -> 9.63 us  [the longest x1 6.38 us: per_device(): across = lax.ppermute(half(1 - q // 2), 'sec', xor_route(SECTIONS, 2))]
    ppermute x1, starting transfers between devices: 2.28 us -> 6.19 us  [per_device(): cells = cells + lax.ppermute(cells, 'sec', xor_route(SECTIONS, 2))]
    ppermute x1, waiting for transfers between devices: 5.28 us -> 1.63 us  [per_device(): cells = cells + lax.ppermute(cells, 'sec', xor_route(SECTIONS, 2))]
    ppermute x1, waiting for transfers between devices: 6.07 us -> 3.59 us  [per_device(): far = swap_odd(jnp.stack([cells, near]))]
    pallas_call x1, Pallas kernels: 1.64 us -> 0.89 us  [per_device(): pl.pallas_call(functools.partial(relax_kernel, tile_count), out_shape=(ja...]
    ppermute x7 -> x4, waiting for transfers between devices: 16.6 us -> 16.9 us  [the longest x1 8.97 us: per_device(): far = swap_odd(rows(to_odd))]
  transfers between devices with their start and end apart: 12 -> 9, of which waited for: 9 -> 8; matrix products, arithmetic and copies ran while one was open for 0% -> 1% of each run, Pallas kernels for 0% -> 0%
where the time goes in v1:
time: 62.2 us; the launch traced here: 61.7 us
  waiting for transfers between devices  30.3 us (49%)
  starting transfers between devices  20.6 us (33%)
  Pallas kernels  6.63 us (11%)
  other arithmetic  1.71 us (3%)
  between operations  1.5 us (2%)
  local copies, waits for them, and re-layouts  1.04 us (2%)
    ppermute x1, waiting for transfers between devices, per_device(): far = swap_odd(rows(to_odd))  8.97 us
    ppermute x1, waiting for transfers between devices, per_device(): across = lax.ppermute(half(1 - q // 2), 'sec', xor_route(SECTIONS, 2))  6.76 us
    ppermute x1, starting transfers between devices, per_device(): across = lax.ppermute(half(1 - q // 2), 'sec', xor_route(SECTIONS, 2))  6.38 us
    ppermute x1, starting transfers between devices, per_device(): cells = cells + lax.ppermute(cells, 'sec', xor_route(SECTIONS, 2))  6.19 us
    pallas_call x1, Pallas kernels, per_device(): pl.pallas_call(functools.partial(correlate_kernel, tile_count), out_shape...  5.74 us
    ppermute x1, starting transfers between devices, per_device(): far = swap_odd(jnp.stack([cells, near]))  4.36 us
    ppermute x1, waiting for transfers between devices, per_device(): third = swap_even(far[0])  3.65 us
    ppermute x1, waiting for transfers between devices, per_device(): far = swap_odd(jnp.stack([cells, near]))  3.59 us
  transfers between devices with their start and end apart: 9, of which 8 were waited for; matrix products, arithmetic and copies ran while one was open for 1% of the time, Pallas kernels for 0%

profile of v1, /device:TPU:32, one launch (start us, length us, event | category | flops | bytes accessed | tf_op | source)
XLA Modules:
  0.0 61.7 jit_solution(18171142835452084234)
XLA Ops:
  1.3 1.1 %fusion = (bf16[64,1152]{1,0:T(8,128)(2,1)S(1)}, bf16[64,1152]{1,0:T(8,128)(2,1)S(1)}) fusion(s32[]{:T(128)S(6)} %select_n.60, bf16[64,2048]{1,0:T(8,128)(2,1)} %bitcast.17, pred[1152]{0:T(1024)(128)(4,1)S(1)} %iota_compare_fusion, bf16[]{:T(256)} %bitcast, s32[]{:T(128)S(6)} %select_n.64), kind=kLoop, calls=%fused_computation.13 | loop fusion | flops 147456 | bytes 558218 | tf_op jit(solution)/shard_map/jit(_where)/select_n | solution.py:363
  2.5 6.4 %collective-permute-start = (bf16[64,1152]{1,0:T(8,128)(2,1)S(1)}, bf16[64,1152]{1,0:T(8,128)(2,1)S(1)}, u32[]{:S(2)}, u32[]{:S(2)}) collective-permute-start(bf16[64,1152]{1,0:T(8,128)(2,1)S(1)} %get-tuple-element.6), channel_id=1, source_target_pairs={{0,128},{64,192},{128,0},{192,64},{1,129},{65,193},{129,1},{193,65... | collective-permute-start | bytes 442376 | tf_op jit(solution)/shard_map/ppermute | solution.py:366
  8.9 0.1 constant_dynamic-slice_fusion.3
  9.0 0.1 slice.14
  9.1 0.1 fusion.5
  9.1 0.0 copy-start.7
  9.2 6.8 %collective-permute-done = bf16[64,1152]{1,0:T(8,128)(2,1)S(1)} collective-permute-done((bf16[64,1152]{1,0:T(8,128)(2,1)S(1)}, bf16[64,1152]{1,0:T(8,128)(2,1)S(1)}, u32[]{:S(2)}, u32[]{:S(2)}) %collective-permute-start) | collective-permute-done | bytes 147488 | tf_op jit(solution)/shard_map/ppermute | solution.py:366
  15.9 0.1 constant_dynamic-slice_fusion.2
  16.0 0.1 slice.15
  16.1 0.1 fusion.3
  16.2 0.1 collective-permute-start.1
  16.4 0.0 copy-done.7
  16.4 0.2 pad_dynamic-slice_fusion
  16.5 1.2 %collective-permute-done.1.sib = bf16[2,64,640]{2,1,0:T(8,128)(2,1)S(1)} collective-permute-done((bf16[2,64,640]{2,1,0:T(8,128)(2,1)S(1)}, bf16[2,64,640]{2,1,0:T(8,128)(2,1)S(1)}, u32[]{:S(2)}, u32[]{:S(2)}) %collective-permute-start.1) | collective-permute-done | bytes 163872 | tf_op jit(solution)/shard_map/ppermute | solution.py:377
  17.7 0.0 copy-start.4
  17.8 2.6 %collective-permute-start.3 = (bf16[6,32,640]{2,1,0:T(8,128)(2,1)S(1)}, bf16[6,32,640]{2,1,0:T(8,128)(2,1)S(1)}, u32[]{:S(2)}, u32[]{:S(2)}) collective-permute-start(bf16[6,32,640]{2,1,0:T(8,128)(2,1)S(1)} %pad_maximum_fusion.1), channel_id=1, source_target_pairs={{0,64},{1,2},{2,1},{3,4},{4,3},{5,6},{6,5},{7,8},{8,7},{9,10},{10,... | collective-permute-start | bytes 737288 | tf_op jit(solution)/shard_map/ppermute | solution.py:389
  20.4 0.0 copy-start.2
  20.4 0.0 copy-start.3
  20.5 0.0 copy-start
  20.5 0.5 collective-permute-start.2
  21.0 0.0 copy-start.1
  21.0 0.0 copy-start.5
  21.0 0.1 pad_dynamic-slice_fusion.2
  21.1 9.0 %collective-permute-done.3.far = bf16[6,32,640]{2,1,0:T(8,128)(2,1)S(1)} collective-permute-done((bf16[6,32,640]{2,1,0:T(8,128)(2,1)S(1)}, bf16[6,32,640]{2,1,0:T(8,128)(2,1)S(1)}, u32[]{:S(2)}, u32[]{:S(2)}) %collective-permute-start.3) | collective-permute-done | bytes 245792 | tf_op jit(solution)/shard_map/ppermute | solution.py:389
  30.1 0.0 collective-permute-done.2.near
  30.1 0.0 copy-start.6
  30.1 0.0 copy-done.4
  30.1 0.0 copy-done.2
  30.1 0.0 copy-done.3
  30.1 0.0 copy-done
  30.1 0.0 copy-done.1
  30.1 0.0 copy-done.5
  30.2 0.6 copy-done.6
  30.8 5.7 %correlate.1 = f32[16,128]{1,0:T(8,128)S(1)} custom-call(bf16[2,64,640]{2,1,0:T(8,128)(2,1)S(1)} %get-tuple-element.22.mine, bf16[2,64,640]{2,1,0:T(8,128)(2,1)S(1)} %collective-permute-done.1.sib, bf16[2,64,640]{2,1,0:T(8,128)(2,1)S(1)} %get-tuple-element.21.eq, bf16[6,32,640]{2,1,0:T(8,128)(2,1)S(1)} %collective-permute-done.2.near, ...), custom_call_target="tpu_custom_call" | custom-call | tf_op jit(solution)/shard_map/correlate/pallas_call | solution.py:393
  36.5 0.1 collective-permute-start.4
  36.6 1.2 %collective-permute-done.4 = f32[16,128]{1,0:T(8,128)S(1)} collective-permute-done((f32[16,128]{1,0:T(8,128)S(1)}, f32[16,128]{1,0:T(8,128)S(1)}, u32[]{:S(2)}, u32[]{:S(2)}) %collective-permute-start.4) | collective-permute-done | bytes 8224 | tf_op jit(solution)/shard_map/ppermute | solution.py:412
  37.8 6.2 %collective-permute-start.5 = (f32[16,128]{1,0:T(8,128)S(1)}, f32[16,128]{1,0:T(8,128)S(1)}, u32[]{:S(2)}, u32[]{:S(2)}) collective-permute-start(f32[16,128]{1,0:T(8,128)S(1)} %add.54), channel_id=1, source_target_pairs={{0,128},{64,192},{128,0},{192,64},{1,129},{65,193},{129,1},{193,65... | collective-permute-start | bytes 24584 | tf_op jit(solution)/shard_map/ppermute | solution.py:413
  44.0 1.6 %collective-permute-done.5 = f32[16,128]{1,0:T(8,128)S(1)} collective-permute-done((f32[16,128]{1,0:T(8,128)S(1)}, f32[16,128]{1,0:T(8,128)S(1)}, u32[]{:S(2)}, u32[]{:S(2)}) %collective-permute-start.5) | collective-permute-done | bytes 8224 | tf_op jit(solution)/shard_map/ppermute | solution.py:413
  45.6 0.3 collective-permute-start.6
  45.9 3.4 %collective-permute-done.6.near = f32[16,128]{1,0:T(8,128)S(1)} collective-permute-done((f32[16,128]{1,0:T(8,128)S(1)}, f32[16,128]{1,0:T(8,128)S(1)}, u32[]{:S(2)}, u32[]{:S(2)}) %collective-permute-start.6) | collective-permute-done | bytes 8224 | tf_op jit(solution)/shard_map/ppermute | solution.py:414
  49.2 4.4 %collective-permute-start.7 = (f32[2,16,128]{2,1,0:T(8,128)S(1)}, f32[2,16,128]{2,1,0:T(8,128)S(1)}, u32[]{:S(2)}, u32[]{:S(2)}) collective-permute-start(f32[2,16,128]{2,1,0:T(8,128)S(1)} %pad_maximum_fusion.8), channel_id=1, source_target_pairs={{0,64},{1,2},{2,1},{3,4},{4,3},{5,6},{6,5},{7,8},{8,7},{9,10},{10,... | collective-permute-start | bytes 49160 | tf_op jit(solution)/shard_map/ppermute | solution.py:415
  53.6 3.6 %collective-permute-done.7.far = f32[2,16,128]{2,1,0:T(8,128)S(1)} collective-permute-done((f32[2,16,128]{2,1,0:T(8,128)S(1)}, f32[2,16,128]{2,1,0:T(8,128)S(1)}, u32[]{:S(2)}, u32[]{:S(2)}) %collective-permute-start.7) | collective-permute-done | bytes 16416 | tf_op jit(solution)/shard_map/ppermute | solution.py:415
  57.2 0.0 collective-permute-start.8
  57.2 3.6 %collective-permute-done.8.third = f32[16,128]{1,0:T(8,128)S(1)} collective-permute-done((f32[16,128]{1,0:T(8,128)S(1)}, f32[16,128]{1,0:T(8,128)S(1)}, u32[]{:S(2)}, u32[]{:S(2)}) %collective-permute-start.8) | collective-permute-done | bytes 8224 | tf_op jit(solution)/shard_map/ppermute | solution.py:416
  60.9 0.9 %relax.1 = (f32[1,2,1,32]{3,2,1,0:T(1,128)}, f32[1,1,32]{2,1,0:T(1,128)}, f32[1,2,1,32]{3,2,1,0:T(1,128)}) custom-call(f32[16,128]{1,0:T(8,128)S(1)} %add.55.own, f32[16,128]{1,0:T(8,128)S(1)} %collective-permute-done.6.near, f32[2,16,128]{2,1,0:T(8,128)S(1)} %collective-permute-done.7.far, f32[16,128]{1,0:T(8,128)S(1)} %collective-permute-done.8.third), custom_call_target="tpu_custom_call" | custom-call | tf_op jit(solution)/shard_map/relax/pallas_call | solution.py:417
  (9 shorter events, 0.1 us)
Async XLA Ops:
  2.5 13.4 %collective-permute-start = (bf16[64,1152]{1,0:T(8,128)(2,1)S(1)}, bf16[64,1152]{1,0:T(8,128)(2,1)S(1)}, u32[]{:S(2)}, u32[]{:S(2)}) collective-permute-start(bf16[64,1152]{1,0:T(8,128)(2,1)S(1)} %get-tuple-element.6), channel_id=1, source_target_pairs={{0,128},{64,192},{128,0},{192,64},{1,129},{65,193},{129,1},{193,65... | collective-permute-start | bytes 442376 | tf_op jit(solution)/shard_map/ppermute | solution.py:366
  9.1 7.2 %copy-start.7 = (bf16[2,64,2048]{2,1,0:T(8,128)(2,1)S(1)}, bf16[2,64,2048]{2,1,0:T(8,128)(2,1)}, u32[]{:S(2)}) copy-start(bf16[2,64,2048]{2,1,0:T(8,128)(2,1)} %param.11) | copy-start | bytes 1572868
  16.2 1.5 %collective-permute-start.1 = (bf16[2,64,640]{2,1,0:T(8,128)(2,1)S(1)}, bf16[2,64,640]{2,1,0:T(8,128)(2,1)S(1)}, u32[]{:S(2)}, u32[]{:S(2)}) collective-permute-start(bf16[2,64,640]{2,1,0:T(8,128)(2,1)S(1)} %pad_maximum_fusion.3), channel_id=1, source_target_pairs={{0,64},{64,0},{128,192},{192,128},{1,65},{65,1},{129,193},{193,129... | collective-permute-start | bytes 491528 | tf_op jit(solution)/shard_map/ppermute | solution.py:377
  17.7 12.4 %copy-start.4 = (bf16[256,256]{1,0:T(8,128)(2,1)S(1)}, bf16[256,256]{1,0:T(8,128)(2,1)}, u32[]{:S(2)}) copy-start(bf16[256,256]{1,0:T(8,128)(2,1)} %constant.104.clone.back2) | copy-start | bytes 393220
  17.8 12.3 %collective-permute-start.3 = (bf16[6,32,640]{2,1,0:T(8,128)(2,1)S(1)}, bf16[6,32,640]{2,1,0:T(8,128)(2,1)S(1)}, u32[]{:S(2)}, u32[]{:S(2)}) collective-permute-start(bf16[6,32,640]{2,1,0:T(8,128)(2,1)S(1)} %pad_maximum_fusion.1), channel_id=1, source_target_pairs={{0,64},{1,2},{2,1},{3,4},{4,3},{5,6},{6,5},{7,8},{8,7},{9,10},{10,... | collective-permute-start | bytes 737288 | tf_op jit(solution)/shard_map/ppermute | solution.py:389
  20.4 9.7 %copy-start.2 = (bf16[512,256]{1,0:T(8,128)(2,1)S(1)}, bf16[512,256]{1,0:T(8,128)(2,1)}, u32[]{:S(2)}) copy-start(bf16[512,256]{1,0:T(8,128)(2,1)} %constant.103.clone.inv2) | copy-start | bytes 786436
  20.4 9.7 %copy-start.3 = (bf16[256,512]{1,0:T(8,128)(2,1)S(1)}, bf16[256,512]{1,0:T(8,128)(2,1)}, u32[]{:S(2)}) copy-start(bf16[256,512]{1,0:T(8,128)(2,1)} %constant.105.clone.edge_fwd) | copy-start | bytes 786436
  20.5 9.7 %copy-start = (bf16[1024,256]{1,0:T(8,128)(2,1)S(1)}, bf16[1024,256]{1,0:T(8,128)(2,1)}, u32[]{:S(2)}) copy-start(bf16[1024,256]{1,0:T(8,128)(2,1)} %constant.106.clone.edge_inv) | copy-start | bytes 1572868
  20.5 9.6 %collective-permute-start.2 = (bf16[6,32,640]{2,1,0:T(8,128)(2,1)S(1)}, bf16[6,32,640]{2,1,0:T(8,128)(2,1)S(1)}, u32[]{:S(2)}, u32[]{:S(2)}) collective-permute-start(bf16[6,32,640]{2,1,0:T(8,128)(2,1)S(1)} %pad_maximum_fusion), channel_id=1, source_target_pairs={{0,1},{1,0},{2,3},{3,2},{4,5},{5,4},{6,7},{7,6},{8,9},{9,8},{10,11... | collective-permute-start | bytes 737288 | tf_op jit(solution)/shard_map/ppermute | solution.py:390
  21.0 9.1 %copy-start.1 = (bf16[768,256]{1,0:T(8,128)(2,1)S(1)}, bf16[768,256]{1,0:T(8,128)(2,1)}, u32[]{:S(2)}) copy-start(bf16[768,256]{1,0:T(8,128)(2,1)} %constant.102.clone.fwd) | copy-start | bytes 1179652
  21.0 9.1 %copy-start.5 = (bf16[256,128]{1,0:T(8,128)(2,1)S(1)}, bf16[256,128]{1,0:T(8,128)(2,1)}, u32[]{:S(2)}) copy-start(bf16[256,128]{1,0:T(8,128)(2,1)} %constant.101.clone.rows2) | copy-start | bytes 196612
  30.1 0.7 %copy-start.6 = (s32[1,1,32]{2,1,0:T(1,128)S(1)}, s32[1,1,32]{2,1,0:T(1,128)}, u32[]{:S(2)}) copy-start(s32[1,1,32]{2,1,0:T(1,128)} %valid.1) | copy-start | bytes 388
  36.5 1.3 %collective-permute-start.4 = (f32[16,128]{1,0:T(8,128)S(1)}, f32[16,128]{1,0:T(8,128)S(1)}, u32[]{:S(2)}, u32[]{:S(2)}) collective-permute-start(f32[16,128]{1,0:T(8,128)S(1)} %correlate.1), channel_id=1, source_target_pairs={{0,64},{64,0},{128,192},{192,128},{1,65},{65,1},{129,193},{193,129... | collective-permute-start | bytes 24584 | tf_op jit(solution)/shard_map/ppermute | solution.py:412
  37.8 7.8 %collective-permute-start.5 = (f32[16,128]{1,0:T(8,128)S(1)}, f32[16,128]{1,0:T(8,128)S(1)}, u32[]{:S(2)}, u32[]{:S(2)}) collective-permute-start(f32[16,128]{1,0:T(8,128)S(1)} %add.54), channel_id=1, source_target_pairs={{0,128},{64,192},{128,0},{192,64},{1,129},{65,193},{129,1},{193,65... | collective-permute-start | bytes 24584 | tf_op jit(solution)/shard_map/ppermute | solution.py:413
  45.6 3.7 %collective-permute-start.6 = (f32[16,128]{1,0:T(8,128)S(1)}, f32[16,128]{1,0:T(8,128)S(1)}, u32[]{:S(2)}, u32[]{:S(2)}) collective-permute-start(f32[16,128]{1,0:T(8,128)S(1)} %add.55.own), channel_id=1, source_target_pairs={{0,1},{1,0},{2,3},{3,2},{4,5},{5,4},{6,7},{7,6},{8,9},{9,8},{10,11... | collective-permute-start | bytes 24584 | tf_op jit(solution)/shard_map/ppermute | solution.py:414
  49.2 8.0 %collective-permute-start.7 = (f32[2,16,128]{2,1,0:T(8,128)S(1)}, f32[2,16,128]{2,1,0:T(8,128)S(1)}, u32[]{:S(2)}, u32[]{:S(2)}) collective-permute-start(f32[2,16,128]{2,1,0:T(8,128)S(1)} %pad_maximum_fusion.8), channel_id=1, source_target_pairs={{0,64},{1,2},{2,1},{3,4},{4,3},{5,6},{6,5},{7,8},{8,7},{9,10},{10,... | collective-permute-start | bytes 49160 | tf_op jit(solution)/shard_map/ppermute | solution.py:415
  57.2 3.7 %collective-permute-start.8 = (f32[16,128]{1,0:T(8,128)S(1)}, f32[16,128]{1,0:T(8,128)S(1)}, u32[]{:S(2)}, u32[]{:S(2)}) collective-permute-start(f32[16,128]{1,0:T(8,128)S(1)} %slice_bitcast_fusion), channel_id=1, source_target_pairs={{0,1},{1,0},{2,3},{3,2},{4,5},{5,4},{6,7},{7,6},{8,9},{9,8},{10,11... | collective-permute-start | bytes 24584 | tf_op jit(solution)/shard_map/ppermute | solution.py:416

commit v2 on v1

--- a/solution.py
+++ b/solution.py
@@ -43,7 +43,6 @@
     c[np.abs(c) < 1e-12] = 0.0
     s[np.abs(s) < 1e-12] = 0.0
     alt = (-1.0) ** n
-    z = np.zeros_like(c)
     rows = np.concatenate([c[:HALF], alt[None], s[1:HALF]], axis=0)
     rows_hi, rows_lo = split_table(rows)
     rows2 = np.concatenate([rows_hi, rows_lo], axis=0)
@@ -66,27 +65,11 @@
         [np.concatenate([back_hi, back_hi], axis=1), np.concatenate([back_lo, back_lo], axis=1)],
         axis=0,
     )
-    pair = np.concatenate([c[:HALF], -s[:HALF]], axis=1)
-    zero = np.zeros_like(pair)
-    edge_fwd = np.concatenate(
-        [np.concatenate([pair, zero], axis=1), np.concatenate([zero, pair], axis=1)], axis=0
-    )
-    edge_inv = np.concatenate(
-        [
-            np.concatenate([c, z], axis=1),
-            np.concatenate([-s, z], axis=1),
-            np.concatenate([z, c], axis=1),
-            np.concatenate([z, -s], axis=1),
-        ],
-        axis=0,
-    )
     return (
         rows2,
         fwd,
         inv2,
         back2,
-        np.concatenate(split_table(edge_fwd), axis=0),
-        np.concatenate(split_table(edge_inv), axis=0),
     )
 
 
@@ -111,7 +94,7 @@
 def correlate_kernel(
     tile_count,
     mine, sib, eq, near, far, valid, off,
-    rows2, fwd, inv2, back2, edge_fwd, edge_inv,
+    rows2, fwd, inv2, back2,
     out,
     x_ref, spec, spec0, row0, energy, u_ref, part, peak, off_s,
 ):
@@ -172,25 +155,26 @@
                 first, second = do[HALF * v : HALF * (v + 1)], de[HALF * (v + 1) : HALF * (v + 2)]
             spec[slot, j] = first + second
 
-    d0 = dot3(row0[...], edge_fwd[0:PATCH], edge_fwd[PATCH:])
+    edges = row0[...]
+    edges = jnp.concatenate([edges, pltpu.roll(edges, HALF, 1)], axis=0)[:, :HALF]
+    d0 = dot3(edges, fwd[0:HALF], fwd[256 : 256 + HALF])
     flip = (iota(d0.shape, 0) & iota(d0.shape, 1) & 1) == 1
     d0 = jnp.where(flip, -d0, d0)
     for i in range(6):
-        slot = slots[i]
-        spec0[slot] = d0[16 * i : 16 * i + QCOLS] + d0[16 * i + 1 : 16 * i + QCOLS + 1]
+        for h in range(2):
+            first = 96 * h + 16 * i
+            spec0[slots[i], h] = d0[first : first + QCOLS] + d0[first + 1 : first + QCOLS + 1]
     products = []
     prior = []
     for s in range(SECTIONS):
         prev = s + 2 - off_s[s]
         prior.append(prev)
-        f, g = spec0[s + 2], spec0[prev]
-        parts = []
         for h in range(2):
-            fr, fi = f[:, 256 * h : 256 * h + 128], f[:, 256 * h + 128 : 256 * h + 256]
-            gr, gi = g[:, 256 * h : 256 * h + 128], g[:, 256 * h + 128 : 256 * h + 256]
-            parts += [fr * gr + fi * gi, fi * gr - fr * gi]
-        products.append(jnp.concatenate(parts, axis=1))
-    u0 = dot3(jnp.concatenate(products, axis=0), edge_inv[0:512], edge_inv[512:])
+            f, g = spec0[s + 2, h], spec0[prev, h]
+            fr, fi = f[:, :PATCH], f[:, PATCH:]
+            gr, gi = g[:, :PATCH], g[:, PATCH:]
+            products.append(jnp.concatenate([fr * gr + fi * gi, fi * gr - fr * gi], axis=1))
+    u0 = dot3(jnp.concatenate(products, axis=0), inv2[0:256, 0:PATCH], inv2[256:512, 0:PATCH])
 
     lane1 = iota((1, LANES), 1)
     shift_lane = jnp.where(lane1 < HALF, lane1, lane1 - PATCH).astype(f32)
@@ -212,7 +196,9 @@
         u = dot(ph, inv2[0:256]) + dot(plo, inv2[0:256]) + dot(ph, inv2[256:512])
         for j in range(QCOLS):
             u_ref[s, j] = u[HALF * j : HALF * (j + 1)]
-            u_ref[s, j, 0:1, :] = u0[QCOLS * s + j : QCOLS * s + j + 1]
+            first = 2 * QCOLS * s + j
+            u_ref[s, j, 0:1, :PATCH] = u0[first : first + 1]
+            u_ref[s, j, 0:1, PATCH:] = u0[first + QCOLS : first + QCOLS + 1]
         for j in range(0, QCOLS, 2):
             sides = []
             for k in (j, j + 1):
@@ -269,20 +255,22 @@
     out[12:16, :] = jnp.where(row4 == q, flags, 0.0)
 
 
-def relax_kernel(tile_count, own, near, far, third, flows_out, conf_out, pos_out):
+def relax_kernel(tile_count, mine, sib, flows_out, conf_out, pos_out):
     q = lax.axis_index("sec")
     t = lax.axis_index("tile")
     even = lax.rem(t, 2) == 0
     step = jnp.where(even, 1, -1)
     inside = lambda row: jnp.logical_and(row >= 0, row < tile_count)
-    rows = [far[1], far[0], own[...], near[...], third[...]]
+    bundle = jnp.where(lax.rem(q, 2) == 1, mine[...], sib[...])
+    own, near, far, beyond, third = [bundle[i] for i in range(5)]
+    rows = [beyond, far, own, near, third]
     shape = (2 * SECTIONS, LANES)
     lane = iota(shape, 1)
     row = iota(shape, 0)
     sec = lax.rem(row, SECTIONS)
     live = lane < COLS
     offsets = jnp.max(
-        jnp.where(iota((SECTIONS, LANES), 1) >= COLS, own[12:16, :], 0.0), axis=1, keepdims=True
+        jnp.where(iota((SECTIONS, LANES), 1) >= COLS, own[12:16], 0.0), axis=1, keepdims=True
     )
     offsets = jnp.broadcast_to(jnp.concatenate([offsets, offsets], axis=0), shape)
     one = offsets < 1.5
@@ -328,7 +316,7 @@
         flows_out[0, c] = jnp.sum(jnp.where(chosen, flows[2], 0.0), axis=0, keepdims=True)[:, :COLS]
         pos_out[0, c] = jnp.sum(jnp.where(chosen, positions[2], 0.0), axis=0, keepdims=True)[:, :COLS]
     chosen = iota((SECTIONS, LANES), 0) == q
-    conf_out[0] = jnp.sum(jnp.where(chosen, own[8:12, :], 0.0), axis=0, keepdims=True)[:, :COLS]
+    conf_out[0] = jnp.sum(jnp.where(chosen, own[8:12], 0.0), axis=0, keepdims=True)[:, :COLS]
 
 
 def xor_route(count, d):
@@ -341,6 +329,20 @@
         for t in range(tile_count):
             to = t ^ 1 if not odd else t + (1 if t % 2 else -1)
             pair = (s, to) if 0 <= to < tile_count else (s ^ 1, t)
+            route.append((s * tile_count + t, pair[0] * tile_count + pair[1]))
+    return route
+
+
+def gather_route(tile_count, kind):
+    route = []
+    for s in range(SECTIONS):
+        for t in range(tile_count):
+            pair = (s, t ^ 1)
+            if s % 2 == 1 and kind == "z":
+                pair = (s ^ 2, t)
+            if s % 2 == 1 and kind == "odd":
+                to = t + (1 if t % 2 else -1)
+                pair = (s, to) if 0 <= to < tile_count else (s ^ 2, t)
             route.append((s * tile_count + t, pair[0] * tile_count + pair[1]))
     return route
 
@@ -393,12 +395,12 @@
     cells = pl.pallas_call(
         functools.partial(correlate_kernel, tile_count),
         out_shape=jax.ShapeDtypeStruct((FEATS, LANES), f32),
-        in_specs=[vmem] * 13,
+        in_specs=[vmem] * 11,
         out_specs=vmem,
         scratch_shapes=[
             pltpu.VMEM((6, PATCH, MSG), bf16),
             pltpu.VMEM((6, QCOLS, HALF, 256), f32),
-            pltpu.VMEM((6, QCOLS, 512), f32),
+            pltpu.VMEM((6, 2, QCOLS, 256), f32),
             pltpu.VMEM((96, LANES), f32),
             pltpu.VMEM((6, QCOLS, LANES), f32),
             pltpu.VMEM((SECTIONS, QCOLS, HALF, 256), f32),
@@ -410,10 +412,12 @@
         name="correlate",
     )(mine, sib, eq, near, far, patch_valid, offsets.astype(f32)[None], *consts)
     cells = cells + lax.ppermute(cells, "sec", xor_route(SECTIONS, 1))
-    cells = cells + lax.ppermute(cells, "sec", xor_route(SECTIONS, 2))
-    near = swap_even(cells)
-    far = swap_odd(jnp.stack([cells, near]))
-    third = swap_even(far[0])
+    cells = cells + swap(cells, perm=gather_route(tile_count, "z"))
+    near = swap(cells, perm=gather_route(tile_count, "even"))
+    far = swap(jnp.stack([cells, near]), perm=gather_route(tile_count, "odd"))
+    third = swap(far[0], perm=gather_route(tile_count, "even"))
+    bundle = jnp.stack([cells, near, far[0], far[1], third])
+    shared = lax.ppermute(bundle, "sec", xor_route(SECTIONS, 1))
     return pl.pallas_call(
         functools.partial(relax_kernel, tile_count),
         out_shape=(
@@ -421,11 +425,11 @@
             jax.ShapeDtypeStruct((1, 1, COLS), f32),
             jax.ShapeDtypeStruct((1, 2, 1, COLS), f32),
         ),
-        in_specs=[vmem] * 4,
+        in_specs=[vmem] * 2,
         out_specs=(vmem,) * 3,
         compiler_params=pltpu.CompilerParams(vmem_limit_bytes=8 * 1024 * 1024),
         name="relax",
-    )(cells, near, far, third)
+    )(bundle, shared)
 
 
 def solution(mesh):

time: 62.2 us -> 59.6 us (0.958)
  starting transfers between devices: 20.6 us -> 14 us
  waiting for transfers between devices: 30.3 us -> 33.6 us
    ppermute x4 -> x5, starting transfers between devices: 10.8 us -> 4.25 us  [the longest x1 4.24 us: per_device(): shared = lax.ppermute(bundle, 'sec', xor_route(SECTIONS, 1))]
    ppermute x4 -> x5, waiting for transfers between devices: 12.2 us -> 15.5 us  [the longest x1 3.74 us: per_device(): far = swap(jnp.stack([cells, near]), perm=gather_route(tile_count, 'odd'))]
  transfers between devices with their start and end apart: 9 -> 10, of which waited for: 8 -> 9; matrix products, arithmetic and copies ran while one was open for 1% -> 1% of each run, Pallas kernels for 0% -> 0%
where the time goes in v2:
time: 59.6 us; the launch traced here: 58.9 us
  waiting for transfers between devices  33.6 us (56%)
  starting transfers between devices  14 us (23%)
  Pallas kernels  7.06 us (12%)
  other arithmetic  1.72 us (3%)
  between operations  1.48 us (2%)
  local copies, waits for them, and re-layouts  1.04 us (2%)
    ppermute x1, waiting for transfers between devices, per_device(): far = swap_odd(rows(to_odd))  8.97 us
    ppermute x1, waiting for transfers between devices, per_device(): across = lax.ppermute(half(1 - q // 2), 'sec', xor_route(SECTIONS, 2))  6.76 us
    ppermute x1, starting transfers between devices, per_device(): across = lax.ppermute(half(1 - q // 2), 'sec', xor_route(SECTIONS, 2))  6.38 us
    pallas_call x1, Pallas kernels, per_device(): pl.pallas_call(functools.partial(correlate_kernel, tile_count), out_shape...  6.17 us
    ppermute x1, starting transfers between devices, per_device(): shared = lax.ppermute(bundle, 'sec', xor_route(SECTIONS, 1))  4.24 us
    ppermute x1, waiting for transfers between devices, per_device(): far = swap(jnp.stack([cells, near]), perm=gather_route(tile_count, 'odd'))  3.74 us
    ppermute x1, waiting for transfers between devices, per_device(): cells = cells + swap(cells, perm=gather_route(tile_count, 'z'))  3.65 us
    ppermute x1, waiting for transfers between devices, per_device(): near = swap(cells, perm=gather_route(tile_count, 'even'))  3.65 us
  transfers between devices with their start and end apart: 10, of which 9 were waited for; matrix products, arithmetic and copies ran while one was open for 1% of the time, Pallas kernels for 0%

profile of v2, /device:TPU:32, one launch (start us, length us, event | category | flops | bytes accessed | tf_op | source)
XLA Modules:
  0.0 58.9 jit_solution(6789526102686428943)
XLA Ops:
  1.3 1.1 %fusion = (bf16[64,1152]{1,0:T(8,128)(2,1)S(1)}, bf16[64,1152]{1,0:T(8,128)(2,1)S(1)}) fusion(s32[]{:T(128)S(6)} %select_n.60, bf16[64,2048]{1,0:T(8,128)(2,1)} %bitcast.16, pred[1152]{0:T(1024)(128)(4,1)S(1)} %iota_compare_fusion, bf16[]{:T(256)} %bitcast, s32[]{:T(128)S(6)} %select_n.64), kind=kLoop, calls=%fused_computation.13 | loop fusion | flops 147456 | bytes 558218 | tf_op jit(solution)/shard_map/jit(_where)/select_n | solution.py:365
  2.5 6.4 %collective-permute-start = (bf16[64,1152]{1,0:T(8,128)(2,1)S(1)}, bf16[64,1152]{1,0:T(8,128)(2,1)S(1)}, u32[]{:S(2)}, u32[]{:S(2)}) collective-permute-start(bf16[64,1152]{1,0:T(8,128)(2,1)S(1)} %get-tuple-element.6), channel_id=1, source_target_pairs={{0,128},{64,192},{128,0},{192,64},{1,129},{65,193},{129,1},{193,65... | collective-permute-start | bytes 442376 | tf_op jit(solution)/shard_map/ppermute | solution.py:368
  8.9 0.1 constant_dynamic-slice_fusion.3
  9.0 0.1 slice.17
  9.1 0.1 fusion.5
  9.1 0.0 copy-start.5
  9.2 6.8 %collective-permute-done = bf16[64,1152]{1,0:T(8,128)(2,1)S(1)} collective-permute-done((bf16[64,1152]{1,0:T(8,128)(2,1)S(1)}, bf16[64,1152]{1,0:T(8,128)(2,1)S(1)}, u32[]{:S(2)}, u32[]{:S(2)}) %collective-permute-start) | collective-permute-done | bytes 147488 | tf_op jit(solution)/shard_map/ppermute | solution.py:368
  15.9 0.1 constant_dynamic-slice_fusion.2
  16.0 0.1 slice.18
  16.1 0.1 fusion.3
  16.2 0.1 collective-permute-start.1
  16.4 0.0 copy-done.5
  16.4 0.2 pad_dynamic-slice_fusion
  16.5 1.2 %collective-permute-done.1.sib = bf16[2,64,640]{2,1,0:T(8,128)(2,1)S(1)} collective-permute-done((bf16[2,64,640]{2,1,0:T(8,128)(2,1)S(1)}, bf16[2,64,640]{2,1,0:T(8,128)(2,1)S(1)}, u32[]{:S(2)}, u32[]{:S(2)}) %collective-permute-start.1) | collective-permute-done | bytes 163872 | tf_op jit(solution)/shard_map/ppermute | solution.py:379
  17.8 2.6 %collective-permute-start.3 = (bf16[6,32,640]{2,1,0:T(8,128)(2,1)S(1)}, bf16[6,32,640]{2,1,0:T(8,128)(2,1)S(1)}, u32[]{:S(2)}, u32[]{:S(2)}) collective-permute-start(bf16[6,32,640]{2,1,0:T(8,128)(2,1)S(1)} %pad_maximum_fusion.1), channel_id=1, source_target_pairs={{0,64},{1,2},{2,1},{3,4},{4,3},{5,6},{6,5},{7,8},{8,7},{9,10},{10,... | collective-permute-start | bytes 737288 | tf_op jit(solution)/shard_map/ppermute | solution.py:391
  20.4 0.5 collective-permute-start.2
  21.0 0.0 copy-start
  21.0 0.0 copy-start.1
  21.0 0.0 copy-start.2
  21.0 0.0 copy-start.3
  21.0 0.1 pad_dynamic-slice_fusion.2
  21.1 9.0 %collective-permute-done.3.far = bf16[6,32,640]{2,1,0:T(8,128)(2,1)S(1)} collective-permute-done((bf16[6,32,640]{2,1,0:T(8,128)(2,1)S(1)}, bf16[6,32,640]{2,1,0:T(8,128)(2,1)S(1)}, u32[]{:S(2)}, u32[]{:S(2)}) %collective-permute-start.3) | collective-permute-done | bytes 245792 | tf_op jit(solution)/shard_map/ppermute | solution.py:391
  30.1 0.0 collective-permute-done.2.near
  30.1 0.0 copy-start.4
  30.1 0.0 copy-done
  30.1 0.0 copy-done.1
  30.1 0.0 copy-done.2
  30.1 0.0 copy-done.3
  30.1 0.6 %copy-done.4 = s32[1,1,32]{2,1,0:T(1,128)S(1)} copy-done((s32[1,1,32]{2,1,0:T(1,128)S(1)}, s32[1,1,32]{2,1,0:T(1,128)}, u32[]{:S(2)}) %copy-start.4) | copy-done | bytes 152
  30.7 6.2 %correlate.1 = f32[16,128]{1,0:T(8,128)S(1)} custom-call(bf16[2,64,640]{2,1,0:T(8,128)(2,1)S(1)} %get-tuple-element.22.mine, bf16[2,64,640]{2,1,0:T(8,128)(2,1)S(1)} %collective-permute-done.1.sib, bf16[2,64,640]{2,1,0:T(8,128)(2,1)S(1)} %get-tuple-element.21.eq, bf16[6,32,640]{2,1,0:T(8,128)(2,1)S(1)} %collective-permute-done.2.near, ...), custom_call_target="tpu_custom_call" | custom-call | tf_op jit(solution)/shard_map/correlate/pallas_call | solution.py:395
  36.9 0.1 collective-permute-start.4
  37.0 1.2 %collective-permute-done.4 = f32[16,128]{1,0:T(8,128)S(1)} collective-permute-done((f32[16,128]{1,0:T(8,128)S(1)}, f32[16,128]{1,0:T(8,128)S(1)}, u32[]{:S(2)}, u32[]{:S(2)}) %collective-permute-start.4) | collective-permute-done | bytes 8224 | tf_op jit(solution)/shard_map/ppermute | solution.py:414
  38.2 0.0 collective-permute-start.5
  38.2 3.6 %collective-permute-done.5 = f32[16,128]{1,0:T(8,128)S(1)} collective-permute-done((f32[16,128]{1,0:T(8,128)S(1)}, f32[16,128]{1,0:T(8,128)S(1)}, u32[]{:S(2)}, u32[]{:S(2)}) %collective-permute-start.5) | collective-permute-done | bytes 8224 | tf_op jit(solution)/shard_map/ppermute | solution.py:415
  41.8 0.0 collective-permute-start.6
  41.8 3.6 %collective-permute-done.6 = f32[16,128]{1,0:T(8,128)S(1)} collective-permute-done((f32[16,128]{1,0:T(8,128)S(1)}, f32[16,128]{1,0:T(8,128)S(1)}, u32[]{:S(2)}, u32[]{:S(2)}) %collective-permute-start.6) | collective-permute-done | bytes 8224 | tf_op jit(solution)/shard_map/ppermute | solution.py:416
  45.5 0.0 collective-permute-start.7
  45.5 3.7 %collective-permute-done.7 = f32[2,16,128]{2,1,0:T(8,128)S(1)} collective-permute-done((f32[2,16,128]{2,1,0:T(8,128)S(1)}, f32[2,16,128]{2,1,0:T(8,128)S(1)}, u32[]{:S(2)}, u32[]{:S(2)}) %collective-permute-start.7) | collective-permute-done | bytes 16416 | tf_op jit(solution)/shard_map/ppermute | solution.py:417
  49.2 0.0 collective-permute-start.8
  49.2 3.6 %collective-permute-done.8 = f32[16,128]{1,0:T(8,128)S(1)} collective-permute-done((f32[16,128]{1,0:T(8,128)S(1)}, f32[16,128]{1,0:T(8,128)S(1)}, u32[]{:S(2)}, u32[]{:S(2)}) %collective-permute-start.8) | collective-permute-done | bytes 8224 | tf_op jit(solution)/shard_map/ppermute | solution.py:418
  52.9 4.2 %collective-permute-start.9 = (f32[5,16,128]{2,1,0:T(8,128)S(1)}, f32[5,16,128]{2,1,0:T(8,128)S(1)}, u32[]{:S(2)}, u32[]{:S(2)}) collective-permute-start(f32[5,16,128]{2,1,0:T(8,128)S(1)} %pad_maximum_fusion.8.mine), channel_id=1, source_target_pairs={{0,64},{64,0},{128,192},{192,128},{1,65},{65,1},{129,193},{193,129... | collective-permute-start | bytes 122888 | tf_op jit(solution)/shard_map/ppermute | solution.py:420
  57.1 0.9 %collective-permute-done.9.sib = f32[5,16,128]{2,1,0:T(8,128)S(1)} collective-permute-done((f32[5,16,128]{2,1,0:T(8,128)S(1)}, f32[5,16,128]{2,1,0:T(8,128)S(1)}, u32[]{:S(2)}, u32[]{:S(2)}) %collective-permute-start.9) | collective-permute-done | bytes 40992 | tf_op jit(solution)/shard_map/ppermute | solution.py:420
  58.0 0.9 %relax.1 = (f32[1,2,1,32]{3,2,1,0:T(1,128)}, f32[1,1,32]{2,1,0:T(1,128)}, f32[1,2,1,32]{3,2,1,0:T(1,128)}) custom-call(f32[5,16,128]{2,1,0:T(8,128)S(1)} %pad_maximum_fusion.8.mine, f32[5,16,128]{2,1,0:T(8,128)S(1)} %collective-permute-done.9.sib), custom_call_target="tpu_custom_call" | custom-call | tf_op jit(solution)/shard_map/relax/pallas_call | solution.py:421
  (10 shorter events, 0.1 us)
Async XLA Ops:
  2.5 13.4 %collective-permute-start = (bf16[64,1152]{1,0:T(8,128)(2,1)S(1)}, bf16[64,1152]{1,0:T(8,128)(2,1)S(1)}, u32[]{:S(2)}, u32[]{:S(2)}) collective-permute-start(bf16[64,1152]{1,0:T(8,128)(2,1)S(1)} %get-tuple-element.6), channel_id=1, source_target_pairs={{0,128},{64,192},{128,0},{192,64},{1,129},{65,193},{129,1},{193,65... | collective-permute-start | bytes 442376 | tf_op jit(solution)/shard_map/ppermute | solution.py:368
  9.1 7.2 %copy-start.5 = (bf16[2,64,2048]{2,1,0:T(8,128)(2,1)S(1)}, bf16[2,64,2048]{2,1,0:T(8,128)(2,1)}, u32[]{:S(2)}) copy-start(bf16[2,64,2048]{2,1,0:T(8,128)(2,1)} %param.9) | copy-start | bytes 1572868
  16.2 1.5 %collective-permute-start.1 = (bf16[2,64,640]{2,1,0:T(8,128)(2,1)S(1)}, bf16[2,64,640]{2,1,0:T(8,128)(2,1)S(1)}, u32[]{:S(2)}, u32[]{:S(2)}) collective-permute-start(bf16[2,64,640]{2,1,0:T(8,128)(2,1)S(1)} %pad_maximum_fusion.3), channel_id=1, source_target_pairs={{0,64},{64,0},{128,192},{192,128},{1,65},{65,1},{129,193},{193,129... | collective-permute-start | bytes 491528 | tf_op jit(solution)/shard_map/ppermute | solution.py:379
  17.8 12.3 %collective-permute-start.3 = (bf16[6,32,640]{2,1,0:T(8,128)(2,1)S(1)}, bf16[6,32,640]{2,1,0:T(8,128)(2,1)S(1)}, u32[]{:S(2)}, u32[]{:S(2)}) collective-permute-start(bf16[6,32,640]{2,1,0:T(8,128)(2,1)S(1)} %pad_maximum_fusion.1), channel_id=1, source_target_pairs={{0,64},{1,2},{2,1},{3,4},{4,3},{5,6},{6,5},{7,8},{8,7},{9,10},{10,... | collective-permute-start | bytes 737288 | tf_op jit(solution)/shard_map/ppermute | solution.py:391
  20.4 9.6 %collective-permute-start.2 = (bf16[6,32,640]{2,1,0:T(8,128)(2,1)S(1)}, bf16[6,32,640]{2,1,0:T(8,128)(2,1)S(1)}, u32[]{:S(2)}, u32[]{:S(2)}) collective-permute-start(bf16[6,32,640]{2,1,0:T(8,128)(2,1)S(1)} %pad_maximum_fusion), channel_id=1, source_target_pairs={{0,1},{1,0},{2,3},{3,2},{4,5},{5,4},{6,7},{7,6},{8,9},{9,8},{10,11... | collective-permute-start | bytes 737288 | tf_op jit(solution)/shard_map/ppermute | solution.py:392
  21.0 9.1 %copy-start = (bf16[768,256]{1,0:T(8,128)(2,1)S(1)}, bf16[768,256]{1,0:T(8,128)(2,1)}, u32[]{:S(2)}) copy-start(bf16[768,256]{1,0:T(8,128)(2,1)} %constant.98.clone.fwd) | copy-start | bytes 1179652
  21.0 9.1 %copy-start.1 = (bf16[512,256]{1,0:T(8,128)(2,1)S(1)}, bf16[512,256]{1,0:T(8,128)(2,1)}, u32[]{:S(2)}) copy-start(bf16[512,256]{1,0:T(8,128)(2,1)} %constant.99.clone.inv2) | copy-start | bytes 786436
  21.0 9.1 %copy-start.2 = (bf16[256,256]{1,0:T(8,128)(2,1)S(1)}, bf16[256,256]{1,0:T(8,128)(2,1)}, u32[]{:S(2)}) copy-start(bf16[256,256]{1,0:T(8,128)(2,1)} %constant.100.clone.back2) | copy-start | bytes 393220
  21.0 9.1 %copy-start.3 = (bf16[256,128]{1,0:T(8,128)(2,1)S(1)}, bf16[256,128]{1,0:T(8,128)(2,1)}, u32[]{:S(2)}) copy-start(bf16[256,128]{1,0:T(8,128)(2,1)} %constant.97.clone.rows2) | copy-start | bytes 196612
  30.1 0.7 %copy-start.4 = (s32[1,1,32]{2,1,0:T(1,128)S(1)}, s32[1,1,32]{2,1,0:T(1,128)}, u32[]{:S(2)}) copy-start(s32[1,1,32]{2,1,0:T(1,128)} %valid.1) | copy-start | bytes 388
  36.9 1.3 %collective-permute-start.4 = (f32[16,128]{1,0:T(8,128)S(1)}, f32[16,128]{1,0:T(8,128)S(1)}, u32[]{:S(2)}, u32[]{:S(2)}) collective-permute-start(f32[16,128]{1,0:T(8,128)S(1)} %correlate.1), channel_id=1, source_target_pairs={{0,64},{64,0},{128,192},{192,128},{1,65},{65,1},{129,193},{193,129... | collective-permute-start | bytes 24584 | tf_op jit(solution)/shard_map/ppermute | solution.py:414
  38.2 3.7 %collective-permute-start.5 = (f32[16,128]{1,0:T(8,128)S(1)}, f32[16,128]{1,0:T(8,128)S(1)}, u32[]{:S(2)}, u32[]{:S(2)}) collective-permute-start(f32[16,128]{1,0:T(8,128)S(1)} %add.54), channel_id=1, source_target_pairs={{0,1},{1,0},{2,3},{3,2},{4,5},{5,4},{6,7},{7,6},{8,9},{9,8},{10,11... | collective-permute-start | bytes 24584 | tf_op jit(solution)/shard_map/ppermute | solution.py:415
  41.8 3.7 %collective-permute-start.6 = (f32[16,128]{1,0:T(8,128)S(1)}, f32[16,128]{1,0:T(8,128)S(1)}, u32[]{:S(2)}, u32[]{:S(2)}) collective-permute-start(f32[16,128]{1,0:T(8,128)S(1)} %add.55), channel_id=1, source_target_pairs={{0,1},{1,0},{2,3},{3,2},{4,5},{5,4},{6,7},{7,6},{8,9},{9,8},{10,11... | collective-permute-start | bytes 24584 | tf_op jit(solution)/shard_map/ppermute | solution.py:416
  45.5 3.7 %collective-permute-start.7 = (f32[2,16,128]{2,1,0:T(8,128)S(1)}, f32[2,16,128]{2,1,0:T(8,128)S(1)}, u32[]{:S(2)}, u32[]{:S(2)}) collective-permute-start(f32[2,16,128]{2,1,0:T(8,128)S(1)} %pad_maximum_fusion.9), channel_id=1, source_target_pairs={{0,1},{1,0},{2,3},{3,2},{4,5},{5,4},{6,7},{7,6},{8,9},{9,8},{10,11... | collective-permute-start | bytes 49160 | tf_op jit(solution)/shard_map/ppermute | solution.py:417
  49.2 3.7 %collective-permute-start.8 = (f32[16,128]{1,0:T(8,128)S(1)}, f32[16,128]{1,0:T(8,128)S(1)}, u32[]{:S(2)}, u32[]{:S(2)}) collective-permute-start(f32[16,128]{1,0:T(8,128)S(1)} %slice_bitcast_fusion), channel_id=1, source_target_pairs={{0,1},{1,0},{2,3},{3,2},{4,5},{5,4},{6,7},{7,6},{8,9},{9,8},{10,11... | collective-permute-start | bytes 24584 | tf_op jit(solution)/shard_map/ppermute | solution.py:418
  52.9 5.1 %collective-permute-start.9 = (f32[5,16,128]{2,1,0:T(8,128)S(1)}, f32[5,16,128]{2,1,0:T(8,128)S(1)}, u32[]{:S(2)}, u32[]{:S(2)}) collective-permute-start(f32[5,16,128]{2,1,0:T(8,128)S(1)} %pad_maximum_fusion.8.mine), channel_id=1, source_target_pairs={{0,64},{64,0},{128,192},{192,128},{1,65},{65,1},{129,193},{193,129... | collective-permute-start | bytes 122888 | tf_op jit(solution)/shard_map/ppermute | solution.py:420

commit v3 on v2

--- a/solution.py
+++ b/solution.py
@@ -18,7 +18,6 @@
 QCOLS = COLS // SECTIONS
 QPIX = QCOLS * HALF
 MSG = QPIX + PATCH
-HALF_MSG = 2 * QPIX + PATCH
 LANES = 128
 FEATS = 16
 
@@ -91,30 +90,36 @@
     return lax.broadcasted_iota(jnp.int32, shape, dim)
 
 
-def correlate_kernel(
-    tile_count,
-    mine, sib, eq, near, far, valid, off,
-    rows2, fwd, inv2, back2,
-    out,
-    x_ref, spec, spec0, row0, energy, u_ref, part, peak, off_s,
-):
+def prepare_kernel(strip, off, keep, send, wide):
     q = lax.axis_index("sec")
+    h, c = lax.div(q, 2), lax.rem(q, 2)
+    blank = jnp.zeros((HALF, LANES), bf16)
+    wide[:, :LANES] = blank
+    wide[:, LANES : LANES + COLS * HALF] = strip[0]
+    wide[:, LANES + COLS * HALF :] = blank
+    offset = off[0].astype(f32)
+    marked = iota((HALF, MSG), 1) >= MSG - HALF
+    for out, core in ((keep, c), (send, 1 - c)):
+        for i, side in enumerate((h, 1 - h)):
+            start = pl.multiple_of(QPIX * (2 * side + core), LANES)
+            cut = wide[:, pl.ds(start, MSG + LANES)].astype(f32)
+            cut = pltpu.roll(cut, MSG + RIM, 1)[:, :MSG]
+            out[i] = jnp.where(marked, offset, cut).astype(bf16)
+
+
+def place(x_ref, i, center, near, far, tile_count):
     t = lax.axis_index("tile")
     even = lax.rem(t, 2) == 0
     at_even = pl.multiple_of(jnp.where(even, PATCH - RIM, 0), RIM)
     at_odd = pl.multiple_of(jnp.where(even, 0, PATCH - RIM), RIM)
     no_odd = jnp.logical_or(t == 0, t == tile_count - 1)
     keep = jnp.where(no_odd, 0.0, 1.0).astype(bf16)
-    centers = [eq.at[0], eq.at[1], mine.at[0], mine.at[1], sib.at[0], sib.at[1]]
-    slots = [0, 1, q + 2, (q ^ 2) + 2, (q ^ 1) + 2, (q ^ 3) + 2]
-    for i, center in enumerate(centers):
-        x_ref[i, RIM : RIM + HALF, :] = center[...]
-        x_ref[i, pl.ds(at_even, RIM), :] = near[i]
-        x_ref[i, pl.ds(at_odd, RIM), :] = far[i] * keep
-        if i >= 2:
-            offset = jnp.max(center[:16, MSG - HALF :].astype(f32))
-            off_s[slots[i] - 2] = offset.astype(jnp.int32)
-
+    x_ref[i, RIM : RIM + HALF, :] = center
+    x_ref[i, pl.ds(at_even, RIM), :] = near
+    x_ref[i, pl.ds(at_odd, RIM), :] = far * keep
+
+
+def transform(x_ref, row0, count, rows2, fwd, spec_at, edge_at, energy_at):
     lane = iota((HALF, LANES), 1)
     low = lane < HALF
     window_row = iota((QCOLS, MSG), 0)
@@ -122,13 +127,12 @@
     in_window = jnp.logical_and(
         window_lane >= window_row * HALF, window_lane < window_row * HALF + PATCH
     )
-    for i in range(6):
-        slot = slots[i]
+    for i in range(count):
         x = x_ref[i]
         xf = x.astype(f32)
         column = jnp.sum(xf * xf, axis=0, keepdims=True)
         windows = jnp.sum(jnp.where(in_window, column, 0.0), axis=1, keepdims=True)
-        energy[slot] = jnp.broadcast_to(windows, (QCOLS, LANES))
+        energy_at(i)[...] = jnp.broadcast_to(windows, (QCOLS, LANES))
         y2 = dot(rows2[...], x)
         y = y2[:PATCH] + y2[PATCH:]
         evens, odds = [], []
@@ -153,17 +157,59 @@
                 first, second = de[HALF * v : HALF * (v + 1)], do[HALF * v : HALF * (v + 1)]
             else:
                 first, second = do[HALF * v : HALF * (v + 1)], de[HALF * (v + 1) : HALF * (v + 2)]
-            spec[slot, j] = first + second
-
+            spec_at(i)[j] = first + second
     edges = row0[...]
     edges = jnp.concatenate([edges, pltpu.roll(edges, HALF, 1)], axis=0)[:, :HALF]
     d0 = dot3(edges, fwd[0:HALF], fwd[256 : 256 + HALF])
     flip = (iota(d0.shape, 0) & iota(d0.shape, 1) & 1) == 1
     d0 = jnp.where(flip, -d0, d0)
-    for i in range(6):
+    for i in range(count):
         for h in range(2):
-            first = 96 * h + 16 * i
-            spec0[slots[i], h] = d0[first : first + QCOLS] + d0[first + 1 : first + QCOLS + 1]
+            first = 16 * count * h + 16 * i
+            edge_at(i)[h] = d0[first : first + QCOLS] + d0[first + 1 : first + QCOLS + 1]
+
+
+def early_kernel(
+    tile_count, eq, keep, sib, near, far, rows2, fwd, spec, edge, energy, x_ref, row0
+):
+    centers = [eq[0], eq[1], keep[0], sib[0]]
+    for i, center in enumerate(centers):
+        place(x_ref, i, center, near[i], far[i], tile_count)
+    transform(
+        x_ref, row0, 4, rows2, fwd,
+        lambda i: spec.at[i], lambda i: edge.at[i], lambda i: energy.at[i],
+    )
+
+
+def correlate_kernel(
+    tile_count,
+    spec_in, edge_in, energy_in, keep, sib, across, near, far, valid, off,
+    rows2, fwd, inv2, back2,
+    out,
+    x_ref, spec, spec0, row0, energy, u_ref, part, peak, off_s, sems,
+):
+    q = lax.axis_index("sec")
+    slots = [0, 1, q + 2, (q ^ 1) + 2, (q ^ 2) + 2, (q ^ 3) + 2]
+    copies = [
+        pltpu.make_async_copy(spec_in.at[i], spec.at[slots[i]], sems.at[i]) for i in range(4)
+    ]
+    for copy in copies:
+        copy.start()
+    for i in range(4):
+        spec0[slots[i]] = edge_in[i]
+        energy[slots[i]] = energy_in[i]
+    for i, center in enumerate((keep.at[0], sib.at[0], across.at[0], across.at[1])):
+        offset = jnp.max(center[:16, MSG - HALF :].astype(f32))
+        off_s[slots[2 + i] - 2] = offset.astype(jnp.int32)
+    for i in range(2):
+        place(x_ref, i, across[i], near[i], far[i], tile_count)
+    transform(
+        x_ref, row0, 2, rows2, fwd,
+        lambda i: spec.at[slots[4 + i]],
+        lambda i: spec0.at[slots[4 + i]],
+        lambda i: energy.at[slots[4 + i]],
+    )
+
     products = []
     prior = []
     for s in range(SECTIONS):
@@ -175,6 +221,8 @@
             gr, gi = g[:, :PATCH], g[:, PATCH:]
             products.append(jnp.concatenate([fr * gr + fi * gi, fi * gr - fr * gi], axis=1))
     u0 = dot3(jnp.concatenate(products, axis=0), inv2[0:256, 0:PATCH], inv2[256:512, 0:PATCH])
+    for copy in copies:
+        copy.wait()
 
     lane1 = iota((1, LANES), 1)
     shift_lane = jnp.where(lane1 < HALF, lane1, lane1 - PATCH).astype(f32)
@@ -184,6 +232,10 @@
         prev = prior[s]
         scale8 = score_scale / jnp.sqrt(energy[s + 2] * energy[prev] + 1e-6)
         scales.append(scale8)
+        first = 2 * QCOLS * s
+        edge_rows = jnp.concatenate(
+            [u0[first : first + QCOLS], u0[first + QCOLS : first + 2 * QCOLS]], axis=1
+        )
         highs, lows = [], []
         for j in range(QCOLS):
             f, g = spec[s + 2, j], spec[prev, j]
@@ -196,9 +248,7 @@
         u = dot(ph, inv2[0:256]) + dot(plo, inv2[0:256]) + dot(ph, inv2[256:512])
         for j in range(QCOLS):
             u_ref[s, j] = u[HALF * j : HALF * (j + 1)]
-            first = 2 * QCOLS * s + j
-            u_ref[s, j, 0:1, :PATCH] = u0[first : first + 1]
-            u_ref[s, j, 0:1, PATCH:] = u0[first + QCOLS : first + QCOLS + 1]
+            u_ref[s, j, 0:1, :] = edge_rows[j : j + 1]
         for j in range(0, QCOLS, 2):
             sides = []
             for k in (j, j + 1):
@@ -355,62 +405,74 @@
     swap = functools.partial(lax.ppermute, axis_name=("sec", "tile"))
     swap_even = functools.partial(swap, perm=joint_route(tile_count, False))
     swap_odd = functools.partial(swap, perm=joint_route(tile_count, True))
-    right = 2 * QPIX * (SECTIONS // 2 - 1) + HALF_MSG - RIM - COLS * HALF
-    offset = offsets.astype(bf16)[0]
-    wide = jnp.pad(sections[0], ((0, 0), (RIM, right)))
-    half_lane = lax.broadcasted_iota(jnp.int32, (HALF, HALF_MSG), 1)
-
-    def half(h):
-        cut = lax.dynamic_slice_in_dim(wide, 2 * QPIX * h, HALF_MSG, axis=1)
-        return jnp.where(half_lane >= HALF_MSG - HALF, offset, cut)
-
-    own = half(q // 2)
-    across = lax.ppermute(half(1 - q // 2), "sec", xor_route(SECTIONS, 2))
-
-    def quarter(strip, c):
-        cut = lax.dynamic_slice_in_dim(strip, QPIX * c, MSG - HALF, axis=1)
-        return jnp.concatenate([cut, strip[:, HALF_MSG - HALF :]], axis=1)
-
-    def quarters(c):
-        return jnp.stack([quarter(own, c), quarter(across, c)])
-
-    core = q % 2
-    mine = quarters(core)
-    sib = lax.ppermute(quarters(1 - core), "sec", xor_route(SECTIONS, 1))
+    vmem = pl.BlockSpec(memory_space=pltpu.VMEM)
+    smem = pl.BlockSpec(memory_space=pltpu.SMEM)
+    quarters = jax.ShapeDtypeStruct((2, HALF, MSG), bf16)
+    keep, send = pl.pallas_call(
+        prepare_kernel,
+        out_shape=(quarters, quarters),
+        in_specs=[vmem, smem],
+        out_specs=(vmem, vmem),
+        scratch_shapes=[pltpu.VMEM((HALF, 2 * LANES + COLS * HALF), bf16)],
+        compiler_params=pltpu.CompilerParams(vmem_limit_bytes=8 * 1024 * 1024),
+        name="prepare",
+    )(sections, offsets)
+    sib = lax.ppermute(send, "sec", xor_route(SECTIONS, 1))
+    across = lax.ppermute(jnp.stack([keep[1], sib[1]]), "sec", xor_route(SECTIONS, 2))
+    right = QPIX * (SECTIONS - 1) + MSG - RIM - COLS * HALF
     eq = lax.dynamic_slice_in_dim(
         jnp.pad(earlier, ((0, 0), (0, 0), (RIM, right))), QPIX * q, MSG, axis=2
     )
     to_even = jnp.where(even, RIM, 0)
     to_odd = jnp.where(even, 0, RIM)
 
-    def rows(start):
+    def rows(images, start):
         return jnp.concatenate(
-            [lax.dynamic_slice_in_dim(x, start, RIM, axis=1) for x in (eq, mine, sib)], axis=0
+            [lax.dynamic_slice_in_dim(x, start, RIM, axis=1) for x in images], axis=0
         )
 
-    far = swap_odd(rows(to_odd))
-    near = swap_even(rows(to_even))
-    vmem = pl.BlockSpec(memory_space=pltpu.VMEM)
-    consts = [jnp.asarray(x) for x in tables()]
+    local = (eq, keep[:1], sib[:1])
+    far_local = swap_odd(rows(local, to_odd))
+    near_local = swap_even(rows(local, to_even))
+    far_across = swap_odd(rows((across,), to_odd))
+    near_across = swap_even(rows((across,), to_even))
+    rows2, fwd, inv2, back2 = [jnp.asarray(x) for x in tables()]
+    spec, edge, energy = pl.pallas_call(
+        functools.partial(early_kernel, tile_count),
+        out_shape=(
+            jax.ShapeDtypeStruct((4, QCOLS, HALF, 256), f32),
+            jax.ShapeDtypeStruct((4, 2, QCOLS, 256), f32),
+            jax.ShapeDtypeStruct((4, QCOLS, LANES), f32),
+        ),
+        in_specs=[vmem] * 7,
+        out_specs=(vmem,) * 3,
+        scratch_shapes=[pltpu.VMEM((4, PATCH, MSG), bf16), pltpu.VMEM((64, LANES), f32)],
+        compiler_params=pltpu.CompilerParams(vmem_limit_bytes=24 * 1024 * 1024),
+        name="early",
+    )(eq, keep, sib, near_local, far_local, rows2, fwd)
     cells = pl.pallas_call(
         functools.partial(correlate_kernel, tile_count),
         out_shape=jax.ShapeDtypeStruct((FEATS, LANES), f32),
-        in_specs=[vmem] * 11,
+        in_specs=[pl.BlockSpec(memory_space=pl.ANY)] + [vmem] * 13,
         out_specs=vmem,
         scratch_shapes=[
-            pltpu.VMEM((6, PATCH, MSG), bf16),
+            pltpu.VMEM((2, PATCH, MSG), bf16),
             pltpu.VMEM((6, QCOLS, HALF, 256), f32),
             pltpu.VMEM((6, 2, QCOLS, 256), f32),
-            pltpu.VMEM((96, LANES), f32),
+            pltpu.VMEM((32, LANES), f32),
             pltpu.VMEM((6, QCOLS, LANES), f32),
             pltpu.VMEM((SECTIONS, QCOLS, HALF, 256), f32),
             pltpu.VMEM((QCOLS, FEATS, LANES), f32),
             pltpu.VMEM((QCOLS, SECTIONS, LANES), f32),
             pltpu.SMEM((SECTIONS,), jnp.int32),
+            pltpu.SemaphoreType.DMA((4,)),
         ],
-        compiler_params=pltpu.CompilerParams(vmem_limit_bytes=48 * 1024 * 1024),
+        compiler_params=pltpu.CompilerParams(vmem_limit_bytes=32 * 1024 * 1024),
         name="correlate",
-    )(mine, sib, eq, near, far, patch_valid, offsets.astype(f32)[None], *consts)
+    )(
+        spec, edge, energy, keep, sib, across, near_across, far_across,
+        patch_valid, offsets.astype(f32)[None], rows2, fwd, inv2, back2,
+    )
     cells = cells + lax.ppermute(cells, "sec", xor_route(SECTIONS, 1))
     cells = cells + swap(cells, perm=gather_route(tile_count, "z"))
     near = swap(cells, perm=gather_route(tile_count, "even"))

time: 59.6 us -> 56.3 us (0.945)
  waiting for transfers between devices: 33.6 us -> 23 us
  starting transfers between devices: 14 us -> 20.8 us
  other arithmetic: 1.72 us -> 0.09 us
  local copies, waits for them, and re-layouts: 1.04 us -> 2.3 us
  Pallas kernels: 7.06 us -> 7.84 us
    ppermute x4 -> x6, waiting for transfers between devices: 16.9 us -> 6.34 us  [the longest x1 3.91 us: per_device(): far_local = swap_odd(rows(local, to_odd))]
    ppermute x4 -> x6, starting transfers between devices: 9.63 us -> 17 us  [the longest x1 6.38 us: per_device(): lax.ppermute(jnp.stack([keep[1], sib[1]]), 'sec', xor_route(SECTIONS, 2))]
    pallas_call x0 -> x2, Pallas kernels: none -> 2.14 us  [the longest x1 1.95 us: per_device(): pl.pallas_call(functools.partial(early_kernel, tile_count), out_shape=(ja...]
    pallas_call x1, Pallas kernels: 6.17 us -> 4.81 us  [per_device(): pl.pallas_call(functools.partial(correlate_kernel, tile_count), out_shape...]
    dynamic_slice x1 -> x3, local copies, waits for them, and re-layouts: 0.02 us -> 1.17 us  [rows(): lax.dynamic_slice_in_dim(x, start, RIM, axis=1)]
    select_n x1 -> x0, other arithmetic: 1.15 us -> none  [half(): return jnp.where(half_lane >= HALF_MSG - HALF, offset, cut)]
  transfers between devices with their start and end apart: 10 -> 12, of which waited for: 9 -> 9; matrix products, arithmetic and copies ran while one was open for 1% -> 2% of each run, Pallas kernels for 0% -> 3%
where the time goes in v3:
time: 56.3 us; the launch traced here: 55.7 us
  waiting for transfers between devices  23 us (41%)
  starting transfers between devices  20.8 us (37%)
  Pallas kernels  7.84 us (14%)
  local copies, waits for them, and re-layouts  2.3 us (4%)
  between operations  1.55 us (3%)
    ppermute x1, starting transfers between devices, per_device(): lax.ppermute(jnp.stack([keep[1], sib[1]]), 'sec', xor_route(SECTIONS, 2))  6.38 us
    ppermute x1, starting transfers between devices, per_device(): far_local = swap_odd(rows(local, to_odd))  5.74 us
    pallas_call x1, Pallas kernels, per_device(): pl.pallas_call(functools.partial(correlate_kernel, tile_count), out_shape...  4.81 us
    ppermute x1, waiting for transfers between devices, per_device(): far_local = swap_odd(rows(local, to_odd))  3.91 us
    ppermute x1, waiting for transfers between devices, per_device(): far = swap(jnp.stack([cells, near]), perm=gather_route(tile_count, 'odd'))  3.74 us
    ppermute x1, starting transfers between devices, per_device(): shared = lax.ppermute(bundle, 'sec', xor_route(SECTIONS, 1))  3.69 us
    ppermute x1, waiting for transfers between devices, per_device(): cells = cells + swap(cells, perm=gather_route(tile_count, 'z'))  3.65 us
    ppermute x1, waiting for transfers between devices, per_device(): third = swap(far[0], perm=gather_route(tile_count, 'even'))  3.65 us
  transfers between devices with their start and end apart: 12, of which 9 were waited for; matrix products, arithmetic and copies ran while one was open for 2% of the time, Pallas kernels for 3%

profile of v3, /device:TPU:32, one launch (start us, length us, event | category | flops | bytes accessed | tf_op | source)
XLA Modules:
  0.0 55.7 jit_solution(18395491119754158576)
XLA Ops:
  0.6 0.0 copy-start.1
  0.6 0.0 copy-start
  1.4 0.0 copy-start.3
  1.4 0.9 %copy-done.3 = bf16[1,64,2048]{2,1,0:T(8,128)(2,1)S(1)} copy-done((bf16[1,64,2048]{2,1,0:T(8,128)(2,1)S(1)}, bf16[1,64,2048]{2,1,0:T(8,128)(2,1)}, u32[]{:S(2)}) %copy-start.3) | copy-done | bytes 262168
  2.3 0.0 copy-start.6
  2.3 0.2 prepare.1
  2.5 0.1 collective-permute-start
  2.7 1.1 %pad_dynamic-slice_fusion = (bf16[2,32,640]{2,1,0:T(8,128)(2,1)S(1)}, bf16[2,32,640]{2,1,0:T(8,128)(2,1)S(1)}) fusion(s32[]{:T(128)S(6)} %select_n.37, s32[]{:T(128)S(6)} %select_n.35, bf16[2,64,2048]{2,1,0:T(8,128)(2,1)} %param.9, s32[]{:T(128)S(6)} %select_n.34), kind=kLoop, calls=%fused_computation | loop fusion | bytes 688140 | tf_op jit(solution)/shard_map/dynamic_slice | solution.py:431
  3.8 0.0 copy-start.2
  3.8 0.0 copy-start.4
  3.8 0.0 copy-start.5
  3.8 0.2 collective-permute-done.sib
  4.0 6.4 %collective-permute-start.3 = (bf16[2,64,640]{2,1,0:T(8,128)(2,1)S(1)}, bf16[2,64,640]{2,1,0:T(8,128)(2,1)S(1)}, u32[]{:S(2)}, u32[]{:S(2)}) collective-permute-start(bf16[2,64,640]{2,1,0:T(8,128)(2,1)S(1)} %pad_maximum_fusion.2), channel_id=1, source_target_pairs={{0,128},{64,192},{128,0},{192,64},{1,129},{65,193},{129,1},{193,65... | collective-permute-start | bytes 491528 | tf_op jit(solution)/shard_map/ppermute | solution.py:421
  10.5 5.7 %collective-permute-start.2 = (bf16[4,32,640]{2,1,0:T(8,128)(2,1)S(1)}, bf16[4,32,640]{2,1,0:T(8,128)(2,1)S(1)}, u32[]{:S(2)}, u32[]{:S(2)}) collective-permute-start(bf16[4,32,640]{2,1,0:T(8,128)(2,1)S(1)} %pad_maximum_fusion.1), channel_id=1, source_target_pairs={{0,64},{1,2},{2,1},{3,4},{4,3},{5,6},{6,5},{7,8},{8,7},{9,10},{10,... | collective-permute-start | bytes 491528 | tf_op jit(solution)/shard_map/ppermute | solution.py:435
  16.2 0.1 collective-permute-start.1
  16.3 2.3 %collective-permute-done.3.across = bf16[2,64,640]{2,1,0:T(8,128)(2,1)S(1)} collective-permute-done((bf16[2,64,640]{2,1,0:T(8,128)(2,1)S(1)}, bf16[2,64,640]{2,1,0:T(8,128)(2,1)S(1)}, u32[]{:S(2)}, u32[]{:S(2)}) %collective-permute-start.3) | collective-permute-done | bytes 163872 | tf_op jit(solution)/shard_map/ppermute | solution.py:421
  18.6 1.4 %collective-permute-start.4 = (bf16[2,32,640]{2,1,0:T(8,128)(2,1)S(1)}, bf16[2,32,640]{2,1,0:T(8,128)(2,1)S(1)}, u32[]{:S(2)}, u32[]{:S(2)}) collective-permute-start(bf16[2,32,640]{2,1,0:T(8,128)(2,1)S(1)} %get-tuple-element.16), channel_id=1, source_target_pairs={{0,1},{1,0},{2,3},{3,2},{4,5},{5,4},{6,7},{7,6},{8,9},{9,8},{10,11... | collective-permute-start | bytes 245768 | tf_op jit(solution)/shard_map/ppermute | solution.py:438
  20.0 3.4 %collective-permute-start.5 = (bf16[2,32,640]{2,1,0:T(8,128)(2,1)S(1)}, bf16[2,32,640]{2,1,0:T(8,128)(2,1)S(1)}, u32[]{:S(2)}, u32[]{:S(2)}) collective-permute-start(bf16[2,32,640]{2,1,0:T(8,128)(2,1)S(1)} %get-tuple-element.15), channel_id=1, source_target_pairs={{0,64},{1,2},{2,1},{3,4},{4,3},{5,6},{6,5},{7,8},{8,7},{9,10},{10,... | collective-permute-start | bytes 245768 | tf_op jit(solution)/shard_map/ppermute | solution.py:437
  23.4 0.0 copy-done.6
  23.4 0.1 pad_dynamic-slice_fusion.2.eq
  23.5 3.9 %collective-permute-done.2.far = bf16[4,32,640]{2,1,0:T(8,128)(2,1)S(1)} collective-permute-done((bf16[4,32,640]{2,1,0:T(8,128)(2,1)S(1)}, bf16[4,32,640]{2,1,0:T(8,128)(2,1)S(1)}, u32[]{:S(2)}, u32[]{:S(2)}) %collective-permute-start.2) | collective-permute-done | bytes 163872 | tf_op jit(solution)/shard_map/ppermute | solution.py:435
  27.4 0.0 collective-permute-done.1.near
  27.4 0.0 copy-done.1
  27.4 0.0 copy-done
  27.4 1.9 %early.1 = (f32[4,8,64,256]{3,2,1,0:T(8,128)S(1)}, f32[4,2,8,256]{3,2,1,0:T(8,128)S(1)}, f32[4,8,128]{2,1,0:T(8,128)S(1)}) custom-call(bf16[2,64,640]{2,1,0:T(8,128)(2,1)S(1)} %pad_dynamic-slice_fusion.2.eq, bf16[2,64,640]{2,1,0:T(8,128)(2,1)S(1)} %get-tuple-element.8.keep, bf16[2,64,640]{2,1,0:T(8,128)(2,1)S(1)} %collective-permute-done.sib, ...), custom_call_target="tpu_custom_call" | custom-call | tf_op jit(solution)/shard_map/early/pallas_call | solution.py:440
  29.4 0.0 collective-permute-done.4.near
  29.4 0.0 collective-permute-done.5.far
  29.4 0.0 copy-done.2
  29.4 0.0 copy-done.4
  29.4 0.0 copy-done.5
  29.4 4.8 %correlate.1 = f32[16,128]{1,0:T(8,128)S(1)} custom-call(f32[4,8,64,256]{3,2,1,0:T(8,128)S(1)} %get-tuple-element.10.spec_in, f32[4,2,8,256]{3,2,1,0:T(8,128)S(1)} %get-tuple-element.11.edge_in, f32[4,8,128]{2,1,0:T(8,128)S(1)} %get-tuple-element.12.energy_in, bf16[2,64,640]{2,1,0:T(8,128)(2,1)S(1)} %get-tuple-element.8.keep, ...), custom_call_target="tpu_custom_call" | custom-call | tf_op jit(solution)/shard_map/correlate/pallas_call | solution.py:453
  34.2 0.1 collective-permute-start.6
  34.3 1.2 %collective-permute-done.6 = f32[16,128]{1,0:T(8,128)S(1)} collective-permute-done((f32[16,128]{1,0:T(8,128)S(1)}, f32[16,128]{1,0:T(8,128)S(1)}, u32[]{:S(2)}, u32[]{:S(2)}) %collective-permute-start.6) | collective-permute-done | bytes 8224 | tf_op jit(solution)/shard_map/ppermute | solution.py:476
  35.5 0.0 collective-permute-start.7
  35.5 3.6 %collective-permute-done.7 = f32[16,128]{1,0:T(8,128)S(1)} collective-permute-done((f32[16,128]{1,0:T(8,128)S(1)}, f32[16,128]{1,0:T(8,128)S(1)}, u32[]{:S(2)}, u32[]{:S(2)}) %collective-permute-start.7) | collective-permute-done | bytes 8224 | tf_op jit(solution)/shard_map/ppermute | solution.py:477
  39.2 0.0 collective-permute-start.8
  39.2 3.6 %collective-permute-done.8 = f32[16,128]{1,0:T(8,128)S(1)} collective-permute-done((f32[16,128]{1,0:T(8,128)S(1)}, f32[16,128]{1,0:T(8,128)S(1)}, u32[]{:S(2)}, u32[]{:S(2)}) %collective-permute-start.8) | collective-permute-done | bytes 8224 | tf_op jit(solution)/shard_map/ppermute | solution.py:478
  42.8 0.0 collective-permute-start.9
  42.8 3.7 %collective-permute-done.9 = f32[2,16,128]{2,1,0:T(8,128)S(1)} collective-permute-done((f32[2,16,128]{2,1,0:T(8,128)S(1)}, f32[2,16,128]{2,1,0:T(8,128)S(1)}, u32[]{:S(2)}, u32[]{:S(2)}) %collective-permute-start.9) | collective-permute-done | bytes 16416 | tf_op jit(solution)/shard_map/ppermute | solution.py:479
  46.6 0.0 collective-permute-start.10
  46.6 3.6 %collective-permute-done.10 = f32[16,128]{1,0:T(8,128)S(1)} collective-permute-done((f32[16,128]{1,0:T(8,128)S(1)}, f32[16,128]{1,0:T(8,128)S(1)}, u32[]{:S(2)}, u32[]{:S(2)}) %collective-permute-start.10) | collective-permute-done | bytes 8224 | tf_op jit(solution)/shard_map/ppermute | solution.py:480
  50.2 3.7 %collective-permute-start.11 = (f32[5,16,128]{2,1,0:T(8,128)S(1)}, f32[5,16,128]{2,1,0:T(8,128)S(1)}, u32[]{:S(2)}, u32[]{:S(2)}) collective-permute-start(f32[5,16,128]{2,1,0:T(8,128)S(1)} %pad_maximum_fusion.3.mine), channel_id=1, source_target_pairs={{0,64},{64,0},{128,192},{192,128},{1,65},{65,1},{129,193},{193,129... | collective-permute-start | bytes 122888 | tf_op jit(solution)/shard_map/ppermute | solution.py:482
  53.9 0.9 %collective-permute-done.11.sib = f32[5,16,128]{2,1,0:T(8,128)S(1)} collective-permute-done((f32[5,16,128]{2,1,0:T(8,128)S(1)}, f32[5,16,128]{2,1,0:T(8,128)S(1)}, u32[]{:S(2)}, u32[]{:S(2)}) %collective-permute-start.11) | collective-permute-done | bytes 40992 | tf_op jit(solution)/shard_map/ppermute | solution.py:482
  54.8 0.9 %relax.1 = (f32[1,2,1,32]{3,2,1,0:T(1,128)}, f32[1,1,32]{2,1,0:T(1,128)}, f32[1,2,1,32]{3,2,1,0:T(1,128)}) custom-call(f32[5,16,128]{2,1,0:T(8,128)S(1)} %pad_maximum_fusion.3.mine, f32[5,16,128]{2,1,0:T(8,128)S(1)} %collective-permute-done.11.sib), custom_call_target="tpu_custom_call" | custom-call | tf_op jit(solution)/shard_map/relax/pallas_call | solution.py:483
  (12 shorter events, 0.2 us)
Async XLA Ops:
  0.6 26.8 %copy-start.1 = (bf16[256,128]{1,0:T(8,128)(2,1)S(1)}, bf16[256,128]{1,0:T(8,128)(2,1)}, u32[]{:S(2)}) copy-start(bf16[256,128]{1,0:T(8,128)(2,1)} %constant.73.clone.rows2) | copy-start | bytes 196612
  0.6 26.8 %copy-start = (bf16[768,256]{1,0:T(8,128)(2,1)S(1)}, bf16[768,256]{1,0:T(8,128)(2,1)}, u32[]{:S(2)}) copy-start(bf16[768,256]{1,0:T(8,128)(2,1)} %constant.74.clone.fwd) | copy-start | bytes 1179652
  1.4 1.0 %copy-start.3 = (bf16[1,64,2048]{2,1,0:T(8,128)(2,1)S(1)}, bf16[1,64,2048]{2,1,0:T(8,128)(2,1)}, u32[]{:S(2)}) copy-start(bf16[1,64,2048]{2,1,0:T(8,128)(2,1)} %strip.1) | copy-start | bytes 786436
  2.3 21.1 %copy-start.6 = (bf16[2,64,2048]{2,1,0:T(8,128)(2,1)S(1)}, bf16[2,64,2048]{2,1,0:T(8,128)(2,1)}, u32[]{:S(2)}) copy-start(bf16[2,64,2048]{2,1,0:T(8,128)(2,1)} %param.9) | copy-start | bytes 1572868
  2.5 1.5 %collective-permute-start = (bf16[2,64,640]{2,1,0:T(8,128)(2,1)S(1)}, bf16[2,64,640]{2,1,0:T(8,128)(2,1)S(1)}, u32[]{:S(2)}, u32[]{:S(2)}) collective-permute-start(bf16[2,64,640]{2,1,0:T(8,128)(2,1)S(1)} %get-tuple-element.9), channel_id=1, source_target_pairs={{0,64},{64,0},{128,192},{192,128},{1,65},{65,1},{129,193},{193,129... | collective-permute-start | bytes 491528 | tf_op jit(solution)/shard_map/ppermute | solution.py:420
  3.8 25.6 %copy-start.2 = (bf16[512,256]{1,0:T(8,128)(2,1)S(1)}, bf16[512,256]{1,0:T(8,128)(2,1)}, u32[]{:S(2)}) copy-start(bf16[512,256]{1,0:T(8,128)(2,1)} %constant.75.clone.inv2) | copy-start | bytes 786436
  3.8 25.6 %copy-start.4 = (bf16[256,256]{1,0:T(8,128)(2,1)S(1)}, bf16[256,256]{1,0:T(8,128)(2,1)}, u32[]{:S(2)}) copy-start(bf16[256,256]{1,0:T(8,128)(2,1)} %constant.76.clone.back2) | copy-start | bytes 393220
  3.8 25.6 %copy-start.5 = (s32[1,1,32]{2,1,0:T(1,128)S(1)}, s32[1,1,32]{2,1,0:T(1,128)}, u32[]{:S(2)}) copy-start(s32[1,1,32]{2,1,0:T(1,128)} %valid.1) | copy-start | bytes 388
  4.0 14.6 %collective-permute-start.3 = (bf16[2,64,640]{2,1,0:T(8,128)(2,1)S(1)}, bf16[2,64,640]{2,1,0:T(8,128)(2,1)S(1)}, u32[]{:S(2)}, u32[]{:S(2)}) collective-permute-start(bf16[2,64,640]{2,1,0:T(8,128)(2,1)S(1)} %pad_maximum_fusion.2), channel_id=1, source_target_pairs={{0,128},{64,192},{128,0},{192,64},{1,129},{65,193},{129,1},{193,65... | collective-permute-start | bytes 491528 | tf_op jit(solution)/shard_map/ppermute | solution.py:421
  10.5 16.9 %collective-permute-start.2 = (bf16[4,32,640]{2,1,0:T(8,128)(2,1)S(1)}, bf16[4,32,640]{2,1,0:T(8,128)(2,1)S(1)}, u32[]{:S(2)}, u32[]{:S(2)}) collective-permute-start(bf16[4,32,640]{2,1,0:T(8,128)(2,1)S(1)} %pad_maximum_fusion.1), channel_id=1, source_target_pairs={{0,64},{1,2},{2,1},{3,4},{4,3},{5,6},{6,5},{7,8},{8,7},{9,10},{10,... | collective-permute-start | bytes 491528 | tf_op jit(solution)/shard_map/ppermute | solution.py:435
  16.2 11.2 %collective-permute-start.1 = (bf16[4,32,640]{2,1,0:T(8,128)(2,1)S(1)}, bf16[4,32,640]{2,1,0:T(8,128)(2,1)S(1)}, u32[]{:S(2)}, u32[]{:S(2)}) collective-permute-start(bf16[4,32,640]{2,1,0:T(8,128)(2,1)S(1)} %pad_maximum_fusion), channel_id=1, source_target_pairs={{0,1},{1,0},{2,3},{3,2},{4,5},{5,4},{6,7},{7,6},{8,9},{9,8},{10,11... | collective-permute-start | bytes 491528 | tf_op jit(solution)/shard_map/ppermute | solution.py:436
  18.6 10.7 %collective-permute-start.4 = (bf16[2,32,640]{2,1,0:T(8,128)(2,1)S(1)}, bf16[2,32,640]{2,1,0:T(8,128)(2,1)S(1)}, u32[]{:S(2)}, u32[]{:S(2)}) collective-permute-start(bf16[2,32,640]{2,1,0:T(8,128)(2,1)S(1)} %get-tuple-element.16), channel_id=1, source_target_pairs={{0,1},{1,0},{2,3},{3,2},{4,5},{5,4},{6,7},{7,6},{8,9},{9,8},{10,11... | collective-permute-start | bytes 245768 | tf_op jit(solution)/shard_map/ppermute | solution.py:438
  20.0 9.4 %collective-permute-start.5 = (bf16[2,32,640]{2,1,0:T(8,128)(2,1)S(1)}, bf16[2,32,640]{2,1,0:T(8,128)(2,1)S(1)}, u32[]{:S(2)}, u32[]{:S(2)}) collective-permute-start(bf16[2,32,640]{2,1,0:T(8,128)(2,1)S(1)} %get-tuple-element.15), channel_id=1, source_target_pairs={{0,64},{1,2},{2,1},{3,4},{4,3},{5,6},{6,5},{7,8},{8,7},{9,10},{10,... | collective-permute-start | bytes 245768 | tf_op jit(solution)/shard_map/ppermute | solution.py:437
  34.2 1.3 %collective-permute-start.6 = (f32[16,128]{1,0:T(8,128)S(1)}, f32[16,128]{1,0:T(8,128)S(1)}, u32[]{:S(2)}, u32[]{:S(2)}) collective-permute-start(f32[16,128]{1,0:T(8,128)S(1)} %correlate.1), channel_id=1, source_target_pairs={{0,64},{64,0},{128,192},{192,128},{1,65},{65,1},{129,193},{193,129... | collective-permute-start | bytes 24584 | tf_op jit(solution)/shard_map/ppermute | solution.py:476
  35.5 3.7 %collective-permute-start.7 = (f32[16,128]{1,0:T(8,128)S(1)}, f32[16,128]{1,0:T(8,128)S(1)}, u32[]{:S(2)}, u32[]{:S(2)}) collective-permute-start(f32[16,128]{1,0:T(8,128)S(1)} %add.31), channel_id=1, source_target_pairs={{0,1},{1,0},{2,3},{3,2},{4,5},{5,4},{6,7},{7,6},{8,9},{9,8},{10,11... | collective-permute-start | bytes 24584 | tf_op jit(solution)/shard_map/ppermute | solution.py:477
  39.2 3.7 %collective-permute-start.8 = (f32[16,128]{1,0:T(8,128)S(1)}, f32[16,128]{1,0:T(8,128)S(1)}, u32[]{:S(2)}, u32[]{:S(2)}) collective-permute-start(f32[16,128]{1,0:T(8,128)S(1)} %add.32), channel_id=1, source_target_pairs={{0,1},{1,0},{2,3},{3,2},{4,5},{5,4},{6,7},{7,6},{8,9},{9,8},{10,11... | collective-permute-start | bytes 24584 | tf_op jit(solution)/shard_map/ppermute | solution.py:478
  42.8 3.7 %collective-permute-start.9 = (f32[2,16,128]{2,1,0:T(8,128)S(1)}, f32[2,16,128]{2,1,0:T(8,128)S(1)}, u32[]{:S(2)}, u32[]{:S(2)}) collective-permute-start(f32[2,16,128]{2,1,0:T(8,128)S(1)} %pad_maximum_fusion.4), channel_id=1, source_target_pairs={{0,1},{1,0},{2,3},{3,2},{4,5},{5,4},{6,7},{7,6},{8,9},{9,8},{10,11... | collective-permute-start | bytes 49160 | tf_op jit(solution)/shard_map/ppermute | solution.py:479
  46.6 3.7 %collective-permute-start.10 = (f32[16,128]{1,0:T(8,128)S(1)}, f32[16,128]{1,0:T(8,128)S(1)}, u32[]{:S(2)}, u32[]{:S(2)}) collective-permute-start(f32[16,128]{1,0:T(8,128)S(1)} %slice_bitcast_fusion), channel_id=1, source_target_pairs={{0,1},{1,0},{2,3},{3,2},{4,5},{5,4},{6,7},{7,6},{8,9},{9,8},{10,11... | collective-permute-start | bytes 24584 | tf_op jit(solution)/shard_map/ppermute | solution.py:480
  50.2 4.6 %collective-permute-start.11 = (f32[5,16,128]{2,1,0:T(8,128)S(1)}, f32[5,16,128]{2,1,0:T(8,128)S(1)}, u32[]{:S(2)}, u32[]{:S(2)}) collective-permute-start(f32[5,16,128]{2,1,0:T(8,128)S(1)} %pad_maximum_fusion.3.mine), channel_id=1, source_target_pairs={{0,64},{64,0},{128,192},{192,128},{1,65},{65,1},{129,193},{193,129... | collective-permute-start | bytes 122888 | tf_op jit(solution)/shard_map/ppermute | solution.py:482

commit v4 on v3

--- a/solution.py
+++ b/solution.py
@@ -1,4 +1,5 @@
 import functools
+import math
 
 import jax
 import jax.numpy as jnp
@@ -44,7 +45,7 @@
     alt = (-1.0) ** n
     rows = np.concatenate([c[:HALF], alt[None], s[1:HALF]], axis=0)
     rows_hi, rows_lo = split_table(rows)
-    rows2 = np.concatenate([rows_hi, rows_lo], axis=0)
+    rows2 = np.concatenate([rows_hi, rows_lo], axis=1)
     cols_cos = np.concatenate([c[:HALF], -s[:HALF]], axis=1)
     cols_sin = np.concatenate([-s[:HALF], -c[:HALF]], axis=1)
     even = np.concatenate([cols_cos, cols_sin], axis=0)
@@ -55,20 +56,18 @@
     inv = np.concatenate(
         [np.concatenate([c, s], axis=1), np.concatenate([-s, c], axis=1)], axis=0
     )
-    inv2 = np.concatenate(split_table(inv), axis=0)
+    inv_hi, inv_lo = split_table(inv)
+    inv3 = np.concatenate([inv_hi, inv_hi, inv_lo], axis=0)
     back = np.concatenate([2.0 * c[:, :HALF], -2.0 * s[:, :HALF]], axis=1)
     back[:, 0] = 1.0
     back[:, HALF] = alt
     back_hi, back_lo = split_table(back / (PATCH * PATCH))
-    back2 = np.concatenate(
-        [np.concatenate([back_hi, back_hi], axis=1), np.concatenate([back_lo, back_lo], axis=1)],
-        axis=0,
-    )
+    back3 = np.concatenate([back_hi, back_hi, back_lo], axis=1)
     return (
         rows2,
         fwd,
-        inv2,
-        back2,
+        inv3,
+        back3,
     )
 
 
@@ -97,9 +96,9 @@
     wide[:, :LANES] = blank
     wide[:, LANES : LANES + COLS * HALF] = strip[0]
     wide[:, LANES + COLS * HALF :] = blank
-    offset = off[0].astype(f32)
+    offset = jnp.broadcast_to(off[...].astype(f32), (HALF, MSG))
     marked = iota((HALF, MSG), 1) >= MSG - HALF
-    for out, core in ((keep, c), (send, 1 - c)):
+    for out, core in ((send, 1 - c), (keep, c)):
         for i, side in enumerate((h, 1 - h)):
             start = pl.multiple_of(QPIX * (2 * side + core), LANES)
             cut = wide[:, pl.ds(start, MSG + LANES)].astype(f32)
@@ -133,8 +132,7 @@
         column = jnp.sum(xf * xf, axis=0, keepdims=True)
         windows = jnp.sum(jnp.where(in_window, column, 0.0), axis=1, keepdims=True)
         energy_at(i)[...] = jnp.broadcast_to(windows, (QCOLS, LANES))
-        y2 = dot(rows2[...], x)
-        y = y2[:PATCH] + y2[PATCH:]
+        y = dot(rows2[...], jnp.concatenate([x, x], axis=0))
         evens, odds = [], []
         for v in range(QCOLS // 2 + 1):
             a = y[:HALF, LANES * v : LANES * (v + 1)]
@@ -148,9 +146,9 @@
                 row0[16 * i + 2 * v + 1 : 16 * i + 2 * v + 2, :] = pltpu.roll(g[0:1], HALF, 1)
         row0[16 * i + QCOLS + 1 : 16 * i + 16, :] = jnp.zeros((7, LANES), f32)
         gh, gl = split(jnp.concatenate(evens, axis=0))
-        de = dot(jnp.concatenate([gh, gl], axis=1), fwd[0:256]) + dot(gh, fwd[256:384])
+        de = dot(jnp.concatenate([gh, gl, gh], axis=1), fwd[0:384])
         gh, gl = split(jnp.concatenate(odds, axis=0))
-        do = dot(jnp.concatenate([gh, gl], axis=1), fwd[384:640]) + dot(gh, fwd[640:768])
+        do = dot(jnp.concatenate([gh, gl, gh], axis=1), fwd[384:768])
         for j in range(QCOLS):
             v = j // 2
             if j % 2 == 0:
@@ -183,10 +181,10 @@
 
 def correlate_kernel(
     tile_count,
-    spec_in, edge_in, energy_in, keep, sib, across, near, far, valid, off,
-    rows2, fwd, inv2, back2,
+    spec_in, edge_in, energy_in, keep, sib, across, far, near, valid,
+    rows2, fwd, inv3, back3,
     out,
-    x_ref, spec, spec0, row0, energy, u_ref, part, peak, off_s, sems,
+    x_ref, spec, spec0, row0, energy, u_ref, c_ref, part, peak, off_s, sems,
 ):
     q = lax.axis_index("sec")
     slots = [0, 1, q + 2, (q ^ 1) + 2, (q ^ 2) + 2, (q ^ 3) + 2]
@@ -220,7 +218,7 @@
             fr, fi = f[:, :PATCH], f[:, PATCH:]
             gr, gi = g[:, :PATCH], g[:, PATCH:]
             products.append(jnp.concatenate([fr * gr + fi * gi, fi * gr - fr * gi], axis=1))
-    u0 = dot3(jnp.concatenate(products, axis=0), inv2[0:256, 0:PATCH], inv2[256:512, 0:PATCH])
+    u0 = dot3(jnp.concatenate(products, axis=0), inv3[0:256, 0:PATCH], inv3[512:768, 0:PATCH])
     for copy in copies:
         copy.wait()
 
@@ -228,14 +226,10 @@
     shift_lane = jnp.where(lane1 < HALF, lane1, lane1 - PATCH).astype(f32)
     sub8 = iota((8, LANES), 0).astype(f32)
     scales = []
-    for s in range(SECTIONS):
+
+    def inverse(s):
         prev = prior[s]
-        scale8 = score_scale / jnp.sqrt(energy[s + 2] * energy[prev] + 1e-6)
-        scales.append(scale8)
-        first = 2 * QCOLS * s
-        edge_rows = jnp.concatenate(
-            [u0[first : first + QCOLS], u0[first + QCOLS : first + 2 * QCOLS]], axis=1
-        )
+        scales.append(score_scale / jnp.sqrt(energy[s + 2] * energy[prev] + 1e-6))
         highs, lows = [], []
         for j in range(QCOLS):
             f, g = spec[s + 2, j], spec[prev, j]
@@ -245,53 +239,76 @@
             highs.append(ph)
             lows.append(plo)
         ph, plo = jnp.concatenate(highs, axis=0), jnp.concatenate(lows, axis=0)
-        u = dot(ph, inv2[0:256]) + dot(plo, inv2[0:256]) + dot(ph, inv2[256:512])
+        u = dot(jnp.concatenate([ph, plo, ph], axis=1), inv3[...])
+        first = 2 * QCOLS * s
+        edge_rows = jnp.concatenate(
+            [u0[first : first + QCOLS], u0[first + QCOLS : first + 2 * QCOLS]], axis=1
+        )
         for j in range(QCOLS):
             u_ref[s, j] = u[HALF * j : HALF * (j + 1)]
             u_ref[s, j, 0:1, :] = edge_rows[j : j + 1]
+
+    def shifts(s):
         for j in range(0, QCOLS, 2):
             sides = []
             for k in (j, j + 1):
                 uh, ul = split(u_ref[s, k])
+                high = [uh[:, :PATCH], uh[:, PATCH:]]
                 sides.append(
-                    jnp.concatenate([uh[:, :PATCH], uh[:, PATCH:], ul[:, :PATCH], ul[:, PATCH:]], axis=0)
+                    jnp.concatenate(high + [ul[:, :PATCH], ul[:, PATCH:]] + high, axis=0)
                 )
-            c2 = dot(back2[...], jnp.concatenate(sides, axis=1))
-            both = c2[:PATCH] + c2[PATCH:]
+            both = dot(back3[...], jnp.concatenate(sides, axis=1))
             for k in (j, j + 1):
                 c = both[:, PATCH * (k - j) : PATCH * (k - j + 1)]
-                top = jnp.max(jnp.max(c, axis=0, keepdims=True), axis=1, keepdims=True)
-                rate = scale8[k : k + 1, :]
-                w = jnp.exp((c - top) * rate)
-                total = w[0:8]
-                moment = jnp.zeros((8, LANES), f32)
-                for a in range(1, PATCH // 8):
-                    block = w[8 * a : 8 * a + 8]
-                    total = total + block
-                    moment = moment + block * float(8 * a if 8 * a < HALF else 8 * a - PATCH)
-                moment = moment + total * sub8
-                total = jnp.sum(total, axis=0, keepdims=True)
-                part[k, s : s + 1, :] = jnp.sum(moment, axis=0, keepdims=True)
-                part[k, 4 + s : 5 + s, :] = total * shift_lane
-                part[k, 8 + s : 9 + s, :] = total
-                peak[k, s : s + 1, :] = jnp.broadcast_to(top, (1, LANES))
+                c_ref[s % 2, k] = c
+                peak[s, k : k + 1, :] = jnp.max(c, axis=0, keepdims=True)
+
+    def soften(s):
+        top8 = jnp.broadcast_to(jnp.max(peak[s], axis=1, keepdims=True), (QCOLS, LANES))
+        peak[s] = top8
+        rate8 = scales[s] * math.log2(math.e)
+        for k in range(QCOLS):
+            top = top8[k : k + 1, :]
+            rate = rate8[k : k + 1, :]
+            total = jnp.zeros((8, LANES), f32)
+            moment = jnp.zeros((8, LANES), f32)
+            for a in range(15, -1, -1):
+                row = 8 * ((a + 8) % 16)
+                total = total + jnp.exp2((c_ref[s % 2, k, row : row + 8, :] - top) * rate)
+                if a:
+                    moment = moment + total
+            moment = 8.0 * moment + total * (sub8 - HALF)
+            total = jnp.sum(total, axis=0, keepdims=True)
+            part[k, s : s + 1, :] = jnp.sum(moment, axis=0, keepdims=True)
+            part[k, 4 + s : 5 + s, :] = total * shift_lane
+            part[k, 8 + s : 9 + s, :] = total
+
+    inverse(0)
+    for s in range(SECTIONS):
+        if s + 1 < SECTIONS:
+            inverse(s + 1)
+        shifts(s)
+        soften(s)
 
     lane16 = iota((FEATS, LANES), 1)
     lane4 = iota((SECTIONS, LANES), 1)
     lane8 = iota((QCOLS, LANES), 1)
     first_lane = q * QCOLS
     sums = jnp.zeros((FEATS, LANES), f32)
-    tops = jnp.zeros((SECTIONS, LANES), f32)
     for j in range(QCOLS):
         part[j, 12:16, :] = jnp.zeros((4, LANES), f32)
         sums = sums + jnp.where(
             lane16 == first_lane + j, jnp.sum(part[j], axis=1, keepdims=True), 0.0
         )
-        tops = tops + jnp.where(lane4 == first_lane + j, peak[j], 0.0)
     pick = lane8 == first_lane + iota((QCOLS, LANES), 0)
-    rates = jnp.concatenate(
-        [jnp.sum(jnp.where(pick, scale8, 0.0), axis=0, keepdims=True) for scale8 in scales], axis=0
-    )
+
+    def gathered(rows):
+        return jnp.concatenate(
+            [jnp.sum(jnp.where(pick, x, 0.0), axis=0, keepdims=True) for x in rows], axis=0
+        )
+
+    rates = gathered(scales)
+    tops = gathered([peak[s] for s in range(SECTIONS)])
     mine = jnp.logical_and(lane4 >= first_lane, lane4 < first_lane + QCOLS)
     total = jnp.where(mine, sums[8:12], 1.0)
     out[0:4, :] = sums[0:4] / total
@@ -299,7 +316,11 @@
     out[8:12, :] = jnp.where(mine, (tops * rates + jnp.log(total)) / score_scale, 0.0)
     row4 = iota((SECTIONS, LANES), 0)
     flags = jnp.concatenate(
-        [valid[0].astype(f32), jnp.broadcast_to(off[...], (1, COLS)), jnp.zeros((1, HALF), f32)],
+        [
+            valid[0].astype(f32),
+            keep[0, 0:1, MSG - COLS :].astype(f32),
+            jnp.zeros((1, HALF), f32),
+        ],
         axis=1,
     )
     out[12:16, :] = jnp.where(row4 == q, flags, 0.0)
@@ -406,17 +427,16 @@
     swap_even = functools.partial(swap, perm=joint_route(tile_count, False))
     swap_odd = functools.partial(swap, perm=joint_route(tile_count, True))
     vmem = pl.BlockSpec(memory_space=pltpu.VMEM)
-    smem = pl.BlockSpec(memory_space=pltpu.SMEM)
     quarters = jax.ShapeDtypeStruct((2, HALF, MSG), bf16)
     keep, send = pl.pallas_call(
         prepare_kernel,
         out_shape=(quarters, quarters),
-        in_specs=[vmem, smem],
+        in_specs=[vmem, vmem],
         out_specs=(vmem, vmem),
         scratch_shapes=[pltpu.VMEM((HALF, 2 * LANES + COLS * HALF), bf16)],
         compiler_params=pltpu.CompilerParams(vmem_limit_bytes=8 * 1024 * 1024),
         name="prepare",
-    )(sections, offsets)
+    )(sections, offsets[None])
     sib = lax.ppermute(send, "sec", xor_route(SECTIONS, 1))
     across = lax.ppermute(jnp.stack([keep[1], sib[1]]), "sec", xor_route(SECTIONS, 2))
     right = QPIX * (SECTIONS - 1) + MSG - RIM - COLS * HALF
@@ -436,7 +456,7 @@
     near_local = swap_even(rows(local, to_even))
     far_across = swap_odd(rows((across,), to_odd))
     near_across = swap_even(rows((across,), to_even))
-    rows2, fwd, inv2, back2 = [jnp.asarray(x) for x in tables()]
+    rows2, fwd, inv3, back3 = [jnp.asarray(x) for x in tables()]
     spec, edge, energy = pl.pallas_call(
         functools.partial(early_kernel, tile_count),
         out_shape=(
@@ -453,7 +473,7 @@
     cells = pl.pallas_call(
         functools.partial(correlate_kernel, tile_count),
         out_shape=jax.ShapeDtypeStruct((FEATS, LANES), f32),
-        in_specs=[pl.BlockSpec(memory_space=pl.ANY)] + [vmem] * 13,
+        in_specs=[pl.BlockSpec(memory_space=pl.ANY)] + [vmem] * 12,
         out_specs=vmem,
         scratch_shapes=[
             pltpu.VMEM((2, PATCH, MSG), bf16),
@@ -462,16 +482,17 @@
             pltpu.VMEM((32, LANES), f32),
             pltpu.VMEM((6, QCOLS, LANES), f32),
             pltpu.VMEM((SECTIONS, QCOLS, HALF, 256), f32),
+            pltpu.VMEM((2, QCOLS, PATCH, LANES), f32),
             pltpu.VMEM((QCOLS, FEATS, LANES), f32),
-            pltpu.VMEM((QCOLS, SECTIONS, LANES), f32),
+            pltpu.VMEM((SECTIONS, QCOLS, LANES), f32),
             pltpu.SMEM((SECTIONS,), jnp.int32),
             pltpu.SemaphoreType.DMA((4,)),
         ],
         compiler_params=pltpu.CompilerParams(vmem_limit_bytes=32 * 1024 * 1024),
         name="correlate",
     )(
-        spec, edge, energy, keep, sib, across, near_across, far_across,
-        patch_valid, offsets.astype(f32)[None], rows2, fwd, inv2, back2,
+        spec, edge, energy, keep, sib, across, far_across, near_across,
+        patch_valid, rows2, fwd, inv3, back3,
     )
     cells = cells + lax.ppermute(cells, "sec", xor_route(SECTIONS, 1))
     cells = cells + swap(cells, perm=gather_route(tile_count, "z"))

time: 56.3 us -> 54.9 us (0.975)
  Pallas kernels: 7.84 us -> 6.44 us
    ppermute x1, starting transfers between devices: 1.35 us -> 0.01 us  [per_device(): near_across = swap_even(rows((across,), to_even))]
    pallas_call x1, Pallas kernels: 4.81 us -> 3.52 us  [per_device(): pl.pallas_call(functools.partial(correlate_kernel, tile_count), out_shape...]
    ppermute x1, starting transfers between devices: 3.38 us -> 4.54 us  [per_device(): far_across = swap_odd(rows((across,), to_odd))]
  transfers between devices with their start and end apart: 12 -> 12, of which waited for: 9 -> 9; matrix products, arithmetic and copies ran while one was open for 2% -> 3% of each run, Pallas kernels for 3% -> 3%
where the time goes in v4:
time: 54.9 us; the launch traced here: 54.3 us
  waiting for transfers between devices  23.2 us (42%)
  starting transfers between devices  20.6 us (38%)
  Pallas kernels  6.44 us (12%)
  local copies, waits for them, and re-layouts  2.31 us (4%)
  between operations  1.55 us (3%)
    ppermute x1, starting transfers between devices, per_device(): lax.ppermute(jnp.stack([keep[1], sib[1]]), 'sec', xor_route(SECTIONS, 2))  6.38 us
    ppermute x1, starting transfers between devices, per_device(): far_local = swap_odd(rows(local, to_odd))  5.74 us
    ppermute x1, starting transfers between devices, per_device(): far_across = swap_odd(rows((across,), to_odd))  4.54 us
    ppermute x1, waiting for transfers between devices, per_device(): far_local = swap_odd(rows(local, to_odd))  4.01 us
    ppermute x1, waiting for transfers between devices, per_device(): far = swap(jnp.stack([cells, near]), perm=gather_route(tile_count, 'odd'))  3.74 us
    ppermute x1, starting transfers between devices, per_device(): shared = lax.ppermute(bundle, 'sec', xor_route(SECTIONS, 1))  3.69 us
    ppermute x1, waiting for transfers between devices, per_device(): cells = cells + swap(cells, perm=gather_route(tile_count, 'z'))  3.65 us
    ppermute x1, waiting for transfers between devices, per_device(): near = swap(cells, perm=gather_route(tile_count, 'even'))  3.65 us
  transfers between devices with their start and end apart: 12, of which 9 were waited for; matrix products, arithmetic and copies ran while one was open for 3% of the time, Pallas kernels for 3%

profile of v4, /device:TPU:32, one launch (start us, length us, event | category | flops | bytes accessed | tf_op | source)
XLA Modules:
  0.0 54.3 jit_solution(15719688150710877615)
XLA Ops:
  0.6 0.0 copy-start.2
  0.6 0.0 copy-start
  1.4 0.0 copy-start.3
  1.4 0.9 %copy-done.3 = bf16[1,64,2048]{2,1,0:T(8,128)(2,1)S(1)} copy-done((bf16[1,64,2048]{2,1,0:T(8,128)(2,1)S(1)}, bf16[1,64,2048]{2,1,0:T(8,128)(2,1)}, u32[]{:S(2)}) %copy-start.3) | copy-done | bytes 262168
  2.3 0.0 copy-start.6
  2.3 0.2 prepare.1
  2.5 0.1 collective-permute-start
  2.7 1.1 %pad_dynamic-slice_fusion = (bf16[2,32,640]{2,1,0:T(8,128)(2,1)S(1)}, bf16[2,32,640]{2,1,0:T(8,128)(2,1)S(1)}) fusion(s32[]{:T(128)S(6)} %select_n.37, s32[]{:T(128)S(6)} %select_n.35, bf16[2,64,2048]{2,1,0:T(8,128)(2,1)} %param.9, s32[]{:T(128)S(6)} %select_n.34), kind=kLoop, calls=%fused_computation | loop fusion | bytes 688140 | tf_op jit(solution)/shard_map/dynamic_slice | solution.py:451
  3.8 0.0 copy-start.1
  3.8 0.0 copy-start.4
  3.8 0.0 copy-start.5
  3.8 0.2 collective-permute-done.sib
  4.0 6.4 %collective-permute-start.3 = (bf16[2,64,640]{2,1,0:T(8,128)(2,1)S(1)}, bf16[2,64,640]{2,1,0:T(8,128)(2,1)S(1)}, u32[]{:S(2)}, u32[]{:S(2)}) collective-permute-start(bf16[2,64,640]{2,1,0:T(8,128)(2,1)S(1)} %pad_maximum_fusion.2), channel_id=1, source_target_pairs={{0,128},{64,192},{128,0},{192,64},{1,129},{65,193},{129,1},{193,65... | collective-permute-start | bytes 491528 | tf_op jit(solution)/shard_map/ppermute | solution.py:441
  10.5 5.7 %collective-permute-start.2 = (bf16[4,32,640]{2,1,0:T(8,128)(2,1)S(1)}, bf16[4,32,640]{2,1,0:T(8,128)(2,1)S(1)}, u32[]{:S(2)}, u32[]{:S(2)}) collective-permute-start(bf16[4,32,640]{2,1,0:T(8,128)(2,1)S(1)} %pad_maximum_fusion.1), channel_id=1, source_target_pairs={{0,64},{1,2},{2,1},{3,4},{4,3},{5,6},{6,5},{7,8},{8,7},{9,10},{10,... | collective-permute-start | bytes 491528 | tf_op jit(solution)/shard_map/ppermute | solution.py:455
  16.2 0.1 collective-permute-start.1
  16.3 2.4 %collective-permute-done.3.across = bf16[2,64,640]{2,1,0:T(8,128)(2,1)S(1)} collective-permute-done((bf16[2,64,640]{2,1,0:T(8,128)(2,1)S(1)}, bf16[2,64,640]{2,1,0:T(8,128)(2,1)S(1)}, u32[]{:S(2)}, u32[]{:S(2)}) %collective-permute-start.3) | collective-permute-done | bytes 163872 | tf_op jit(solution)/shard_map/ppermute | solution.py:441
  18.7 4.5 %collective-permute-start.4 = (bf16[2,32,640]{2,1,0:T(8,128)(2,1)S(1)}, bf16[2,32,640]{2,1,0:T(8,128)(2,1)S(1)}, u32[]{:S(2)}, u32[]{:S(2)}) collective-permute-start(bf16[2,32,640]{2,1,0:T(8,128)(2,1)S(1)} %get-tuple-element.16), channel_id=1, source_target_pairs={{0,64},{1,2},{2,1},{3,4},{4,3},{5,6},{6,5},{7,8},{8,7},{9,10},{10,... | collective-permute-start | bytes 245768 | tf_op jit(solution)/shard_map/ppermute | solution.py:457
  23.3 0.0 collective-permute-start.5
  23.3 0.0 copy-done.6
  23.3 0.1 pad_dynamic-slice_fusion.2.eq
  23.4 4.0 %collective-permute-done.2.far = bf16[4,32,640]{2,1,0:T(8,128)(2,1)S(1)} collective-permute-done((bf16[4,32,640]{2,1,0:T(8,128)(2,1)S(1)}, bf16[4,32,640]{2,1,0:T(8,128)(2,1)S(1)}, u32[]{:S(2)}, u32[]{:S(2)}) %collective-permute-start.2) | collective-permute-done | bytes 163872 | tf_op jit(solution)/shard_map/ppermute | solution.py:455
  27.4 0.0 collective-permute-done.1.near
  27.4 0.0 copy-done.2
  27.4 0.0 copy-done
  27.4 1.8 %early.1 = (f32[4,8,64,256]{3,2,1,0:T(8,128)S(1)}, f32[4,2,8,256]{3,2,1,0:T(8,128)S(1)}, f32[4,8,128]{2,1,0:T(8,128)S(1)}) custom-call(bf16[2,64,640]{2,1,0:T(8,128)(2,1)S(1)} %pad_dynamic-slice_fusion.2.eq, bf16[2,64,640]{2,1,0:T(8,128)(2,1)S(1)} %get-tuple-element.8.keep, bf16[2,64,640]{2,1,0:T(8,128)(2,1)S(1)} %collective-permute-done.sib, ...), custom_call_target="tpu_custom_call" | custom-call | tf_op jit(solution)/shard_map/early/pallas_call | solution.py:460
  29.3 0.0 collective-permute-done.4.far
  29.3 0.0 collective-permute-done.5.near
  29.3 0.0 copy-done.1
  29.3 0.0 copy-done.4
  29.3 0.0 copy-done.5
  29.3 3.5 %correlate.1 = f32[16,128]{1,0:T(8,128)S(1)} custom-call(f32[4,8,64,256]{3,2,1,0:T(8,128)S(1)} %get-tuple-element.10.spec_in, f32[4,2,8,256]{3,2,1,0:T(8,128)S(1)} %get-tuple-element.11.edge_in, f32[4,8,128]{2,1,0:T(8,128)S(1)} %get-tuple-element.12.energy_in, bf16[2,64,640]{2,1,0:T(8,128)(2,1)S(1)} %get-tuple-element.8.keep, ...), custom_call_target="tpu_custom_call" | custom-call | tf_op jit(solution)/shard_map/correlate/pallas_call | solution.py:473
  32.8 0.1 collective-permute-start.6
  32.9 1.2 %collective-permute-done.6 = f32[16,128]{1,0:T(8,128)S(1)} collective-permute-done((f32[16,128]{1,0:T(8,128)S(1)}, f32[16,128]{1,0:T(8,128)S(1)}, u32[]{:S(2)}, u32[]{:S(2)}) %collective-permute-start.6) | collective-permute-done | bytes 8224 | tf_op jit(solution)/shard_map/ppermute | solution.py:497
  34.1 0.0 collective-permute-start.7
  34.1 3.6 %collective-permute-done.7 = f32[16,128]{1,0:T(8,128)S(1)} collective-permute-done((f32[16,128]{1,0:T(8,128)S(1)}, f32[16,128]{1,0:T(8,128)S(1)}, u32[]{:S(2)}, u32[]{:S(2)}) %collective-permute-start.7) | collective-permute-done | bytes 8224 | tf_op jit(solution)/shard_map/ppermute | solution.py:498
  37.8 0.0 collective-permute-start.8
  37.8 3.6 %collective-permute-done.8 = f32[16,128]{1,0:T(8,128)S(1)} collective-permute-done((f32[16,128]{1,0:T(8,128)S(1)}, f32[16,128]{1,0:T(8,128)S(1)}, u32[]{:S(2)}, u32[]{:S(2)}) %collective-permute-start.8) | collective-permute-done | bytes 8224 | tf_op jit(solution)/shard_map/ppermute | solution.py:499
  41.4 0.0 collective-permute-start.9
  41.4 3.7 %collective-permute-done.9 = f32[2,16,128]{2,1,0:T(8,128)S(1)} collective-permute-done((f32[2,16,128]{2,1,0:T(8,128)S(1)}, f32[2,16,128]{2,1,0:T(8,128)S(1)}, u32[]{:S(2)}, u32[]{:S(2)}) %collective-permute-start.9) | collective-permute-done | bytes 16416 | tf_op jit(solution)/shard_map/ppermute | solution.py:500
  45.2 0.0 collective-permute-start.10
  45.2 3.6 %collective-permute-done.10 = f32[16,128]{1,0:T(8,128)S(1)} collective-permute-done((f32[16,128]{1,0:T(8,128)S(1)}, f32[16,128]{1,0:T(8,128)S(1)}, u32[]{:S(2)}, u32[]{:S(2)}) %collective-permute-start.10) | collective-permute-done | bytes 8224 | tf_op jit(solution)/shard_map/ppermute | solution.py:501
  48.8 3.7 %collective-permute-start.11 = (f32[5,16,128]{2,1,0:T(8,128)S(1)}, f32[5,16,128]{2,1,0:T(8,128)S(1)}, u32[]{:S(2)}, u32[]{:S(2)}) collective-permute-start(f32[5,16,128]{2,1,0:T(8,128)S(1)} %pad_maximum_fusion.3.mine), channel_id=1, source_target_pairs={{0,64},{64,0},{128,192},{192,128},{1,65},{65,1},{129,193},{193,129... | collective-permute-start | bytes 122888 | tf_op jit(solution)/shard_map/ppermute | solution.py:503
  52.5 0.9 %collective-permute-done.11.sib = f32[5,16,128]{2,1,0:T(8,128)S(1)} collective-permute-done((f32[5,16,128]{2,1,0:T(8,128)S(1)}, f32[5,16,128]{2,1,0:T(8,128)S(1)}, u32[]{:S(2)}, u32[]{:S(2)}) %collective-permute-start.11) | collective-permute-done | bytes 40992 | tf_op jit(solution)/shard_map/ppermute | solution.py:503
  53.4 0.9 %relax.1 = (f32[1,2,1,32]{3,2,1,0:T(1,128)}, f32[1,1,32]{2,1,0:T(1,128)}, f32[1,2,1,32]{3,2,1,0:T(1,128)}) custom-call(f32[5,16,128]{2,1,0:T(8,128)S(1)} %pad_maximum_fusion.3.mine, f32[5,16,128]{2,1,0:T(8,128)S(1)} %collective-permute-done.11.sib), custom_call_target="tpu_custom_call" | custom-call | tf_op jit(solution)/shard_map/relax/pallas_call | solution.py:504
  (12 shorter events, 0.2 us)
Async XLA Ops:
  0.6 26.8 %copy-start.2 = (bf16[128,256]{1,0:T(8,128)(2,1)S(1)}, bf16[128,256]{1,0:T(8,128)(2,1)}, u32[]{:S(2)}) copy-start(bf16[128,256]{1,0:T(8,128)(2,1)} %constant.73.clone.rows2) | copy-start | bytes 196612
  0.6 26.8 %copy-start = (bf16[768,256]{1,0:T(8,128)(2,1)S(1)}, bf16[768,256]{1,0:T(8,128)(2,1)}, u32[]{:S(2)}) copy-start(bf16[768,256]{1,0:T(8,128)(2,1)} %constant.74.clone.fwd) | copy-start | bytes 1179652
  1.4 1.0 %copy-start.3 = (bf16[1,64,2048]{2,1,0:T(8,128)(2,1)S(1)}, bf16[1,64,2048]{2,1,0:T(8,128)(2,1)}, u32[]{:S(2)}) copy-start(bf16[1,64,2048]{2,1,0:T(8,128)(2,1)} %strip.1) | copy-start | bytes 786436
  2.3 21.0 %copy-start.6 = (bf16[2,64,2048]{2,1,0:T(8,128)(2,1)S(1)}, bf16[2,64,2048]{2,1,0:T(8,128)(2,1)}, u32[]{:S(2)}) copy-start(bf16[2,64,2048]{2,1,0:T(8,128)(2,1)} %param.9) | copy-start | bytes 1572868
  2.5 1.5 %collective-permute-start = (bf16[2,64,640]{2,1,0:T(8,128)(2,1)S(1)}, bf16[2,64,640]{2,1,0:T(8,128)(2,1)S(1)}, u32[]{:S(2)}, u32[]{:S(2)}) collective-permute-start(bf16[2,64,640]{2,1,0:T(8,128)(2,1)S(1)} %get-tuple-element.9), channel_id=1, source_target_pairs={{0,64},{64,0},{128,192},{192,128},{1,65},{65,1},{129,193},{193,129... | collective-permute-start | bytes 491528 | tf_op jit(solution)/shard_map/ppermute | solution.py:440
  3.8 25.5 %copy-start.1 = (bf16[768,256]{1,0:T(8,128)(2,1)S(1)}, bf16[768,256]{1,0:T(8,128)(2,1)}, u32[]{:S(2)}) copy-start(bf16[768,256]{1,0:T(8,128)(2,1)} %constant.75.clone.inv3) | copy-start | bytes 1179652
  3.8 25.5 %copy-start.4 = (bf16[128,384]{1,0:T(8,128)(2,1)S(1)}, bf16[128,384]{1,0:T(8,128)(2,1)}, u32[]{:S(2)}) copy-start(bf16[128,384]{1,0:T(8,128)(2,1)} %constant.76.clone.back3) | copy-start | bytes 294916
  3.8 25.5 %copy-start.5 = (s32[1,1,32]{2,1,0:T(1,128)S(1)}, s32[1,1,32]{2,1,0:T(1,128)}, u32[]{:S(2)}) copy-start(s32[1,1,32]{2,1,0:T(1,128)} %valid.1) | copy-start | bytes 388
  4.0 14.7 %collective-permute-start.3 = (bf16[2,64,640]{2,1,0:T(8,128)(2,1)S(1)}, bf16[2,64,640]{2,1,0:T(8,128)(2,1)S(1)}, u32[]{:S(2)}, u32[]{:S(2)}) collective-permute-start(bf16[2,64,640]{2,1,0:T(8,128)(2,1)S(1)} %pad_maximum_fusion.2), channel_id=1, source_target_pairs={{0,128},{64,192},{128,0},{192,64},{1,129},{65,193},{129,1},{193,65... | collective-permute-start | bytes 491528 | tf_op jit(solution)/shard_map/ppermute | solution.py:441
  10.5 16.9 %collective-permute-start.2 = (bf16[4,32,640]{2,1,0:T(8,128)(2,1)S(1)}, bf16[4,32,640]{2,1,0:T(8,128)(2,1)S(1)}, u32[]{:S(2)}, u32[]{:S(2)}) collective-permute-start(bf16[4,32,640]{2,1,0:T(8,128)(2,1)S(1)} %pad_maximum_fusion.1), channel_id=1, source_target_pairs={{0,64},{1,2},{2,1},{3,4},{4,3},{5,6},{6,5},{7,8},{8,7},{9,10},{10,... | collective-permute-start | bytes 491528 | tf_op jit(solution)/shard_map/ppermute | solution.py:455
  16.2 11.2 %collective-permute-start.1 = (bf16[4,32,640]{2,1,0:T(8,128)(2,1)S(1)}, bf16[4,32,640]{2,1,0:T(8,128)(2,1)S(1)}, u32[]{:S(2)}, u32[]{:S(2)}) collective-permute-start(bf16[4,32,640]{2,1,0:T(8,128)(2,1)S(1)} %pad_maximum_fusion), channel_id=1, source_target_pairs={{0,1},{1,0},{2,3},{3,2},{4,5},{5,4},{6,7},{7,6},{8,9},{9,8},{10,11... | collective-permute-start | bytes 491528 | tf_op jit(solution)/shard_map/ppermute | solution.py:456
  18.7 10.5 %collective-permute-start.4 = (bf16[2,32,640]{2,1,0:T(8,128)(2,1)S(1)}, bf16[2,32,640]{2,1,0:T(8,128)(2,1)S(1)}, u32[]{:S(2)}, u32[]{:S(2)}) collective-permute-start(bf16[2,32,640]{2,1,0:T(8,128)(2,1)S(1)} %get-tuple-element.16), channel_id=1, source_target_pairs={{0,64},{1,2},{2,1},{3,4},{4,3},{5,6},{6,5},{7,8},{8,7},{9,10},{10,... | collective-permute-start | bytes 245768 | tf_op jit(solution)/shard_map/ppermute | solution.py:457
  23.3 6.0 %collective-permute-start.5 = (bf16[2,32,640]{2,1,0:T(8,128)(2,1)S(1)}, bf16[2,32,640]{2,1,0:T(8,128)(2,1)S(1)}, u32[]{:S(2)}, u32[]{:S(2)}) collective-permute-start(bf16[2,32,640]{2,1,0:T(8,128)(2,1)S(1)} %get-tuple-element.15), channel_id=1, source_target_pairs={{0,1},{1,0},{2,3},{3,2},{4,5},{5,4},{6,7},{7,6},{8,9},{9,8},{10,11... | collective-permute-start | bytes 245768 | tf_op jit(solution)/shard_map/ppermute | solution.py:458
  32.8 1.3 %collective-permute-start.6 = (f32[16,128]{1,0:T(8,128)S(1)}, f32[16,128]{1,0:T(8,128)S(1)}, u32[]{:S(2)}, u32[]{:S(2)}) collective-permute-start(f32[16,128]{1,0:T(8,128)S(1)} %correlate.1), channel_id=1, source_target_pairs={{0,64},{64,0},{128,192},{192,128},{1,65},{65,1},{129,193},{193,129... | collective-permute-start | bytes 24584 | tf_op jit(solution)/shard_map/ppermute | solution.py:497
  34.1 3.7 %collective-permute-start.7 = (f32[16,128]{1,0:T(8,128)S(1)}, f32[16,128]{1,0:T(8,128)S(1)}, u32[]{:S(2)}, u32[]{:S(2)}) collective-permute-start(f32[16,128]{1,0:T(8,128)S(1)} %add.31), channel_id=1, source_target_pairs={{0,1},{1,0},{2,3},{3,2},{4,5},{5,4},{6,7},{7,6},{8,9},{9,8},{10,11... | collective-permute-start | bytes 24584 | tf_op jit(solution)/shard_map/ppermute | solution.py:498
  37.8 3.7 %collective-permute-start.8 = (f32[16,128]{1,0:T(8,128)S(1)}, f32[16,128]{1,0:T(8,128)S(1)}, u32[]{:S(2)}, u32[]{:S(2)}) collective-permute-start(f32[16,128]{1,0:T(8,128)S(1)} %add.32), channel_id=1, source_target_pairs={{0,1},{1,0},{2,3},{3,2},{4,5},{5,4},{6,7},{7,6},{8,9},{9,8},{10,11... | collective-permute-start | bytes 24584 | tf_op jit(solution)/shard_map/ppermute | solution.py:499
  41.4 3.7 %collective-permute-start.9 = (f32[2,16,128]{2,1,0:T(8,128)S(1)}, f32[2,16,128]{2,1,0:T(8,128)S(1)}, u32[]{:S(2)}, u32[]{:S(2)}) collective-permute-start(f32[2,16,128]{2,1,0:T(8,128)S(1)} %pad_maximum_fusion.4), channel_id=1, source_target_pairs={{0,1},{1,0},{2,3},{3,2},{4,5},{5,4},{6,7},{7,6},{8,9},{9,8},{10,11... | collective-permute-start | bytes 49160 | tf_op jit(solution)/shard_map/ppermute | solution.py:500
  45.2 3.7 %collective-permute-start.10 = (f32[16,128]{1,0:T(8,128)S(1)}, f32[16,128]{1,0:T(8,128)S(1)}, u32[]{:S(2)}, u32[]{:S(2)}) collective-permute-start(f32[16,128]{1,0:T(8,128)S(1)} %slice_bitcast_fusion), channel_id=1, source_target_pairs={{0,1},{1,0},{2,3},{3,2},{4,5},{5,4},{6,7},{7,6},{8,9},{9,8},{10,11... | collective-permute-start | bytes 24584 | tf_op jit(solution)/shard_map/ppermute | solution.py:501
  48.8 4.6 %collective-permute-start.11 = (f32[5,16,128]{2,1,0:T(8,128)S(1)}, f32[5,16,128]{2,1,0:T(8,128)S(1)}, u32[]{:S(2)}, u32[]{:S(2)}) collective-permute-start(f32[5,16,128]{2,1,0:T(8,128)S(1)} %pad_maximum_fusion.3.mine), channel_id=1, source_target_pairs={{0,64},{64,0},{128,192},{192,128},{1,65},{65,1},{129,193},{193,129... | collective-permute-start | bytes 122888 | tf_op jit(solution)/shard_map/ppermute | solution.py:503

commit v5 on v4

--- a/solution.py
+++ b/solution.py
@@ -208,17 +208,7 @@
         lambda i: energy.at[slots[4 + i]],
     )
 
-    products = []
-    prior = []
-    for s in range(SECTIONS):
-        prev = s + 2 - off_s[s]
-        prior.append(prev)
-        for h in range(2):
-            f, g = spec0[s + 2, h], spec0[prev, h]
-            fr, fi = f[:, :PATCH], f[:, PATCH:]
-            gr, gi = g[:, :PATCH], g[:, PATCH:]
-            products.append(jnp.concatenate([fr * gr + fi * gi, fi * gr - fr * gi], axis=1))
-    u0 = dot3(jnp.concatenate(products, axis=0), inv3[0:256, 0:PATCH], inv3[512:768, 0:PATCH])
+    prior = [s + 2 - off_s[s] for s in range(SECTIONS)]
     for copy in copies:
         copy.wait()
 
@@ -240,12 +230,27 @@
             lows.append(plo)
         ph, plo = jnp.concatenate(highs, axis=0), jnp.concatenate(lows, axis=0)
         u = dot(jnp.concatenate([ph, plo, ph], axis=1), inv3[...])
+        for j in range(QCOLS):
+            u_ref[s, j] = u[HALF * j : HALF * (j + 1)]
+
+    def edges():
+        products = []
+        for s in range(SECTIONS):
+            for h in range(2):
+                f, g = spec0[s + 2, h], spec0[prior[s], h]
+                fr, fi = f[:, :PATCH], f[:, PATCH:]
+                gr, gi = g[:, :PATCH], g[:, PATCH:]
+                products.append(jnp.concatenate([fr * gr + fi * gi, fi * gr - fr * gi], axis=1))
+        return dot3(
+            jnp.concatenate(products, axis=0), inv3[0:256, 0:PATCH], inv3[512:768, 0:PATCH]
+        )
+
+    def patch_rows(s):
         first = 2 * QCOLS * s
         edge_rows = jnp.concatenate(
             [u0[first : first + QCOLS], u0[first + QCOLS : first + 2 * QCOLS]], axis=1
         )
         for j in range(QCOLS):
-            u_ref[s, j] = u[HALF * j : HALF * (j + 1)]
             u_ref[s, j, 0:1, :] = edge_rows[j : j + 1]
 
     def shifts(s):
@@ -284,11 +289,15 @@
             part[k, 8 + s : 9 + s, :] = total
 
     inverse(0)
+    u0 = edges()
     for s in range(SECTIONS):
         if s + 1 < SECTIONS:
             inverse(s + 1)
+        patch_rows(s)
         shifts(s)
-        soften(s)
+        if s:
+            soften(s - 1)
+    soften(SECTIONS - 1)
 
     lane16 = iota((FEATS, LANES), 1)
     lane4 = iota((SECTIONS, LANES), 1)

time: 54.9 us -> 54.7 us (level)
  no operation moved by 1% of the time
where the time goes in v5:
time: 54.7 us; the launch traced here: 54.1 us
  waiting for transfers between devices  23.2 us (42%)
  starting transfers between devices  20.6 us (38%)
  Pallas kernels  6.24 us (11%)
  local copies, waits for them, and re-layouts  2.31 us (4%)
  between operations  1.55 us (3%)
    ppermute x1, starting transfers between devices, per_device(): lax.ppermute(jnp.stack([keep[1], sib[1]]), 'sec', xor_route(SECTIONS, 2))  6.38 us
    ppermute x1, starting transfers between devices, per_device(): far_local = swap_odd(rows(local, to_odd))  5.74 us
    ppermute x1, starting transfers between devices, per_device(): far_across = swap_odd(rows((across,), to_odd))  4.54 us
    ppermute x1, waiting for transfers between devices, per_device(): far_local = swap_odd(rows(local, to_odd))  4.01 us
    ppermute x1, waiting for transfers between devices, per_device(): far = swap(jnp.stack([cells, near]), perm=gather_route(tile_count, 'odd'))  3.74 us
    ppermute x1, starting transfers between devices, per_device(): shared = lax.ppermute(bundle, 'sec', xor_route(SECTIONS, 1))  3.69 us
    ppermute x1, waiting for transfers between devices, per_device(): cells = cells + swap(cells, perm=gather_route(tile_count, 'z'))  3.65 us
    ppermute x1, waiting for transfers between devices, per_device(): near = swap(cells, perm=gather_route(tile_count, 'even'))  3.65 us
  transfers between devices with their start and end apart: 12, of which 9 were waited for; matrix products, arithmetic and copies ran while one was open for 3% of the time, Pallas kernels for 3%

profile of v5, /device:TPU:32, one launch (start us, length us, event | category | flops | bytes accessed | tf_op | source)
XLA Modules:
  0.0 54.1 jit_solution(12704347299203592916)
XLA Ops:
  0.6 0.0 copy-start.2
  0.6 0.0 copy-start
  1.4 0.0 copy-start.3
  1.4 0.9 %copy-done.3 = bf16[1,64,2048]{2,1,0:T(8,128)(2,1)S(1)} copy-done((bf16[1,64,2048]{2,1,0:T(8,128)(2,1)S(1)}, bf16[1,64,2048]{2,1,0:T(8,128)(2,1)}, u32[]{:S(2)}) %copy-start.3) | copy-done | bytes 262168
  2.3 0.0 copy-start.6
  2.3 0.2 prepare.1
  2.5 0.1 collective-permute-start
  2.7 1.1 %pad_dynamic-slice_fusion = (bf16[2,32,640]{2,1,0:T(8,128)(2,1)S(1)}, bf16[2,32,640]{2,1,0:T(8,128)(2,1)S(1)}) fusion(s32[]{:T(128)S(6)} %select_n.37, s32[]{:T(128)S(6)} %select_n.35, bf16[2,64,2048]{2,1,0:T(8,128)(2,1)} %param.9, s32[]{:T(128)S(6)} %select_n.34), kind=kLoop, calls=%fused_computation | loop fusion | bytes 688140 | tf_op jit(solution)/shard_map/dynamic_slice | solution.py:460
  3.8 0.0 copy-start.1
  3.8 0.0 copy-start.4
  3.8 0.0 copy-start.5
  3.8 0.2 collective-permute-done.sib
  4.0 6.4 %collective-permute-start.3 = (bf16[2,64,640]{2,1,0:T(8,128)(2,1)S(1)}, bf16[2,64,640]{2,1,0:T(8,128)(2,1)S(1)}, u32[]{:S(2)}, u32[]{:S(2)}) collective-permute-start(bf16[2,64,640]{2,1,0:T(8,128)(2,1)S(1)} %pad_maximum_fusion.2), channel_id=1, source_target_pairs={{0,128},{64,192},{128,0},{192,64},{1,129},{65,193},{129,1},{193,65... | collective-permute-start | bytes 491528 | tf_op jit(solution)/shard_map/ppermute | solution.py:450
  10.5 5.7 %collective-permute-start.2 = (bf16[4,32,640]{2,1,0:T(8,128)(2,1)S(1)}, bf16[4,32,640]{2,1,0:T(8,128)(2,1)S(1)}, u32[]{:S(2)}, u32[]{:S(2)}) collective-permute-start(bf16[4,32,640]{2,1,0:T(8,128)(2,1)S(1)} %pad_maximum_fusion.1), channel_id=1, source_target_pairs={{0,64},{1,2},{2,1},{3,4},{4,3},{5,6},{6,5},{7,8},{8,7},{9,10},{10,... | collective-permute-start | bytes 491528 | tf_op jit(solution)/shard_map/ppermute | solution.py:464
  16.2 0.1 collective-permute-start.1
  16.3 2.4 %collective-permute-done.3.across = bf16[2,64,640]{2,1,0:T(8,128)(2,1)S(1)} collective-permute-done((bf16[2,64,640]{2,1,0:T(8,128)(2,1)S(1)}, bf16[2,64,640]{2,1,0:T(8,128)(2,1)S(1)}, u32[]{:S(2)}, u32[]{:S(2)}) %collective-permute-start.3) | collective-permute-done | bytes 163872 | tf_op jit(solution)/shard_map/ppermute | solution.py:450
  18.7 4.5 %collective-permute-start.4 = (bf16[2,32,640]{2,1,0:T(8,128)(2,1)S(1)}, bf16[2,32,640]{2,1,0:T(8,128)(2,1)S(1)}, u32[]{:S(2)}, u32[]{:S(2)}) collective-permute-start(bf16[2,32,640]{2,1,0:T(8,128)(2,1)S(1)} %get-tuple-element.16), channel_id=1, source_target_pairs={{0,64},{1,2},{2,1},{3,4},{4,3},{5,6},{6,5},{7,8},{8,7},{9,10},{10,... | collective-permute-start | bytes 245768 | tf_op jit(solution)/shard_map/ppermute | solution.py:466
  23.3 0.0 collective-permute-start.5
  23.3 0.0 copy-done.6
  23.3 0.1 pad_dynamic-slice_fusion.2.eq
  23.4 4.0 %collective-permute-done.2.far = bf16[4,32,640]{2,1,0:T(8,128)(2,1)S(1)} collective-permute-done((bf16[4,32,640]{2,1,0:T(8,128)(2,1)S(1)}, bf16[4,32,640]{2,1,0:T(8,128)(2,1)S(1)}, u32[]{:S(2)}, u32[]{:S(2)}) %collective-permute-start.2) | collective-permute-done | bytes 163872 | tf_op jit(solution)/shard_map/ppermute | solution.py:464
  27.4 0.0 collective-permute-done.1.near
  27.4 0.0 copy-done.2
  27.4 0.0 copy-done
  27.4 1.8 %early.1 = (f32[4,8,64,256]{3,2,1,0:T(8,128)S(1)}, f32[4,2,8,256]{3,2,1,0:T(8,128)S(1)}, f32[4,8,128]{2,1,0:T(8,128)S(1)}) custom-call(bf16[2,64,640]{2,1,0:T(8,128)(2,1)S(1)} %pad_dynamic-slice_fusion.2.eq, bf16[2,64,640]{2,1,0:T(8,128)(2,1)S(1)} %get-tuple-element.8.keep, bf16[2,64,640]{2,1,0:T(8,128)(2,1)S(1)} %collective-permute-done.sib, ...), custom_call_target="tpu_custom_call" | custom-call | tf_op jit(solution)/shard_map/early/pallas_call | solution.py:469
  29.3 0.0 collective-permute-done.4.far
  29.3 0.0 collective-permute-done.5.near
  29.3 0.0 copy-done.1
  29.3 0.0 copy-done.4
  29.3 0.0 copy-done.5
  29.3 3.3 %correlate.1 = f32[16,128]{1,0:T(8,128)S(1)} custom-call(f32[4,8,64,256]{3,2,1,0:T(8,128)S(1)} %get-tuple-element.10.spec_in, f32[4,2,8,256]{3,2,1,0:T(8,128)S(1)} %get-tuple-element.11.edge_in, f32[4,8,128]{2,1,0:T(8,128)S(1)} %get-tuple-element.12.energy_in, bf16[2,64,640]{2,1,0:T(8,128)(2,1)S(1)} %get-tuple-element.8.keep, ...), custom_call_target="tpu_custom_call" | custom-call | tf_op jit(solution)/shard_map/correlate/pallas_call | solution.py:482
  32.6 0.1 collective-permute-start.6
  32.7 1.2 %collective-permute-done.6 = f32[16,128]{1,0:T(8,128)S(1)} collective-permute-done((f32[16,128]{1,0:T(8,128)S(1)}, f32[16,128]{1,0:T(8,128)S(1)}, u32[]{:S(2)}, u32[]{:S(2)}) %collective-permute-start.6) | collective-permute-done | bytes 8224 | tf_op jit(solution)/shard_map/ppermute | solution.py:506
  33.9 0.0 collective-permute-start.7
  33.9 3.6 %collective-permute-done.7 = f32[16,128]{1,0:T(8,128)S(1)} collective-permute-done((f32[16,128]{1,0:T(8,128)S(1)}, f32[16,128]{1,0:T(8,128)S(1)}, u32[]{:S(2)}, u32[]{:S(2)}) %collective-permute-start.7) | collective-permute-done | bytes 8224 | tf_op jit(solution)/shard_map/ppermute | solution.py:507
  37.6 0.0 collective-permute-start.8
  37.6 3.6 %collective-permute-done.8 = f32[16,128]{1,0:T(8,128)S(1)} collective-permute-done((f32[16,128]{1,0:T(8,128)S(1)}, f32[16,128]{1,0:T(8,128)S(1)}, u32[]{:S(2)}, u32[]{:S(2)}) %collective-permute-start.8) | collective-permute-done | bytes 8224 | tf_op jit(solution)/shard_map/ppermute | solution.py:508
  41.2 0.0 collective-permute-start.9
  41.2 3.7 %collective-permute-done.9 = f32[2,16,128]{2,1,0:T(8,128)S(1)} collective-permute-done((f32[2,16,128]{2,1,0:T(8,128)S(1)}, f32[2,16,128]{2,1,0:T(8,128)S(1)}, u32[]{:S(2)}, u32[]{:S(2)}) %collective-permute-start.9) | collective-permute-done | bytes 16416 | tf_op jit(solution)/shard_map/ppermute | solution.py:509
  45.0 0.0 collective-permute-start.10
  45.0 3.6 %collective-permute-done.10 = f32[16,128]{1,0:T(8,128)S(1)} collective-permute-done((f32[16,128]{1,0:T(8,128)S(1)}, f32[16,128]{1,0:T(8,128)S(1)}, u32[]{:S(2)}, u32[]{:S(2)}) %collective-permute-start.10) | collective-permute-done | bytes 8224 | tf_op jit(solution)/shard_map/ppermute | solution.py:510
  48.6 3.7 %collective-permute-start.11 = (f32[5,16,128]{2,1,0:T(8,128)S(1)}, f32[5,16,128]{2,1,0:T(8,128)S(1)}, u32[]{:S(2)}, u32[]{:S(2)}) collective-permute-start(f32[5,16,128]{2,1,0:T(8,128)S(1)} %pad_maximum_fusion.3.mine), channel_id=1, source_target_pairs={{0,64},{64,0},{128,192},{192,128},{1,65},{65,1},{129,193},{193,129... | collective-permute-start | bytes 122888 | tf_op jit(solution)/shard_map/ppermute | solution.py:512
  52.3 0.9 %collective-permute-done.11.sib = f32[5,16,128]{2,1,0:T(8,128)S(1)} collective-permute-done((f32[5,16,128]{2,1,0:T(8,128)S(1)}, f32[5,16,128]{2,1,0:T(8,128)S(1)}, u32[]{:S(2)}, u32[]{:S(2)}) %collective-permute-start.11) | collective-permute-done | bytes 40992 | tf_op jit(solution)/shard_map/ppermute | solution.py:512
  53.2 0.9 %relax.1 = (f32[1,2,1,32]{3,2,1,0:T(1,128)}, f32[1,1,32]{2,1,0:T(1,128)}, f32[1,2,1,32]{3,2,1,0:T(1,128)}) custom-call(f32[5,16,128]{2,1,0:T(8,128)S(1)} %pad_maximum_fusion.3.mine, f32[5,16,128]{2,1,0:T(8,128)S(1)} %collective-permute-done.11.sib), custom_call_target="tpu_custom_call" | custom-call | tf_op jit(solution)/shard_map/relax/pallas_call | solution.py:513
  (12 shorter events, 0.2 us)
Async XLA Ops:
  0.6 26.8 %copy-start.2 = (bf16[128,256]{1,0:T(8,128)(2,1)S(1)}, bf16[128,256]{1,0:T(8,128)(2,1)}, u32[]{:S(2)}) copy-start(bf16[128,256]{1,0:T(8,128)(2,1)} %constant.73.clone.rows2) | copy-start | bytes 196612
  0.6 26.8 %copy-start = (bf16[768,256]{1,0:T(8,128)(2,1)S(1)}, bf16[768,256]{1,0:T(8,128)(2,1)}, u32[]{:S(2)}) copy-start(bf16[768,256]{1,0:T(8,128)(2,1)} %constant.74.clone.fwd) | copy-start | bytes 1179652
  1.4 1.0 %copy-start.3 = (bf16[1,64,2048]{2,1,0:T(8,128)(2,1)S(1)}, bf16[1,64,2048]{2,1,0:T(8,128)(2,1)}, u32[]{:S(2)}) copy-start(bf16[1,64,2048]{2,1,0:T(8,128)(2,1)} %strip.1) | copy-start | bytes 786436
  2.3 21.0 %copy-start.6 = (bf16[2,64,2048]{2,1,0:T(8,128)(2,1)S(1)}, bf16[2,64,2048]{2,1,0:T(8,128)(2,1)}, u32[]{:S(2)}) copy-start(bf16[2,64,2048]{2,1,0:T(8,128)(2,1)} %param.9) | copy-start | bytes 1572868
  2.5 1.5 %collective-permute-start = (bf16[2,64,640]{2,1,0:T(8,128)(2,1)S(1)}, bf16[2,64,640]{2,1,0:T(8,128)(2,1)S(1)}, u32[]{:S(2)}, u32[]{:S(2)}) collective-permute-start(bf16[2,64,640]{2,1,0:T(8,128)(2,1)S(1)} %get-tuple-element.9), channel_id=1, source_target_pairs={{0,64},{64,0},{128,192},{192,128},{1,65},{65,1},{129,193},{193,129... | collective-permute-start | bytes 491528 | tf_op jit(solution)/shard_map/ppermute | solution.py:449
  3.8 25.5 %copy-start.1 = (bf16[768,256]{1,0:T(8,128)(2,1)S(1)}, bf16[768,256]{1,0:T(8,128)(2,1)}, u32[]{:S(2)}) copy-start(bf16[768,256]{1,0:T(8,128)(2,1)} %constant.75.clone.inv3) | copy-start | bytes 1179652
  3.8 25.5 %copy-start.4 = (bf16[128,384]{1,0:T(8,128)(2,1)S(1)}, bf16[128,384]{1,0:T(8,128)(2,1)}, u32[]{:S(2)}) copy-start(bf16[128,384]{1,0:T(8,128)(2,1)} %constant.76.clone.back3) | copy-start | bytes 294916
  3.8 25.5 %copy-start.5 = (s32[1,1,32]{2,1,0:T(1,128)S(1)}, s32[1,1,32]{2,1,0:T(1,128)}, u32[]{:S(2)}) copy-start(s32[1,1,32]{2,1,0:T(1,128)} %valid.1) | copy-start | bytes 388
  4.0 14.7 %collective-permute-start.3 = (bf16[2,64,640]{2,1,0:T(8,128)(2,1)S(1)}, bf16[2,64,640]{2,1,0:T(8,128)(2,1)S(1)}, u32[]{:S(2)}, u32[]{:S(2)}) collective-permute-start(bf16[2,64,640]{2,1,0:T(8,128)(2,1)S(1)} %pad_maximum_fusion.2), channel_id=1, source_target_pairs={{0,128},{64,192},{128,0},{192,64},{1,129},{65,193},{129,1},{193,65... | collective-permute-start | bytes 491528 | tf_op jit(solution)/shard_map/ppermute | solution.py:450
  10.5 16.9 %collective-permute-start.2 = (bf16[4,32,640]{2,1,0:T(8,128)(2,1)S(1)}, bf16[4,32,640]{2,1,0:T(8,128)(2,1)S(1)}, u32[]{:S(2)}, u32[]{:S(2)}) collective-permute-start(bf16[4,32,640]{2,1,0:T(8,128)(2,1)S(1)} %pad_maximum_fusion.1), channel_id=1, source_target_pairs={{0,64},{1,2},{2,1},{3,4},{4,3},{5,6},{6,5},{7,8},{8,7},{9,10},{10,... | collective-permute-start | bytes 491528 | tf_op jit(solution)/shard_map/ppermute | solution.py:464
  16.2 11.2 %collective-permute-start.1 = (bf16[4,32,640]{2,1,0:T(8,128)(2,1)S(1)}, bf16[4,32,640]{2,1,0:T(8,128)(2,1)S(1)}, u32[]{:S(2)}, u32[]{:S(2)}) collective-permute-start(bf16[4,32,640]{2,1,0:T(8,128)(2,1)S(1)} %pad_maximum_fusion), channel_id=1, source_target_pairs={{0,1},{1,0},{2,3},{3,2},{4,5},{5,4},{6,7},{7,6},{8,9},{9,8},{10,11... | collective-permute-start | bytes 491528 | tf_op jit(solution)/shard_map/ppermute | solution.py:465
  18.7 10.5 %collective-permute-start.4 = (bf16[2,32,640]{2,1,0:T(8,128)(2,1)S(1)}, bf16[2,32,640]{2,1,0:T(8,128)(2,1)S(1)}, u32[]{:S(2)}, u32[]{:S(2)}) collective-permute-start(bf16[2,32,640]{2,1,0:T(8,128)(2,1)S(1)} %get-tuple-element.16), channel_id=1, source_target_pairs={{0,64},{1,2},{2,1},{3,4},{4,3},{5,6},{6,5},{7,8},{8,7},{9,10},{10,... | collective-permute-start | bytes 245768 | tf_op jit(solution)/shard_map/ppermute | solution.py:466
  23.3 6.0 %collective-permute-start.5 = (bf16[2,32,640]{2,1,0:T(8,128)(2,1)S(1)}, bf16[2,32,640]{2,1,0:T(8,128)(2,1)S(1)}, u32[]{:S(2)}, u32[]{:S(2)}) collective-permute-start(bf16[2,32,640]{2,1,0:T(8,128)(2,1)S(1)} %get-tuple-element.15), channel_id=1, source_target_pairs={{0,1},{1,0},{2,3},{3,2},{4,5},{5,4},{6,7},{7,6},{8,9},{9,8},{10,11... | collective-permute-start | bytes 245768 | tf_op jit(solution)/shard_map/ppermute | solution.py:467
  32.6 1.3 %collective-permute-start.6 = (f32[16,128]{1,0:T(8,128)S(1)}, f32[16,128]{1,0:T(8,128)S(1)}, u32[]{:S(2)}, u32[]{:S(2)}) collective-permute-start(f32[16,128]{1,0:T(8,128)S(1)} %correlate.1), channel_id=1, source_target_pairs={{0,64},{64,0},{128,192},{192,128},{1,65},{65,1},{129,193},{193,129... | collective-permute-start | bytes 24584 | tf_op jit(solution)/shard_map/ppermute | solution.py:506
  33.9 3.7 %collective-permute-start.7 = (f32[16,128]{1,0:T(8,128)S(1)}, f32[16,128]{1,0:T(8,128)S(1)}, u32[]{:S(2)}, u32[]{:S(2)}) collective-permute-start(f32[16,128]{1,0:T(8,128)S(1)} %add.31), channel_id=1, source_target_pairs={{0,1},{1,0},{2,3},{3,2},{4,5},{5,4},{6,7},{7,6},{8,9},{9,8},{10,11... | collective-permute-start | bytes 24584 | tf_op jit(solution)/shard_map/ppermute | solution.py:507
  37.6 3.7 %collective-permute-start.8 = (f32[16,128]{1,0:T(8,128)S(1)}, f32[16,128]{1,0:T(8,128)S(1)}, u32[]{:S(2)}, u32[]{:S(2)}) collective-permute-start(f32[16,128]{1,0:T(8,128)S(1)} %add.32), channel_id=1, source_target_pairs={{0,1},{1,0},{2,3},{3,2},{4,5},{5,4},{6,7},{7,6},{8,9},{9,8},{10,11... | collective-permute-start | bytes 24584 | tf_op jit(solution)/shard_map/ppermute | solution.py:508
  41.2 3.7 %collective-permute-start.9 = (f32[2,16,128]{2,1,0:T(8,128)S(1)}, f32[2,16,128]{2,1,0:T(8,128)S(1)}, u32[]{:S(2)}, u32[]{:S(2)}) collective-permute-start(f32[2,16,128]{2,1,0:T(8,128)S(1)} %pad_maximum_fusion.4), channel_id=1, source_target_pairs={{0,1},{1,0},{2,3},{3,2},{4,5},{5,4},{6,7},{7,6},{8,9},{9,8},{10,11... | collective-permute-start | bytes 49160 | tf_op jit(solution)/shard_map/ppermute | solution.py:509
  45.0 3.7 %collective-permute-start.10 = (f32[16,128]{1,0:T(8,128)S(1)}, f32[16,128]{1,0:T(8,128)S(1)}, u32[]{:S(2)}, u32[]{:S(2)}) collective-permute-start(f32[16,128]{1,0:T(8,128)S(1)} %slice_bitcast_fusion), channel_id=1, source_target_pairs={{0,1},{1,0},{2,3},{3,2},{4,5},{5,4},{6,7},{7,6},{8,9},{9,8},{10,11... | collective-permute-start | bytes 24584 | tf_op jit(solution)/shard_map/ppermute | solution.py:510
  48.6 4.6 %collective-permute-start.11 = (f32[5,16,128]{2,1,0:T(8,128)S(1)}, f32[5,16,128]{2,1,0:T(8,128)S(1)}, u32[]{:S(2)}, u32[]{:S(2)}) collective-permute-start(f32[5,16,128]{2,1,0:T(8,128)S(1)} %pad_maximum_fusion.3.mine), channel_id=1, source_target_pairs={{0,64},{64,0},{128,192},{192,128},{1,65},{65,1},{129,193},{193,129... | collective-permute-start | bytes 122888 | tf_op jit(solution)/shard_map/ppermute | solution.py:512

commit v6 on v5

--- a/solution.py
+++ b/solution.py
@@ -289,9 +289,10 @@
             part[k, 8 + s : 9 + s, :] = total
 
     inverse(0)
+    inverse(1)
     u0 = edges()
     for s in range(SECTIONS):
-        if s + 1 < SECTIONS:
+        if 0 < s < SECTIONS - 1:
             inverse(s + 1)
         patch_rows(s)
         shifts(s)

time: 54.7 us -> 54.8 us (level)
  no operation moved by 1% of the time
where the time goes in v6:
time: 54.8 us; the launch traced here: 54.2 us
  waiting for transfers between devices  23.2 us (42%)
  starting transfers between devices  20.6 us (38%)
  Pallas kernels  6.37 us (12%)
  local copies, waits for them, and re-layouts  2.31 us (4%)
  between operations  1.55 us (3%)
    ppermute x1, starting transfers between devices, per_device(): lax.ppermute(jnp.stack([keep[1], sib[1]]), 'sec', xor_route(SECTIONS, 2))  6.38 us
    ppermute x1, starting transfers between devices, per_device(): far_local = swap_odd(rows(local, to_odd))  5.74 us
    ppermute x1, starting transfers between devices, per_device(): far_across = swap_odd(rows((across,), to_odd))  4.54 us
    ppermute x1, waiting for transfers between devices, per_device(): far_local = swap_odd(rows(local, to_odd))  4.01 us
    ppermute x1, waiting for transfers between devices, per_device(): far = swap(jnp.stack([cells, near]), perm=gather_route(tile_count, 'odd'))  3.74 us
    ppermute x1, starting transfers between devices, per_device(): shared = lax.ppermute(bundle, 'sec', xor_route(SECTIONS, 1))  3.69 us
    ppermute x1, waiting for transfers between devices, per_device(): cells = cells + swap(cells, perm=gather_route(tile_count, 'z'))  3.65 us
    ppermute x1, waiting for transfers between devices, per_device(): near = swap(cells, perm=gather_route(tile_count, 'even'))  3.65 us
  transfers between devices with their start and end apart: 12, of which 9 were waited for; matrix products, arithmetic and copies ran while one was open for 3% of the time, Pallas kernels for 3%

profile of v6, /device:TPU:32, one launch (start us, length us, event | category | flops | bytes accessed | tf_op | source)
XLA Modules:
  0.0 54.2 jit_solution(4197111249304199000)
XLA Ops:
  0.6 0.0 copy-start.2
  0.6 0.0 copy-start
  1.4 0.0 copy-start.3
  1.4 0.9 %copy-done.3 = bf16[1,64,2048]{2,1,0:T(8,128)(2,1)S(1)} copy-done((bf16[1,64,2048]{2,1,0:T(8,128)(2,1)S(1)}, bf16[1,64,2048]{2,1,0:T(8,128)(2,1)}, u32[]{:S(2)}) %copy-start.3) | copy-done | bytes 262168
  2.3 0.0 copy-start.6
  2.3 0.2 prepare.1
  2.5 0.1 collective-permute-start
  2.7 1.1 %pad_dynamic-slice_fusion = (bf16[2,32,640]{2,1,0:T(8,128)(2,1)S(1)}, bf16[2,32,640]{2,1,0:T(8,128)(2,1)S(1)}) fusion(s32[]{:T(128)S(6)} %select_n.37, s32[]{:T(128)S(6)} %select_n.35, bf16[2,64,2048]{2,1,0:T(8,128)(2,1)} %param.9, s32[]{:T(128)S(6)} %select_n.34), kind=kLoop, calls=%fused_computation | loop fusion | bytes 688140 | tf_op jit(solution)/shard_map/dynamic_slice | solution.py:461
  3.8 0.0 copy-start.1
  3.8 0.0 copy-start.4
  3.8 0.0 copy-start.5
  3.8 0.2 collective-permute-done.sib
  4.0 6.4 %collective-permute-start.3 = (bf16[2,64,640]{2,1,0:T(8,128)(2,1)S(1)}, bf16[2,64,640]{2,1,0:T(8,128)(2,1)S(1)}, u32[]{:S(2)}, u32[]{:S(2)}) collective-permute-start(bf16[2,64,640]{2,1,0:T(8,128)(2,1)S(1)} %pad_maximum_fusion.2), channel_id=1, source_target_pairs={{0,128},{64,192},{128,0},{192,64},{1,129},{65,193},{129,1},{193,65... | collective-permute-start | bytes 491528 | tf_op jit(solution)/shard_map/ppermute | solution.py:451
  10.5 5.7 %collective-permute-start.2 = (bf16[4,32,640]{2,1,0:T(8,128)(2,1)S(1)}, bf16[4,32,640]{2,1,0:T(8,128)(2,1)S(1)}, u32[]{:S(2)}, u32[]{:S(2)}) collective-permute-start(bf16[4,32,640]{2,1,0:T(8,128)(2,1)S(1)} %pad_maximum_fusion.1), channel_id=1, source_target_pairs={{0,64},{1,2},{2,1},{3,4},{4,3},{5,6},{6,5},{7,8},{8,7},{9,10},{10,... | collective-permute-start | bytes 491528 | tf_op jit(solution)/shard_map/ppermute | solution.py:465
  16.2 0.1 collective-permute-start.1
  16.3 2.4 %collective-permute-done.3.across = bf16[2,64,640]{2,1,0:T(8,128)(2,1)S(1)} collective-permute-done((bf16[2,64,640]{2,1,0:T(8,128)(2,1)S(1)}, bf16[2,64,640]{2,1,0:T(8,128)(2,1)S(1)}, u32[]{:S(2)}, u32[]{:S(2)}) %collective-permute-start.3) | collective-permute-done | bytes 163872 | tf_op jit(solution)/shard_map/ppermute | solution.py:451
  18.7 4.5 %collective-permute-start.4 = (bf16[2,32,640]{2,1,0:T(8,128)(2,1)S(1)}, bf16[2,32,640]{2,1,0:T(8,128)(2,1)S(1)}, u32[]{:S(2)}, u32[]{:S(2)}) collective-permute-start(bf16[2,32,640]{2,1,0:T(8,128)(2,1)S(1)} %get-tuple-element.16), channel_id=1, source_target_pairs={{0,64},{1,2},{2,1},{3,4},{4,3},{5,6},{6,5},{7,8},{8,7},{9,10},{10,... | collective-permute-start | bytes 245768 | tf_op jit(solution)/shard_map/ppermute | solution.py:467
  23.3 0.0 collective-permute-start.5
  23.3 0.0 copy-done.6
  23.3 0.1 pad_dynamic-slice_fusion.2.eq
  23.4 4.0 %collective-permute-done.2.far = bf16[4,32,640]{2,1,0:T(8,128)(2,1)S(1)} collective-permute-done((bf16[4,32,640]{2,1,0:T(8,128)(2,1)S(1)}, bf16[4,32,640]{2,1,0:T(8,128)(2,1)S(1)}, u32[]{:S(2)}, u32[]{:S(2)}) %collective-permute-start.2) | collective-permute-done | bytes 163872 | tf_op jit(solution)/shard_map/ppermute | solution.py:465
  27.4 0.0 collective-permute-done.1.near
  27.4 0.0 copy-done.2
  27.4 0.0 copy-done
  27.4 1.8 %early.1 = (f32[4,8,64,256]{3,2,1,0:T(8,128)S(1)}, f32[4,2,8,256]{3,2,1,0:T(8,128)S(1)}, f32[4,8,128]{2,1,0:T(8,128)S(1)}) custom-call(bf16[2,64,640]{2,1,0:T(8,128)(2,1)S(1)} %pad_dynamic-slice_fusion.2.eq, bf16[2,64,640]{2,1,0:T(8,128)(2,1)S(1)} %get-tuple-element.8.keep, bf16[2,64,640]{2,1,0:T(8,128)(2,1)S(1)} %collective-permute-done.sib, ...), custom_call_target="tpu_custom_call" | custom-call | tf_op jit(solution)/shard_map/early/pallas_call | solution.py:470
  29.3 0.0 collective-permute-done.4.far
  29.3 0.0 collective-permute-done.5.near
  29.3 0.0 copy-done.1
  29.3 0.0 copy-done.4
  29.3 0.0 copy-done.5
  29.3 3.5 %correlate.1 = f32[16,128]{1,0:T(8,128)S(1)} custom-call(f32[4,8,64,256]{3,2,1,0:T(8,128)S(1)} %get-tuple-element.10.spec_in, f32[4,2,8,256]{3,2,1,0:T(8,128)S(1)} %get-tuple-element.11.edge_in, f32[4,8,128]{2,1,0:T(8,128)S(1)} %get-tuple-element.12.energy_in, bf16[2,64,640]{2,1,0:T(8,128)(2,1)S(1)} %get-tuple-element.8.keep, ...), custom_call_target="tpu_custom_call" | custom-call | tf_op jit(solution)/shard_map/correlate/pallas_call | solution.py:483
  32.8 0.1 collective-permute-start.6
  32.9 1.2 %collective-permute-done.6 = f32[16,128]{1,0:T(8,128)S(1)} collective-permute-done((f32[16,128]{1,0:T(8,128)S(1)}, f32[16,128]{1,0:T(8,128)S(1)}, u32[]{:S(2)}, u32[]{:S(2)}) %collective-permute-start.6) | collective-permute-done | bytes 8224 | tf_op jit(solution)/shard_map/ppermute | solution.py:507
  34.0 0.0 collective-permute-start.7
  34.0 3.6 %collective-permute-done.7 = f32[16,128]{1,0:T(8,128)S(1)} collective-permute-done((f32[16,128]{1,0:T(8,128)S(1)}, f32[16,128]{1,0:T(8,128)S(1)}, u32[]{:S(2)}, u32[]{:S(2)}) %collective-permute-start.7) | collective-permute-done | bytes 8224 | tf_op jit(solution)/shard_map/ppermute | solution.py:508
  37.7 0.0 collective-permute-start.8
  37.7 3.6 %collective-permute-done.8 = f32[16,128]{1,0:T(8,128)S(1)} collective-permute-done((f32[16,128]{1,0:T(8,128)S(1)}, f32[16,128]{1,0:T(8,128)S(1)}, u32[]{:S(2)}, u32[]{:S(2)}) %collective-permute-start.8) | collective-permute-done | bytes 8224 | tf_op jit(solution)/shard_map/ppermute | solution.py:509
  41.3 0.0 collective-permute-start.9
  41.3 3.7 %collective-permute-done.9 = f32[2,16,128]{2,1,0:T(8,128)S(1)} collective-permute-done((f32[2,16,128]{2,1,0:T(8,128)S(1)}, f32[2,16,128]{2,1,0:T(8,128)S(1)}, u32[]{:S(2)}, u32[]{:S(2)}) %collective-permute-start.9) | collective-permute-done | bytes 16416 | tf_op jit(solution)/shard_map/ppermute | solution.py:510
  45.1 0.0 collective-permute-start.10
  45.1 3.6 %collective-permute-done.10 = f32[16,128]{1,0:T(8,128)S(1)} collective-permute-done((f32[16,128]{1,0:T(8,128)S(1)}, f32[16,128]{1,0:T(8,128)S(1)}, u32[]{:S(2)}, u32[]{:S(2)}) %collective-permute-start.10) | collective-permute-done | bytes 8224 | tf_op jit(solution)/shard_map/ppermute | solution.py:511
  48.7 3.7 %collective-permute-start.11 = (f32[5,16,128]{2,1,0:T(8,128)S(1)}, f32[5,16,128]{2,1,0:T(8,128)S(1)}, u32[]{:S(2)}, u32[]{:S(2)}) collective-permute-start(f32[5,16,128]{2,1,0:T(8,128)S(1)} %pad_maximum_fusion.3.mine), channel_id=1, source_target_pairs={{0,64},{64,0},{128,192},{192,128},{1,65},{65,1},{129,193},{193,129... | collective-permute-start | bytes 122888 | tf_op jit(solution)/shard_map/ppermute | solution.py:513
  52.4 0.9 %collective-permute-done.11.sib = f32[5,16,128]{2,1,0:T(8,128)S(1)} collective-permute-done((f32[5,16,128]{2,1,0:T(8,128)S(1)}, f32[5,16,128]{2,1,0:T(8,128)S(1)}, u32[]{:S(2)}, u32[]{:S(2)}) %collective-permute-start.11) | collective-permute-done | bytes 40992 | tf_op jit(solution)/shard_map/ppermute | solution.py:513
  53.3 0.9 %relax.1 = (f32[1,2,1,32]{3,2,1,0:T(1,128)}, f32[1,1,32]{2,1,0:T(1,128)}, f32[1,2,1,32]{3,2,1,0:T(1,128)}) custom-call(f32[5,16,128]{2,1,0:T(8,128)S(1)} %pad_maximum_fusion.3.mine, f32[5,16,128]{2,1,0:T(8,128)S(1)} %collective-permute-done.11.sib), custom_call_target="tpu_custom_call" | custom-call | tf_op jit(solution)/shard_map/relax/pallas_call | solution.py:514
  (12 shorter events, 0.2 us)
Async XLA Ops:
  0.6 26.8 %copy-start.2 = (bf16[128,256]{1,0:T(8,128)(2,1)S(1)}, bf16[128,256]{1,0:T(8,128)(2,1)}, u32[]{:S(2)}) copy-start(bf16[128,256]{1,0:T(8,128)(2,1)} %constant.73.clone.rows2) | copy-start | bytes 196612
  0.6 26.8 %copy-start = (bf16[768,256]{1,0:T(8,128)(2,1)S(1)}, bf16[768,256]{1,0:T(8,128)(2,1)}, u32[]{:S(2)}) copy-start(bf16[768,256]{1,0:T(8,128)(2,1)} %constant.74.clone.fwd) | copy-start | bytes 1179652
  1.4 1.0 %copy-start.3 = (bf16[1,64,2048]{2,1,0:T(8,128)(2,1)S(1)}, bf16[1,64,2048]{2,1,0:T(8,128)(2,1)}, u32[]{:S(2)}) copy-start(bf16[1,64,2048]{2,1,0:T(8,128)(2,1)} %strip.1) | copy-start | bytes 786436
  2.3 21.0 %copy-start.6 = (bf16[2,64,2048]{2,1,0:T(8,128)(2,1)S(1)}, bf16[2,64,2048]{2,1,0:T(8,128)(2,1)}, u32[]{:S(2)}) copy-start(bf16[2,64,2048]{2,1,0:T(8,128)(2,1)} %param.9) | copy-start | bytes 1572868
  2.5 1.5 %collective-permute-start = (bf16[2,64,640]{2,1,0:T(8,128)(2,1)S(1)}, bf16[2,64,640]{2,1,0:T(8,128)(2,1)S(1)}, u32[]{:S(2)}, u32[]{:S(2)}) collective-permute-start(bf16[2,64,640]{2,1,0:T(8,128)(2,1)S(1)} %get-tuple-element.9), channel_id=1, source_target_pairs={{0,64},{64,0},{128,192},{192,128},{1,65},{65,1},{129,193},{193,129... | collective-permute-start | bytes 491528 | tf_op jit(solution)/shard_map/ppermute | solution.py:450
  3.8 25.5 %copy-start.1 = (bf16[768,256]{1,0:T(8,128)(2,1)S(1)}, bf16[768,256]{1,0:T(8,128)(2,1)}, u32[]{:S(2)}) copy-start(bf16[768,256]{1,0:T(8,128)(2,1)} %constant.75.clone.inv3) | copy-start | bytes 1179652
  3.8 25.5 %copy-start.4 = (bf16[128,384]{1,0:T(8,128)(2,1)S(1)}, bf16[128,384]{1,0:T(8,128)(2,1)}, u32[]{:S(2)}) copy-start(bf16[128,384]{1,0:T(8,128)(2,1)} %constant.76.clone.back3) | copy-start | bytes 294916
  3.8 25.5 %copy-start.5 = (s32[1,1,32]{2,1,0:T(1,128)S(1)}, s32[1,1,32]{2,1,0:T(1,128)}, u32[]{:S(2)}) copy-start(s32[1,1,32]{2,1,0:T(1,128)} %valid.1) | copy-start | bytes 388
  4.0 14.7 %collective-permute-start.3 = (bf16[2,64,640]{2,1,0:T(8,128)(2,1)S(1)}, bf16[2,64,640]{2,1,0:T(8,128)(2,1)S(1)}, u32[]{:S(2)}, u32[]{:S(2)}) collective-permute-start(bf16[2,64,640]{2,1,0:T(8,128)(2,1)S(1)} %pad_maximum_fusion.2), channel_id=1, source_target_pairs={{0,128},{64,192},{128,0},{192,64},{1,129},{65,193},{129,1},{193,65... | collective-permute-start | bytes 491528 | tf_op jit(solution)/shard_map/ppermute | solution.py:451
  10.5 16.9 %collective-permute-start.2 = (bf16[4,32,640]{2,1,0:T(8,128)(2,1)S(1)}, bf16[4,32,640]{2,1,0:T(8,128)(2,1)S(1)}, u32[]{:S(2)}, u32[]{:S(2)}) collective-permute-start(bf16[4,32,640]{2,1,0:T(8,128)(2,1)S(1)} %pad_maximum_fusion.1), channel_id=1, source_target_pairs={{0,64},{1,2},{2,1},{3,4},{4,3},{5,6},{6,5},{7,8},{8,7},{9,10},{10,... | collective-permute-start | bytes 491528 | tf_op jit(solution)/shard_map/ppermute | solution.py:465
  16.2 11.2 %collective-permute-start.1 = (bf16[4,32,640]{2,1,0:T(8,128)(2,1)S(1)}, bf16[4,32,640]{2,1,0:T(8,128)(2,1)S(1)}, u32[]{:S(2)}, u32[]{:S(2)}) collective-permute-start(bf16[4,32,640]{2,1,0:T(8,128)(2,1)S(1)} %pad_maximum_fusion), channel_id=1, source_target_pairs={{0,1},{1,0},{2,3},{3,2},{4,5},{5,4},{6,7},{7,6},{8,9},{9,8},{10,11... | collective-permute-start | bytes 491528 | tf_op jit(solution)/shard_map/ppermute | solution.py:466
  18.7 10.5 %collective-permute-start.4 = (bf16[2,32,640]{2,1,0:T(8,128)(2,1)S(1)}, bf16[2,32,640]{2,1,0:T(8,128)(2,1)S(1)}, u32[]{:S(2)}, u32[]{:S(2)}) collective-permute-start(bf16[2,32,640]{2,1,0:T(8,128)(2,1)S(1)} %get-tuple-element.16), channel_id=1, source_target_pairs={{0,64},{1,2},{2,1},{3,4},{4,3},{5,6},{6,5},{7,8},{8,7},{9,10},{10,... | collective-permute-start | bytes 245768 | tf_op jit(solution)/shard_map/ppermute | solution.py:467
  23.3 6.0 %collective-permute-start.5 = (bf16[2,32,640]{2,1,0:T(8,128)(2,1)S(1)}, bf16[2,32,640]{2,1,0:T(8,128)(2,1)S(1)}, u32[]{:S(2)}, u32[]{:S(2)}) collective-permute-start(bf16[2,32,640]{2,1,0:T(8,128)(2,1)S(1)} %get-tuple-element.15), channel_id=1, source_target_pairs={{0,1},{1,0},{2,3},{3,2},{4,5},{5,4},{6,7},{7,6},{8,9},{9,8},{10,11... | collective-permute-start | bytes 245768 | tf_op jit(solution)/shard_map/ppermute | solution.py:468
  32.8 1.3 %collective-permute-start.6 = (f32[16,128]{1,0:T(8,128)S(1)}, f32[16,128]{1,0:T(8,128)S(1)}, u32[]{:S(2)}, u32[]{:S(2)}) collective-permute-start(f32[16,128]{1,0:T(8,128)S(1)} %correlate.1), channel_id=1, source_target_pairs={{0,64},{64,0},{128,192},{192,128},{1,65},{65,1},{129,193},{193,129... | collective-permute-start | bytes 24584 | tf_op jit(solution)/shard_map/ppermute | solution.py:507
  34.0 3.7 %collective-permute-start.7 = (f32[16,128]{1,0:T(8,128)S(1)}, f32[16,128]{1,0:T(8,128)S(1)}, u32[]{:S(2)}, u32[]{:S(2)}) collective-permute-start(f32[16,128]{1,0:T(8,128)S(1)} %add.31), channel_id=1, source_target_pairs={{0,1},{1,0},{2,3},{3,2},{4,5},{5,4},{6,7},{7,6},{8,9},{9,8},{10,11... | collective-permute-start | bytes 24584 | tf_op jit(solution)/shard_map/ppermute | solution.py:508
  37.7 3.7 %collective-permute-start.8 = (f32[16,128]{1,0:T(8,128)S(1)}, f32[16,128]{1,0:T(8,128)S(1)}, u32[]{:S(2)}, u32[]{:S(2)}) collective-permute-start(f32[16,128]{1,0:T(8,128)S(1)} %add.32), channel_id=1, source_target_pairs={{0,1},{1,0},{2,3},{3,2},{4,5},{5,4},{6,7},{7,6},{8,9},{9,8},{10,11... | collective-permute-start | bytes 24584 | tf_op jit(solution)/shard_map/ppermute | solution.py:509
  41.3 3.7 %collective-permute-start.9 = (f32[2,16,128]{2,1,0:T(8,128)S(1)}, f32[2,16,128]{2,1,0:T(8,128)S(1)}, u32[]{:S(2)}, u32[]{:S(2)}) collective-permute-start(f32[2,16,128]{2,1,0:T(8,128)S(1)} %pad_maximum_fusion.4), channel_id=1, source_target_pairs={{0,1},{1,0},{2,3},{3,2},{4,5},{5,4},{6,7},{7,6},{8,9},{9,8},{10,11... | collective-permute-start | bytes 49160 | tf_op jit(solution)/shard_map/ppermute | solution.py:510
  45.1 3.7 %collective-permute-start.10 = (f32[16,128]{1,0:T(8,128)S(1)}, f32[16,128]{1,0:T(8,128)S(1)}, u32[]{:S(2)}, u32[]{:S(2)}) collective-permute-start(f32[16,128]{1,0:T(8,128)S(1)} %slice_bitcast_fusion), channel_id=1, source_target_pairs={{0,1},{1,0},{2,3},{3,2},{4,5},{5,4},{6,7},{7,6},{8,9},{9,8},{10,11... | collective-permute-start | bytes 24584 | tf_op jit(solution)/shard_map/ppermute | solution.py:511
  48.7 4.6 %collective-permute-start.11 = (f32[5,16,128]{2,1,0:T(8,128)S(1)}, f32[5,16,128]{2,1,0:T(8,128)S(1)}, u32[]{:S(2)}, u32[]{:S(2)}) collective-permute-start(f32[5,16,128]{2,1,0:T(8,128)S(1)} %pad_maximum_fusion.3.mine), channel_id=1, source_target_pairs={{0,64},{64,0},{128,192},{192,128},{1,65},{65,1},{129,193},{193,129... | collective-permute-start | bytes 122888 | tf_op jit(solution)/shard_map/ppermute | solution.py:513
